TPU v7x, 512 devices: a whole 4x4x16 slice. The times are simulated.
512 devices in a mesh: node: 32 (over y, z_lo), local: 16 (over x, z_hi, core).
Axes of the slice: x: 4, y: 4, z: 16 (z_hi: 2, z_lo: 8; z = z_hi * 8 + z_lo), core: 2. Of those that a mesh axis runs over, the one named last changes fastest.
Arguments:
- tokens: bfloat16 [65536, 4096], P(('node', 'local')), may hold values from -24 to 24
- key_codes: bfloat16 [4096, 512], P('local'), may hold values from -0.09375 to 0.09375
- key_exponents: int32 [4096, 2], P('local'), may hold values from -1 to 1
- key_cotangent: bfloat16 [65536, 512], P(('node', 'local')), may hold values from -6 to 6
Outputs:
- keys: bfloat16 [65536, 512], P(('node', 'local'))
- input_grad: bfloat16 [65536, 4096], P(('node', 'local'))
- weight_grad: float32 [4096, 512], P(('node', 'local'))
Inputs may be any that keep to these rules, and one draw needn't show every extreme that they name: key_exponents gives the power of two that scales each block of 256 columns of a row of key_codes.
All inputs are finite; a program needn't handle non-finite values.
Results may differ from a plain program's by a relative error of at most 0.015.
Values may be sent and summed in bfloat16 or wider, within the bound.
No kernel may reach another device: no remote copies, remote signals or barrier semaphores. Data moves between devices by JAX's collectives and lax.ppermute only.
A program may use at most 128 MiB of HBM per device.

v0:
```python
import math

import jax
import jax.numpy as jnp
from jax import lax
from jax.sharding import PartitionSpec as P

KVH = 4
HEAD = 128
QBLOCK = 256
SEQ = 8192


THETA = 500000.0


def in_blocks(value, dim, size):
    before, after = (value.shape[:dim], value.shape[dim + 1 :])
    return jnp.moveaxis(value.reshape(*before, size, -1, *after), dim, 0)


def joined_along(blocks, dim):
    blocks = jnp.moveaxis(blocks, 0, dim)
    lengths = blocks.shape
    return blocks.reshape(*lengths[:dim], lengths[dim] * lengths[dim + 1], *lengths[dim + 2 :])


def joined_exchange(value, axis, axes, splits, concats):
    sizes = [lax.axis_size(a) for a in axes]
    blocks = in_blocks(value, splits[0], sizes[0])
    blocks = jnp.moveaxis(in_blocks(blocks, splits[1] + 1, sizes[1]), 0, 1)
    inside = blocks.shape[2:]
    blocks = blocks.reshape(-1, *inside)
    blocks = lax.all_to_all(blocks, axis, split_axis=0, concat_axis=0, tiled=True)
    blocks = joined_along(blocks.reshape(*sizes, *inside), concats[0] + 1)
    return joined_along(blocks, concats[1])


def tables(positions):
    inverse = THETA ** (-(jnp.arange(HEAD // 2, dtype=jnp.float32) * 2.0 / HEAD))
    angles = positions.astype(jnp.float32)[:, None] * inverse[None, :]
    return (jnp.cos(angles), jnp.sin(angles))


def rotate(values, cosine, sine_part):
    count = values.shape[0]
    heads = values.reshape(count, KVH, HEAD)
    first_half = heads[:, :, : HEAD // 2]
    second_half = heads[:, :, HEAD // 2 :]
    cos_rows = cosine[:, None, :]
    sin_rows = sine_part[:, None, :]
    joined = jnp.concatenate(
        [
            first_half * cos_rows - second_half * sin_rows,
            second_half * cos_rows + first_half * sin_rows,
        ],
        axis=2,
    )
    return joined.reshape(count, KVH * HEAD)


def unrotate(values, cosine, sine_part):
    count = values.shape[0]
    heads = values.reshape(count, KVH, HEAD)
    first_half = heads[:, :, : HEAD // 2]
    second_half = heads[:, :, HEAD // 2 :]
    cos_rows = cosine[:, None, :]
    sin_rows = sine_part[:, None, :]
    joined = jnp.concatenate(
        [
            first_half * cos_rows + second_half * sin_rows,
            second_half * cos_rows - first_half * sin_rows,
        ],
        axis=2,
    )
    return joined.reshape(count, KVH * HEAD)


def quantize(partial_value):
    blocks = partial_value.reshape(partial_value.shape[0], partial_value.shape[1] // QBLOCK, QBLOCK)
    largest = jnp.max(jnp.abs(blocks), axis=2)
    block_scale = jnp.exp2(jnp.ceil(jnp.log2(largest + 1e-06)))
    code_values = (blocks / block_scale[:, :, None]).astype(jnp.bfloat16)
    return (code_values, block_scale.astype(jnp.bfloat16))


def expand_codes(code_values, block_scale):
    lead = code_values.shape[:-1]
    blocks = code_values.reshape(lead + (block_scale.shape[-1], QBLOCK))
    values = blocks.astype(jnp.float32) * block_scale.astype(jnp.float32)[..., None]
    return values.reshape(lead + (code_values.shape[-1],))


def on_device(tokens, key_codes, key_exponents, key_cotangent):
    node_count = lax.axis_size("node")
    local_count = lax.axis_size("local")
    tok_count = tokens.shape[0]
    width = tokens.shape[1]
    feature_count = key_codes.shape[1]
    expanded = jnp.repeat(jnp.exp2(key_exponents.astype(jnp.float32)), QBLOCK, axis=1)
    shard_weights = (key_codes.astype(jnp.float32) * expanded).astype(jnp.bfloat16)
    weights = lax.all_gather(shard_weights, "local", axis=0, tiled=True)
    device_index = lax.axis_index("node") * local_count + lax.axis_index("local")
    positions = (device_index * tok_count + jnp.arange(tok_count, dtype=jnp.int32)) % SEQ
    cosine, sine_part = tables(positions)
    pre_grad = unrotate(key_cotangent.astype(jnp.float32), cosine, sine_part).astype(jnp.bfloat16)
    partial_value = lax.dot_general(
        tokens, pre_grad, (((0,), (0,)), ((), ())), preferred_element_type=jnp.float32
    )
    code_values, block_scale = quantize(partial_value)
    row_count = width // (node_count * local_count)
    block_count = feature_count // QBLOCK
    code_grid = code_values.reshape(node_count, local_count, row_count, feature_count)
    scale_grid = block_scale.reshape(node_count, local_count, row_count, block_count)
    projected = jnp.dot(tokens, weights, preferred_element_type=jnp.float32)
    keys = rotate(projected, cosine, sine_part).astype(jnp.bfloat16)
    input_grad = lax.dot_general(
        pre_grad, weights, (((1,), (1,)), ((), ())), preferred_element_type=jnp.float32
    ).astype(jnp.bfloat16)
    got_codes, got_scales = (
        joined_exchange(code_grid, ("local", "node"), ("local", "node"), (1, 0), (1, 0)),
        joined_exchange(scale_grid, ("local", "node"), ("local", "node"), (1, 0), (1, 0)),
    )
    summed = jnp.sum(expand_codes(got_codes, got_scales), axis=(0, 1))
    total_tokens = tok_count * node_count * local_count
    weight_grad = summed * (1.0 / math.sqrt(total_tokens))
    return (keys, input_grad, weight_grad)


def solution(mesh):
    return jax.shard_map(
        on_device,
        mesh=mesh,
        in_specs=(
            P(("node", "local"), None),
            P("local", None),
            P("local", None),
            P(("node", "local"), None),
        ),
        out_specs=(
            P(("node", "local"), None),
            P(("node", "local"), None),
            P(("node", "local"), None),
        ),
        check_vma=False,
    )
```

profile of v0, /device:TPU:1, one launch (start us, length us, event | category | flops | bytes accessed | tf_op | source)
XLA Modules:
  0.0 424.3 jit_solution(15492790936828746594)
XLA Ops:
  7.2 0.0 copy-start
  7.2 0.0 all-gather.2.cloned.1.call-start
  7.2 0.8 multiply_exponential_fusion.1
  8.0 0.1 copy.20
  8.1 0.3 broadcast_in_dim.2
  8.5 1.7 multiply_convert_fusion
  10.3 0.0 all-gather.2.cloned.1.call-update
  10.3 1.0 copy.32
  11.3 0.2 multiply_cosine_fusion
  11.5 125.4 %all-gather.2.cloned.1.call-done = bf16[4096,512]{1,0:T(8,128)(2,1)} async-done(((bf16[256,512]{1,0:T(8,128)(2,1)}), bf16[4096,512]{1,0:T(8,128)(2,1)}) %all-gather.2.cloned.1.call-update) | async-done | bytes 4194320 | tf_op jit(solution)/shard_map/all_gather | solution.py:102
  136.9 0.0 copy-done
  136.9 3.5 fusion.6
  140.4 0.1 add_convert_fusion
  140.5 4.5 %bitcast_reduce_fusion = (f32[4096,2]{0,1:T(2,128)S(1)}, f32[4096,512]{0,1:T(8,128)}) fusion(bf16[128,512]{0,1:T(8,128)(2,1)S(1)} %bitcast.48, bf16[128,4096]{1,0:T(8,128)(2,1)S(1)} %copy-done), kind=kOutput, calls=%fused_computation.3 | convolution fusion | flops 541057024 | bytes 9601024 | tf_op jit(solution)/shard_map/dot_general | solution.py:107
  145.0 0.1 fusion.5
  145.1 0.6 copy.25
  145.7 6.0 %div.25 = f32[4096,2,256]{2,1,0:T(2,128)} broadcast(f32[4096,2]{1,0:T(8,128)S(1)} %copy.25), dimensions={0,1} | broadcast | bytes 8421376 | tf_op jit(solution)/shard_map/div | solution.py:83
  151.7 11.5 %div.26 = f32[32,16,1,8,512]{4,3,1,0,2:T(8,128)} reshape(f32[4096,2,256]{2,1,0:T(2,128)} %div.25) | data formatting | bytes 16777216 | tf_op jit(solution)/shard_map/div | solution.py:83
  163.2 9.0 %copy.24 = f32[4096,512]{1,0:T(8,128)} copy(f32[4096,512]{0,1:T(8,128)} %get-tuple-element.14) | data formatting | bytes 16777216 | tf_op jit(solution)/shard_map/dot_general | solution.py:107
  172.2 0.3 reshape.192
  172.5 1.0 copy.31
  173.5 11.5 %all-to-all-start.1 = ((bf16[512,1,1,8,2]{3,4,2,1,0:T(2,128)(2,1)}), bf16[512,1,1,8,2]{3,4,2,1,0:T(2,128)(2,1)S(1)}, u32[]{:S(2)}, u32[]{:S(2)}) async-start(bf16[512,1,1,8,2]{3,4,2,1,0:T(2,128)(2,1)} %bitcast.14), calls=%async_computation.1 | async-start | bytes 524288 | tf_op jit(solution)/shard_map/all_to_all | solution.py:34
  185.0 7.6 %fusion.2 = bf16[16,32,1,8,512]{4,3,0,1,2:T(8,128)(2,1)S(1)} fusion(f32[32,16,1,8,512]{4,3,1,0,2:T(8,128)} %bitcast.43, f32[32,16,1,8,512]{4,3,1,0,2:T(8,128)} %div.26), kind=kLoop, calls=%fused_computation.7 | loop fusion | flops 4194304 | bytes 20971520 | tf_op jit(solution)/shard_map/transpose | solution.py:19
  192.6 2.4 copy.26
  195.0 14.9 %all-to-all-done.1 = bf16[512,1,1,8,2]{3,4,2,1,0:T(2,128)(2,1)S(1)} async-done(((bf16[512,1,1,8,2]{3,4,2,1,0:T(2,128)(2,1)}), bf16[512,1,1,8,2]{3,4,2,1,0:T(2,128)(2,1)S(1)}, u32[]{:S(2)}, u32[]{:S(2)}) %all-to-all-start.1) | async-done | bytes 16416 | tf_op jit(solution)/shard_map/all_to_all | solution.py:34
  210.0 11.3 %all-to-all-start = ((bf16[512,1,1,8,512]{4,3,2,1,0:T(8,128)(2,1)}), bf16[512,1,1,8,512]{4,3,2,1,0:T(8,128)(2,1)}, u32[]{:S(2)}, u32[]{:S(2)}) async-start(bf16[512,1,1,8,512]{4,3,2,1,0:T(8,128)(2,1)} %bitcast.45), calls=%async_computation | async-start | bytes 8388608 | tf_op jit(solution)/shard_map/all_to_all | solution.py:34
  221.3 0.8 copy.30
  222.1 4.7 %convolution_convert_fusion = bf16[128,4096]{1,0:T(8,128)(2,1)} fusion(bf16[128,512]{0,1:T(8,128)(2,1)S(1)} %bitcast.49, bf16[4096,512]{1,0:T(8,128)(2,1)} %all-gather.2.cloned.1.call-done), kind=kOutput, calls=%fused_computation.6 | convolution fusion | flops 537395200 | bytes 5373952 | tf_op jit(solution)/shard_map/dot_general | solution.py:117
  226.7 0.2 convert_bitcast_fusion.1
  226.9 185.2 %all-to-all-done = bf16[512,1,1,8,512]{4,3,2,1,0:T(8,128)(2,1)} async-done(((bf16[512,1,1,8,512]{4,3,2,1,0:T(8,128)(2,1)}), bf16[512,1,1,8,512]{4,3,2,1,0:T(8,128)(2,1)}, u32[]{:S(2)}, u32[]{:S(2)}) %all-to-all-start) | async-done | bytes 4194336 | tf_op jit(solution)/shard_map/all_to_all | solution.py:34
  412.1 1.2 mul.119
  413.4 0.0 copy-start.1
  413.4 3.4 fusion.1
  416.8 0.6 broadcast_multiply_fusion
  417.4 0.0 copy-done.1
  (4 shorter events, 0.1 us)
Async XLA Ops:
  7.2 129.8 %copy-start = (bf16[128,4096]{1,0:T(8,128)(2,1)S(1)}, bf16[128,4096]{1,0:T(8,128)(2,1)}, u32[]{:S(2)}) copy-start(bf16[128,4096]{1,0:T(8,128)(2,1)} %param.4) | copy-start | bytes 3145732
  7.2 129.7 %all-gather.2.cloned.1.call-start = ((), (), s32[]{:S(2)}) async-start(), calls=%async_computation.2 | async-start | bytes 4456448 | tf_op jit(solution)/shard_map/all_gather | solution.py:102
  173.5 36.5 %all-to-all-start.1 = ((bf16[512,1,1,8,2]{3,4,2,1,0:T(2,128)(2,1)}), bf16[512,1,1,8,2]{3,4,2,1,0:T(2,128)(2,1)S(1)}, u32[]{:S(2)}, u32[]{:S(2)}) async-start(bf16[512,1,1,8,2]{3,4,2,1,0:T(2,128)(2,1)} %bitcast.14), calls=%async_computation.1 | async-start | bytes 524288 | tf_op jit(solution)/shard_map/all_to_all | solution.py:34
  210.0 202.2 %all-to-all-start = ((bf16[512,1,1,8,512]{4,3,2,1,0:T(8,128)(2,1)}), bf16[512,1,1,8,512]{4,3,2,1,0:T(8,128)(2,1)}, u32[]{:S(2)}, u32[]{:S(2)}) async-start(bf16[512,1,1,8,512]{4,3,2,1,0:T(8,128)(2,1)} %bitcast.45), calls=%async_computation | async-start | bytes 8388608 | tf_op jit(solution)/shard_map/all_to_all | solution.py:34
  413.4 4.1 copy-start.1
Sparse Core Ops, SparseCore 0:
  11.9 125.0 all-gather.1
where the time goes:
time: 425 us; the launch traced here: 424 us
  waiting for transfers between devices  326 us (77%)
  local copies, waits for them, and re-layouts  34.4 us (8%)
  starting transfers between devices  22.9 us (5%)
  other arithmetic  14.7 us (3%)
  between operations  14.2 us (3%)
  matrix products  12.6 us (3%)
    all_to_all x2, waiting for transfers between devices, joined_exchange(): lax.all_to_all(blocks, axis, split_axis=0, concat_axis=0, tiled=True)  200 us
    all_gather x1, waiting for transfers between devices, on_device(): weights = lax.all_gather(shard_weights, 'local', axis=0, tiled=True)  125 us
    all_to_all x2, starting transfers between devices, joined_exchange(): lax.all_to_all(blocks, axis, split_axis=0, concat_axis=0, tiled=True)  22.8 us
    div x2, local copies, waits for them, and re-layouts, quantize(): code_values = (blocks / block_scale[:, :, None]).astype(jnp.bfloat16)  17.4 us
    dot_general x1, local copies, waits for them, and re-layouts, on_device(): lax.dot_general(tokens, pre_grad, (((0,), (0,)), ((), ())), preferred_ele...  8.99 us
  transfers between devices with their start and end apart: 3, of which 3 were waited for; matrix products, arithmetic and copies ran while one was open for 4% of the time, Pallas kernels for 0%

commit v1 on v0

v1 whole, which is shorter than its diff:
```python
import math

import jax
import jax.numpy as jnp
from jax import lax
from jax.experimental import pallas as pl
from jax.experimental.pallas import tpu as pltpu
from jax.sharding import Mesh
from jax.sharding import PartitionSpec as P

KVH = 4
HEAD = 128
QBLOCK = 256
SEQ = 8192
THETA = 500000.0

Y, ZL, X, ZH, CORE = 4, 8, 4, 2, 2
AXES = ("y", "zl", "x", "zh", "core")
ROW = 8

F32 = jnp.float32
BF16 = jnp.bfloat16
PARAMS = pltpu.CompilerParams(vmem_limit_bytes=32 * 1024 * 1024)


def dequantize_kernel(code_ref, exponent_ref, weight_ref):
    scale = jnp.exp2(exponent_ref[...].astype(F32))
    for block in range(code_ref.shape[1] // QBLOCK):
        columns = slice(block * QBLOCK, (block + 1) * QBLOCK)
        value = code_ref[:, columns].astype(F32) * scale[:, block : block + 1]
        weight_ref[:, columns] = value.astype(BF16)


def dequantize(key_codes, key_exponents):
    return pl.pallas_call(
        dequantize_kernel,
        out_shape=jax.ShapeDtypeStruct(key_codes.shape, BF16),
        compiler_params=PARAMS,
    )(key_codes, key_exponents)


def tables(positions):
    inverse = THETA ** (-(jnp.arange(HEAD // 2, dtype=F32) * 2.0 / HEAD))
    angles = positions.astype(F32)[:, None] * inverse[None, :]
    cosine, sine = jnp.cos(angles), jnp.sin(angles)
    return (
        jnp.concatenate([cosine, cosine], axis=1),
        jnp.concatenate([-sine, sine], axis=1),
    )


def partial_kernel(core_ref, token_ref, cot_ref, cos_ref, sin_ref, mine_ref, theirs_ref, pre_ref, part_ref):
    @pl.when(pl.program_id(0) == 0)
    def _():
        for head in range(KVH):
            columns = slice(head * HEAD, (head + 1) * HEAD)
            value = cot_ref[:, columns].astype(F32)
            turned = pltpu.roll(value, HEAD // 2, 1)
            pre_ref[:, columns] = (value * cos_ref[...] - turned * sin_ref[...]).astype(BF16)

    part = lax.dot_general(
        token_ref[...], pre_ref[...], (((0,), (0,)), ((), ())), preferred_element_type=F32
    )
    part_ref[...] = part.reshape(part_ref.shape)
    core = core_ref[0]
    for x in range(X):
        for zl in range(ZL):
            for zh in range(ZH):
                place = (zl * X + x) * ZH + zh
                mine_ref[x, 0, zl, zh] = part_ref[place, core].astype(BF16)
                theirs_ref[x, 0, zl, zh] = part_ref[place, 1 - core].astype(BF16)


def partial_products(core, tokens, key_cotangent, cosine, sine):
    count, width = tokens.shape
    features = key_cotangent.shape[1]
    step = width // Y
    half = jax.ShapeDtypeStruct((X, Y, ZL, ZH, ROW, features), BF16)
    half_spec = pl.BlockSpec((X, 1, ZL, ZH, ROW, features), lambda y: (0, y, 0, 0, 0, 0))
    whole = lambda y: (0, 0)
    return pl.pallas_call(
        partial_kernel,
        grid=(Y,),
        in_specs=[
            pl.BlockSpec(memory_space=pltpu.SMEM),
            pl.BlockSpec((count, step), lambda y: (0, y)),
            pl.BlockSpec((count, features), whole),
            pl.BlockSpec((count, HEAD), whole),
            pl.BlockSpec((count, HEAD), whole),
        ],
        out_specs=[half_spec, half_spec, pl.BlockSpec((count, features), whole)],
        out_shape=[half, half, jax.ShapeDtypeStruct((count, features), BF16)],
        scratch_shapes=[pltpu.VMEM((ZL * X * ZH, CORE, ROW, features), F32)],
        compiler_params=PARAMS,
    )(core, tokens, key_cotangent, cosine, sine)


def apply_kernel(place_ref, token_ref, pre_ref, cos_ref, sin_ref, w00_ref, w01_ref, w10_ref, w11_ref, keys_ref, grad_ref):
    zh, core = place_ref[0], place_ref[1]
    rows = token_ref.shape[1] // (X * ZH * CORE)
    pre = pre_ref[...]
    total = jnp.zeros(pre.shape, F32)
    held = ((w00_ref, 0, 0), (w01_ref, 0, 1), (w10_ref, 1, 0), (w11_ref, 1, 1))
    for weight_ref, other_zh, other_core in held:
        near = jnp.where(other_zh == 0, zh, 1 - zh)
        side = jnp.where(other_core == 0, core, 1 - core)
        for x in range(X):
            start = pl.multiple_of(((x * ZH + near) * CORE + side) * rows, rows)
            weight = weight_ref[x * rows : (x + 1) * rows, :]
            total += jnp.dot(token_ref[:, pl.ds(start, rows)], weight, preferred_element_type=F32)
            grad_ref[:, pl.ds(start, rows)] = lax.dot_general(
                pre, weight, (((1,), (1,)), ((), ())), preferred_element_type=F32
            ).astype(BF16)
    for head in range(KVH):
        columns = slice(head * HEAD, (head + 1) * HEAD)
        value = total[:, columns]
        turned = pltpu.roll(value, HEAD // 2, 1)
        keys_ref[:, columns] = (value * cos_ref[...] + turned * sin_ref[...]).astype(BF16)


def apply_weights(place, tokens, pre_grad, cosine, sine, weights):
    vmem = pl.BlockSpec(memory_space=pltpu.VMEM)
    return pl.pallas_call(
        apply_kernel,
        in_specs=[pl.BlockSpec(memory_space=pltpu.SMEM)] + [vmem] * 8,
        out_specs=[vmem, vmem],
        out_shape=[
            jax.ShapeDtypeStruct(pre_grad.shape, BF16),
            jax.ShapeDtypeStruct(tokens.shape, BF16),
        ],
        compiler_params=PARAMS,
        cost_estimate=pl.CostEstimate(
            flops=4 * tokens.shape[0] * tokens.shape[1] * pre_grad.shape[1],
            bytes_accessed=7 * 1024 * 1024,
            transcendentals=0,
        ),
    )(place, tokens, pre_grad, cosine, sine, *weights)


def swap(value, axis):
    return lax.ppermute(value, axis, [(0, 1), (1, 0)])


def on_device(tokens, key_codes, key_exponents, key_cotangent):
    y, zl, x, zh, core = [lax.axis_index(name) for name in AXES]
    count = tokens.shape[0]
    features = key_cotangent.shape[1]

    shard = dequantize(key_codes, key_exponents)
    near = lax.all_gather(shard, "x", axis=0, tiled=True)
    far = lax.all_gather(swap(shard, "zh"), "x", axis=0, tiled=True)
    weights = (near, swap(near, "core"), far, swap(far, "core"))

    device_index = (((y * ZL + zl) * X + x) * ZH + zh) * CORE + core
    positions = (device_index * count + jnp.arange(count, dtype=jnp.int32)) % SEQ
    cosine, sine = tables(positions)
    mine, theirs, pre_grad = partial_products(core[None], tokens, key_cotangent, cosine, sine)

    summed = (mine.astype(F32) + swap(theirs, "core").astype(F32)).astype(BF16)
    summed = summed.reshape(X * Y, ZL * ZH, ROW, features)
    got = lax.all_to_all(summed, ("x", "y"), split_axis=0, concat_axis=0, tiled=True)
    summed = jnp.sum(got.astype(F32), axis=0).astype(BF16)
    got = lax.all_to_all(summed, ("zl", "zh"), split_axis=0, concat_axis=0, tiled=True)
    total_tokens = count * Y * ZL * X * ZH * CORE
    weight_grad = jnp.sum(got.astype(F32), axis=0) * (1.0 / math.sqrt(total_tokens))

    place = jnp.stack([zh, core])
    keys, input_grad = apply_weights(place, tokens, pre_grad, cosine, sine, weights)
    return keys, input_grad, weight_grad


def solution(mesh):
    fine = Mesh(mesh.devices.reshape(Y, ZL, X, ZH, CORE), AXES)
    split = P(AXES, None)
    return jax.shard_map(
        on_device,
        mesh=fine,
        in_specs=(split, P(("x", "zh", "core"), None), P(("x", "zh", "core"), None), split),
        out_specs=(split, split, split),
        check_vma=False,
    )
```

time: 425 us -> 142 us (0.33)
  the two profiles are of different devices: /device:TPU:1 before, /device:TPU:16 now
where the time goes in v1:
time: 142 us
  starting transfers between devices  55.7 us (39%)
  waiting for transfers between devices  50.7 us (36%)
  between operations  14.2 us (10%)
  Pallas kernels  8.66 us (6%)
  other arithmetic  7.55 us (5%)
  local copies, waits for them, and re-layouts  4.87 us (3%)
    all_gather x1, waiting for transfers between devices, on_device(): far = lax.all_gather(swap(shard, 'zh'), 'x', axis=0, tiled=True)  32.9 us
    ppermute x4, starting transfers between devices, swap(): return lax.ppermute(value, axis, [(0, 1), (1, 0)])  21.6 us
    all_to_all x1, starting transfers between devices, on_device(): lax.all_to_all(summed, ('zl', 'zh'), split_axis=0, concat_axis=0, tiled=T...  21.5 us
    all_to_all x1, starting transfers between devices, on_device(): lax.all_to_all(summed, ('x', 'y'), split_axis=0, concat_axis=0, tiled=True)  12.5 us
    all_to_all x1, waiting for transfers between devices, on_device(): lax.all_to_all(summed, ('zl', 'zh'), split_axis=0, concat_axis=0, tiled=T...  10.3 us
    ppermute x4, waiting for transfers between devices, swap(): return lax.ppermute(value, axis, [(0, 1), (1, 0)])  7.47 us
    unnamed x15, local copies, waits for them, and re-layouts  4.87 us
    pallas_call x1, Pallas kernels, apply_weights(): pl.pallas_call(apply_kernel, in_specs=[pl.BlockSpec(memory_space=pltpu.SM...  4.23 us
  transfers between devices with their start and end apart: 8, of which 3 were waited for; matrix products, arithmetic and copies ran while one was open for 5% of the time, Pallas kernels for 4%

profile of v1, /device:TPU:16, one launch (start us, length us, event | category | flops | bytes accessed | tf_op | source)
XLA Modules:
  0.0 141.7 jit_solution(12586640839900558039)
XLA Ops:
  7.2 0.0 copy-start.4
  7.2 0.0 all-gather.3.cloned.1.call-start
  7.3 0.3 fusion
  7.6 0.1 pad_maximum_fusion
  7.7 0.0 copy-start
  7.7 1.2 copy-done
  8.9 0.0 copy-start.5
  8.9 0.9 copy-done.5
  9.8 3.6 %shard_map.67 = (bf16[4,4,8,2,8,512]{5,4,3,2,1,0:T(8,128)(2,1)S(1)}, bf16[4,4,8,2,8,512]{5,4,3,2,1,0:T(8,128)(2,1)}, bf16[128,512]{1,0:T(8,128)(2,1)S(1)}) custom-call(s32[1]{0:T(128)} %bitcast.1.core_ref, bf16[128,4096]{1,0:T(8,128)(2,1)S(1)} %copy-done, bf16[128,512]{1,0:T(8,128)(2,1)S(1)} %copy-done.5, f32[128,128]{1,0:T(8,128)S(1)} %get-tuple-element.16.cos_ref, ...), custom_call_target="tpu_custom_call" | custom-call | tf_op jit(solution)/shard_map/pallas_call | solution.py:81
  13.4 1.9 %collective-permute-start.3 = (bf16[4,4,8,2,8,512]{5,4,3,2,1,0:T(8,128)(2,1)}, bf16[4,4,8,2,8,512]{5,4,3,2,1,0:T(8,128)(2,1)}, u32[]{:S(2)}, u32[]{:S(2)}) collective-permute-start(bf16[4,4,8,2,8,512]{5,4,3,2,1,0:T(8,128)(2,1)} %get-tuple-element.12), channel_id=1, source_target_pairs={{0,1},{1,0},{2,3},{3,2},{4,5},{5,4},{6,7},{7,6},{8,9},{9,8},{10,11... | collective-permute-start | bytes 6291464 | tf_op jit(solution)/shard_map/ppermute | solution.py:141
  15.3 0.8 copy.8.exponent_ref
  16.1 0.0 copy-done.4
  16.2 0.8 shard_map.68
  17.0 0.0 all-gather.3.cloned.1.call-update
  17.0 0.0 all-gather.5.cloned.1.call-start
  17.1 15.7 %collective-permute-start.1 = (bf16[256,512]{1,0:T(8,128)(2,1)}, bf16[256,512]{1,0:T(8,128)(2,1)S(1)}, u32[]{:S(2)}, u32[]{:S(2)}) collective-permute-start(bf16[256,512]{1,0:T(8,128)(2,1)} %shard_map.68), channel_id=1, source_target_pairs={{0,2},{2,0},{1,3},{3,1},{4,6},{6,4},{5,7},{7,5},{8,10},{10,8},{9,1... | collective-permute-start | bytes 786440 | tf_op jit(solution)/shard_map/ppermute | solution.py:141
  32.8 7.5 %collective-permute-done.1 = bf16[256,512]{1,0:T(8,128)(2,1)S(1)} collective-permute-done((bf16[256,512]{1,0:T(8,128)(2,1)}, bf16[256,512]{1,0:T(8,128)(2,1)S(1)}, u32[]{:S(2)}, u32[]{:S(2)}) %collective-permute-start.1) | collective-permute-done | bytes 262176 | tf_op jit(solution)/shard_map/ppermute | solution.py:141
  40.3 0.0 copy-start.6
  40.3 0.7 copy-done.6
  41.0 0.0 all-gather.5.cloned.1.call-update
  41.0 0.0 collective-permute-done.3
  41.0 3.9 %add_convert_fusion = bf16[4,4,8,2,8,512]{5,4,3,2,1,0:T(8,128)(2,1)} fusion(bf16[4,4,8,2,8,512]{5,4,3,2,1,0:T(8,128)(2,1)} %collective-permute-done.3, bf16[4,4,8,2,8,512]{5,4,3,2,1,0:T(8,128)(2,1)S(1)} %get-tuple-element.11), kind=kLoop, calls=%fused_computation | loop fusion | flops 4194304 | bytes 6291456 | tf_op jit(solution)/shard_map/convert_element_type | solution.py:159
  44.9 12.5 %all-to-all-start = ((bf16[16,16,8,512]{3,2,1,0:T(8,128)(2,1)}), bf16[16,16,8,512]{3,2,1,0:T(8,128)(2,1)}, u32[]{:S(2)}, u32[]{:S(2)}) async-start(bf16[16,16,8,512]{3,2,1,0:T(8,128)(2,1)} %bitcast.3), calls=%async_computation | async-start | bytes 4194304 | tf_op jit(solution)/shard_map/all_to_all | solution.py:161
  57.4 0.0 copy-start.1
  57.4 0.0 all-gather.3.cloned.1.call-done.w00_ref
  57.4 0.0 copy-start.2
  57.4 2.1 %collective-permute-start = (bf16[1024,512]{1,0:T(8,128)(2,1)}, bf16[1024,512]{1,0:T(8,128)(2,1)S(1)}, u32[]{:S(2)}, u32[]{:S(2)}) collective-permute-start(bf16[1024,512]{1,0:T(8,128)(2,1)} %all-gather.3.cloned.1.call-done.w00_ref), channel_id=1, source_target_pairs={{0,1},{1,0},{2,3},{3,2},{4,5},{5,4},{6,7},{7,6},{8,9},{9,8},{10,11... | collective-permute-start | bytes 3145736 | tf_op jit(solution)/shard_map/ppermute | solution.py:141
  59.5 32.9 %all-gather.5.cloned.1.call-done.w10_ref = bf16[1024,512]{1,0:T(8,128)(2,1)} async-done(((bf16[256,512]{1,0:T(8,128)(2,1)}), bf16[1024,512]{1,0:T(8,128)(2,1)}) %all-gather.5.cloned.1.call-update) | async-done | bytes 1048592 | tf_op jit(solution)/shard_map/all_gather | solution.py:151
  92.4 1.9 %collective-permute-start.2 = (bf16[1024,512]{1,0:T(8,128)(2,1)}, bf16[1024,512]{1,0:T(8,128)(2,1)}, u32[]{:S(2)}, u32[]{:S(2)}) collective-permute-start(bf16[1024,512]{1,0:T(8,128)(2,1)} %all-gather.5.cloned.1.call-done.w10_ref), channel_id=1, source_target_pairs={{0,1},{1,0},{2,3},{3,2},{4,5},{5,4},{6,7},{7,6},{8,9},{9,8},{10,11... | collective-permute-start | bytes 3145736 | tf_op jit(solution)/shard_map/ppermute | solution.py:141
  94.3 0.0 all-to-all-done
  94.3 2.6 %reduce_sum.21 = bf16[16,8,512]{2,1,0:T(8,128)(2,1)} reduce(bf16[16,16,8,512]{3,2,1,0:T(8,128)(2,1)} %all-to-all-done, bf16[]{:T(256)} %constant.53.clone.1), dimensions={0}, to_apply=%region_0.1 | reduce | flops 983040 | bytes 2228226 | tf_op jit(solution)/shard_map/reduce_sum | solution.py:162
  96.9 21.5 %all-to-all-start.1 = ((bf16[16,8,512]{2,1,0:T(8,128)(2,1)}), bf16[16,8,512]{2,1,0:T(8,128)(2,1)S(1)}, u32[]{:S(2)}, u32[]{:S(2)}) async-start(bf16[16,8,512]{2,1,0:T(8,128)(2,1)} %reduce_sum.21), calls=%async_computation.1 | async-start | bytes 262144 | tf_op jit(solution)/shard_map/all_to_all | solution.py:163
  118.3 0.1 pad_add_fusion.place_ref
  118.4 0.0 collective-permute-done.w01_ref
  118.4 0.0 collective-permute-done.2.w11_ref
  118.4 0.0 copy-done.1
  118.4 0.0 copy-done.2
  118.4 0.0 copy-start.3
  118.4 1.2 copy-done.3
  119.7 4.2 %shard_map.69 = (bf16[128,512]{1,0:T(8,128)(2,1)}, bf16[128,4096]{1,0:T(8,128)(2,1)}) custom-call(s32[2]{0:T(128)S(1)} %pad_add_fusion.place_ref, bf16[128,4096]{1,0:T(8,128)(2,1)S(1)} %copy-done.1, bf16[128,512]{1,0:T(8,128)(2,1)S(1)} %get-tuple-element.8.pre_ref, f32[128,128]{1,0:T(8,128)S(1)} %get-tuple-element.16.cos_ref, ...), custom_call_target="tpu_custom_call" | custom-call | flops 1073741824 | bytes 7340032 | tf_op jit(solution)/shard_map/pallas_call | solution.py:123
  123.9 10.3 %all-to-all-done.1 = bf16[16,8,512]{2,1,0:T(8,128)(2,1)S(1)} async-done(((bf16[16,8,512]{2,1,0:T(8,128)(2,1)}), bf16[16,8,512]{2,1,0:T(8,128)(2,1)S(1)}, u32[]{:S(2)}, u32[]{:S(2)}) %all-to-all-start.1) | async-done | bytes 131104 | tf_op jit(solution)/shard_map/all_to_all | solution.py:163
  134.2 0.6 broadcast_multiply_fusion
  (3 shorter events, 0.0 us)
Async XLA Ops:
  7.2 9.0 %copy-start.4 = (bf16[256,512]{1,0:T(8,128)(2,1)S(1)}, bf16[256,512]{1,0:T(8,128)(2,1)}, u32[]{:S(2)}) copy-start(bf16[256,512]{1,0:T(8,128)(2,1)} %code_ref.1) | copy-start | bytes 786436
  7.2 50.2 %all-gather.3.cloned.1.call-start = ((), (), s32[]{:S(2)}) async-start(), calls=%async_computation.2 | async-start | bytes 1310720 | tf_op jit(solution)/shard_map/all_gather | solution.py:150
  7.7 1.2 copy-start
  8.9 0.9 copy-start.5
  13.4 27.6 %collective-permute-start.3 = (bf16[4,4,8,2,8,512]{5,4,3,2,1,0:T(8,128)(2,1)}, bf16[4,4,8,2,8,512]{5,4,3,2,1,0:T(8,128)(2,1)}, u32[]{:S(2)}, u32[]{:S(2)}) collective-permute-start(bf16[4,4,8,2,8,512]{5,4,3,2,1,0:T(8,128)(2,1)} %get-tuple-element.12), channel_id=1, source_target_pairs={{0,1},{1,0},{2,3},{3,2},{4,5},{5,4},{6,7},{7,6},{8,9},{9,8},{10,11... | collective-permute-start | bytes 6291464 | tf_op jit(solution)/shard_map/ppermute | solution.py:141
  17.0 75.3 %all-gather.5.cloned.1.call-start = ((), (), s32[]{:S(2)}) async-start(), calls=%async_computation.3 | async-start | bytes 1310720 | tf_op jit(solution)/shard_map/all_gather | solution.py:151
  17.1 23.2 %collective-permute-start.1 = (bf16[256,512]{1,0:T(8,128)(2,1)}, bf16[256,512]{1,0:T(8,128)(2,1)S(1)}, u32[]{:S(2)}, u32[]{:S(2)}) collective-permute-start(bf16[256,512]{1,0:T(8,128)(2,1)} %shard_map.68), channel_id=1, source_target_pairs={{0,2},{2,0},{1,3},{3,1},{4,6},{6,4},{5,7},{7,5},{8,10},{10,8},{9,1... | collective-permute-start | bytes 786440 | tf_op jit(solution)/shard_map/ppermute | solution.py:141
  40.3 0.7 copy-start.6
  44.9 49.4 %all-to-all-start = ((bf16[16,16,8,512]{3,2,1,0:T(8,128)(2,1)}), bf16[16,16,8,512]{3,2,1,0:T(8,128)(2,1)}, u32[]{:S(2)}, u32[]{:S(2)}) async-start(bf16[16,16,8,512]{3,2,1,0:T(8,128)(2,1)} %bitcast.3), calls=%async_computation | async-start | bytes 4194304 | tf_op jit(solution)/shard_map/all_to_all | solution.py:161
  57.4 61.0 %copy-start.1 = (bf16[128,4096]{1,0:T(8,128)(2,1)S(1)}, bf16[128,4096]{1,0:T(8,128)(2,1)}, u32[]{:S(2)}) copy-start(bf16[128,4096]{1,0:T(8,128)(2,1)} %token_ref.3) | copy-start | bytes 3145732
  57.4 61.0 %copy-start.2 = (bf16[1024,512]{1,0:T(8,128)(2,1)S(1)}, bf16[1024,512]{1,0:T(8,128)(2,1)}, u32[]{:S(2)}) copy-start(bf16[1024,512]{1,0:T(8,128)(2,1)} %all-gather.3.cloned.1.call-done.w00_ref) | copy-start | bytes 3145732
  57.4 61.0 %collective-permute-start = (bf16[1024,512]{1,0:T(8,128)(2,1)}, bf16[1024,512]{1,0:T(8,128)(2,1)S(1)}, u32[]{:S(2)}, u32[]{:S(2)}) collective-permute-start(bf16[1024,512]{1,0:T(8,128)(2,1)} %all-gather.3.cloned.1.call-done.w00_ref), channel_id=1, source_target_pairs={{0,1},{1,0},{2,3},{3,2},{4,5},{5,4},{6,7},{7,6},{8,9},{9,8},{10,11... | collective-permute-start | bytes 3145736 | tf_op jit(solution)/shard_map/ppermute | solution.py:141
  92.4 26.0 %collective-permute-start.2 = (bf16[1024,512]{1,0:T(8,128)(2,1)}, bf16[1024,512]{1,0:T(8,128)(2,1)}, u32[]{:S(2)}, u32[]{:S(2)}) collective-permute-start(bf16[1024,512]{1,0:T(8,128)(2,1)} %all-gather.5.cloned.1.call-done.w10_ref), channel_id=1, source_target_pairs={{0,1},{1,0},{2,3},{3,2},{4,5},{5,4},{6,7},{7,6},{8,9},{9,8},{10,11... | collective-permute-start | bytes 3145736 | tf_op jit(solution)/shard_map/ppermute | solution.py:141
  96.9 37.3 %all-to-all-start.1 = ((bf16[16,8,512]{2,1,0:T(8,128)(2,1)}), bf16[16,8,512]{2,1,0:T(8,128)(2,1)S(1)}, u32[]{:S(2)}, u32[]{:S(2)}) async-start(bf16[16,8,512]{2,1,0:T(8,128)(2,1)} %reduce_sum.21), calls=%async_computation.1 | async-start | bytes 262144 | tf_op jit(solution)/shard_map/all_to_all | solution.py:163
  118.4 1.2 copy-start.3
Sparse Core Ops, SparseCore 0:
  17.1 36.0 all-gather.2
  55.3 36.9 all-gather.4

commit v2 on v1

--- a/solution.py
+++ b/solution.py
@@ -20,7 +20,7 @@
 
 F32 = jnp.float32
 BF16 = jnp.bfloat16
-PARAMS = pltpu.CompilerParams(vmem_limit_bytes=32 * 1024 * 1024)
+PARAMS = pltpu.CompilerParams(vmem_limit_bytes=20 * 1024 * 1024)
 
 
 def dequantize_kernel(code_ref, exponent_ref, weight_ref):
@@ -95,22 +95,55 @@
     )(core, tokens, key_cotangent, cosine, sine)
 
 
-def apply_kernel(place_ref, token_ref, pre_ref, cos_ref, sin_ref, w00_ref, w01_ref, w10_ref, w11_ref, keys_ref, grad_ref):
-    zh, core = place_ref[0], place_ref[1]
-    rows = token_ref.shape[1] // (X * ZH * CORE)
+def join_kernel(*refs):
+    rows = refs[0].shape[0]
+    for block, ref in enumerate(refs[:-1]):
+        refs[-1][block * rows : (block + 1) * rows, :] = ref[...]
+
+
+def joined(blocks):
+    rows, features = blocks[0].shape
+    return pl.pallas_call(
+        join_kernel,
+        out_shape=jax.ShapeDtypeStruct((len(blocks) * rows, features), BF16),
+        compiler_params=PARAMS,
+    )(*blocks)
+
+
+def first_column(place_ref, block, side, rows):
+    x, zh = place_ref[0], place_ref[1]
+    near = zh if block < X else 1 - zh
+    source = lax.rem(x + (X - block % X), X)
+    return pl.multiple_of(((source * ZH + near) * CORE + side) * rows, rows)
+
+
+def apply_first_kernel(place_ref, token_ref, pre_ref, weight_ref, total_ref, grad_ref):
+    rows = weight_ref.shape[0] // (ZH * X)
     pre = pre_ref[...]
     total = jnp.zeros(pre.shape, F32)
-    held = ((w00_ref, 0, 0), (w01_ref, 0, 1), (w10_ref, 1, 0), (w11_ref, 1, 1))
-    for weight_ref, other_zh, other_core in held:
-        near = jnp.where(other_zh == 0, zh, 1 - zh)
-        side = jnp.where(other_core == 0, core, 1 - core)
-        for x in range(X):
-            start = pl.multiple_of(((x * ZH + near) * CORE + side) * rows, rows)
-            weight = weight_ref[x * rows : (x + 1) * rows, :]
-            total += jnp.dot(token_ref[:, pl.ds(start, rows)], weight, preferred_element_type=F32)
-            grad_ref[:, pl.ds(start, rows)] = lax.dot_general(
-                pre, weight, (((1,), (1,)), ((), ())), preferred_element_type=F32
-            ).astype(BF16)
+    for block in range(ZH * X):
+        start = first_column(place_ref, block, place_ref[2], rows)
+        weight = weight_ref[block * rows : (block + 1) * rows, :]
+        total += jnp.dot(token_ref[:, pl.ds(start, rows)], weight, preferred_element_type=F32)
+        grad_ref[block] = lax.dot_general(
+            pre, weight, (((1,), (1,)), ((), ())), preferred_element_type=F32
+        ).astype(BF16)
+    total_ref[...] = total
+
+
+def apply_second_kernel(place_ref, token_ref, pre_ref, cos_ref, sin_ref, weight_ref, total_ref, half_ref, keys_ref, grad_ref):
+    rows = weight_ref.shape[0] // (ZH * X)
+    pre = pre_ref[...]
+    total = total_ref[...]
+    for block in range(ZH * X):
+        start = first_column(place_ref, block, place_ref[2], rows)
+        grad_ref[:, pl.ds(start, rows)] = half_ref[block]
+        start = first_column(place_ref, block, 1 - place_ref[2], rows)
+        weight = weight_ref[block * rows : (block + 1) * rows, :]
+        total += jnp.dot(token_ref[:, pl.ds(start, rows)], weight, preferred_element_type=F32)
+        grad_ref[:, pl.ds(start, rows)] = lax.dot_general(
+            pre, weight, (((1,), (1,)), ((), ())), preferred_element_type=F32
+        ).astype(BF16)
     for head in range(KVH):
         columns = slice(head * HEAD, (head + 1) * HEAD)
         value = total[:, columns]
@@ -118,23 +151,53 @@
         keys_ref[:, columns] = (value * cos_ref[...] + turned * sin_ref[...]).astype(BF16)
 
 
-def apply_weights(place, tokens, pre_grad, cosine, sine, weights):
+def product_cost(tokens, features):
+    return pl.CostEstimate(
+        flops=2 * tokens.shape[0] * tokens.shape[1] * features,
+        bytes_accessed=4 * 1024 * 1024,
+        transcendentals=0,
+    )
+
+
+def apply_first(place, tokens, pre_grad, weights):
     vmem = pl.BlockSpec(memory_space=pltpu.VMEM)
-    return pl.pallas_call(
-        apply_kernel,
-        in_specs=[pl.BlockSpec(memory_space=pltpu.SMEM)] + [vmem] * 8,
+    count, features = pre_grad.shape
+    blocks = ZH * X
+    return pl.pallas_call(
+        apply_first_kernel,
+        in_specs=[pl.BlockSpec(memory_space=pltpu.SMEM)] + [vmem] * 3,
+        out_specs=[vmem, vmem],
+        out_shape=[
+            jax.ShapeDtypeStruct((count, features), F32),
+            jax.ShapeDtypeStruct((blocks, count, weights.shape[0] // blocks), BF16),
+        ],
+        compiler_params=PARAMS,
+        cost_estimate=product_cost(tokens, features),
+    )(place, tokens, pre_grad, weights)
+
+
+def apply_second(place, tokens, pre_grad, cosine, sine, weights, total, half):
+    vmem = pl.BlockSpec(memory_space=pltpu.VMEM)
+    return pl.pallas_call(
+        apply_second_kernel,
+        in_specs=[pl.BlockSpec(memory_space=pltpu.SMEM)] + [vmem] * 7,
         out_specs=[vmem, vmem],
         out_shape=[
             jax.ShapeDtypeStruct(pre_grad.shape, BF16),
             jax.ShapeDtypeStruct(tokens.shape, BF16),
         ],
         compiler_params=PARAMS,
-        cost_estimate=pl.CostEstimate(
-            flops=4 * tokens.shape[0] * tokens.shape[1] * pre_grad.shape[1],
-            bytes_accessed=7 * 1024 * 1024,
-            transcendentals=0,
-        ),
-    )(place, tokens, pre_grad, cosine, sine, *weights)
+        cost_estimate=product_cost(tokens, pre_grad.shape[1]),
+    )(place, tokens, pre_grad, cosine, sine, weights, total, half)
+
+
+def after(value, *others):
+    return lax.optimization_barrier((value, *others))[0]
+
+
+def from_x(shard):
+    moved = [lax.ppermute(shard, "x", [(i, (i + k) % X) for i in range(X)]) for k in range(1, X)]
+    return [shard, *moved]
 
 
 def swap(value, axis):
@@ -147,25 +210,33 @@
     features = key_cotangent.shape[1]
 
     shard = dequantize(key_codes, key_exponents)
-    near = lax.all_gather(shard, "x", axis=0, tiled=True)
-    far = lax.all_gather(swap(shard, "zh"), "x", axis=0, tiled=True)
-    weights = (near, swap(near, "core"), far, swap(far, "core"))
-
     device_index = (((y * ZL + zl) * X + x) * ZH + zh) * CORE + core
     positions = (device_index * count + jnp.arange(count, dtype=jnp.int32)) % SEQ
     cosine, sine = tables(positions)
-    mine, theirs, pre_grad = partial_products(core[None], tokens, key_cotangent, cosine, sine)
+    mine, theirs, pre_grad = partial_products(core[None], after(tokens, shard), key_cotangent, cosine, sine)
 
     summed = (mine.astype(F32) + swap(theirs, "core").astype(F32)).astype(BF16)
     summed = summed.reshape(X * Y, ZL * ZH, ROW, features)
     got = lax.all_to_all(summed, ("x", "y"), split_axis=0, concat_axis=0, tiled=True)
+
+    shard = after(shard, theirs)
+    far_shard = after(swap(shard, "zh"), summed)
+    near = from_x(shard)
+    far = from_x(far_shard)
+
+    held = joined(near + far)
+    got = after(got, held)
     summed = jnp.sum(got.astype(F32), axis=0).astype(BF16)
     got = lax.all_to_all(summed, ("zl", "zh"), split_axis=0, concat_axis=0, tiled=True)
+
+    place = jnp.stack([x, zh, core])
+    total, half = apply_first(place, tokens, pre_grad, held)
+    keys, input_grad = apply_second(
+        place, tokens, pre_grad, cosine, sine, swap(held, "core"), total, half
+    )
+    got = after(got, keys)
     total_tokens = count * Y * ZL * X * ZH * CORE
     weight_grad = jnp.sum(got.astype(F32), axis=0) * (1.0 / math.sqrt(total_tokens))
-
-    place = jnp.stack([zh, core])
-    keys, input_grad = apply_weights(place, tokens, pre_grad, cosine, sine, weights)
     return keys, input_grad, weight_grad
 
 

time: 142 us -> 113 us (0.80)
  the two profiles are of different devices: /device:TPU:16 before, /device:TPU:1 now
where the time goes in v2:
time: 113 us; the launch traced here: 111 us
  starting transfers between devices  52.1 us (46%)
  waiting for transfers between devices  40.1 us (35%)
  Pallas kernels  8.28 us (7%)
  other arithmetic  6.15 us (5%)
  local copies, waits for them, and re-layouts  3.89 us (3%)
    ppermute x6, waiting for transfers between devices, from_x(): lax.ppermute(shard, 'x', [(i, (i + k) % X) for i in range(X)])  32.1 us
    ppermute x3, starting transfers between devices, swap(): return lax.ppermute(value, axis, [(0, 1), (1, 0)])  22.6 us
    ppermute x6, starting transfers between devices, from_x(): lax.ppermute(shard, 'x', [(i, (i + k) % X) for i in range(X)])  20 us
    all_to_all x1, waiting for transfers between devices, on_device(): lax.all_to_all(summed, ('zl', 'zh'), split_axis=0, concat_axis=0, tiled=T...  8.05 us
    all_to_all x1, starting transfers between devices, on_device(): lax.all_to_all(summed, ('zl', 'zh'), split_axis=0, concat_axis=0, tiled=T...  4.84 us
    all_to_all x1, starting transfers between devices, on_device(): lax.all_to_all(summed, ('x', 'y'), split_axis=0, concat_axis=0, tiled=True)  4.62 us
    unnamed x9, local copies, waits for them, and re-layouts  3.89 us
    pallas_call x1, Pallas kernels, apply_second(): pl.pallas_call(apply_second_kernel, in_specs=[pl.BlockSpec(memory_space=p...  3.63 us
  transfers between devices with their start and end apart: 11, of which 5 were waited for; matrix products, arithmetic and copies ran while one was open for 5% of the time, Pallas kernels for 5%

profile of v2, /device:TPU:1, one launch (start us, length us, event | category | flops | bytes accessed | tf_op | source)
XLA Modules:
  0.0 111.4 jit_solution(14012172449021542942)
XLA Ops:
  0.7 0.8 copy.8.exponent_ref
  1.5 0.0 copy-start.2
  1.5 0.9 copy-done.2
  2.5 0.1 shard_map.67.refs_0_
  2.6 0.3 fusion
  2.9 0.1 pad_maximum_fusion
  3.0 0.0 copy-start
  3.0 1.2 %copy-done = bf16[128,4096]{1,0:T(8,128)(2,1)S(1)} copy-done((bf16[128,4096]{1,0:T(8,128)(2,1)S(1)}, bf16[128,4096]{1,0:T(8,128)(2,1)}, u32[]{:S(2)}) %copy-start) | copy-done | bytes 1048600
  4.3 0.0 copy-start.3
  4.3 0.9 copy-done.3
  5.2 2.8 %shard_map.68 = (bf16[4,4,8,2,8,512]{5,4,3,2,1,0:T(8,128)(2,1)S(1)}, bf16[4,4,8,2,8,512]{5,4,3,2,1,0:T(8,128)(2,1)S(1)}, bf16[128,512]{1,0:T(8,128)(2,1)S(1)}) custom-call(s32[1]{0:T(128)} %bitcast.2.core_ref, bf16[128,4096]{1,0:T(8,128)(2,1)S(1)} %copy-done, bf16[128,512]{1,0:T(8,128)(2,1)S(1)} %copy-done.3, f32[128,128]{1,0:T(8,128)S(1)} %get-tuple-element.30.cos_ref, ...), custom_call_target="tpu_custom_call" | custom-call | tf_op jit(solution)/shard_map/pallas_call | solution.py:81
  7.9 8.8 %collective-permute-start.4 = (bf16[4,4,8,2,8,512]{5,4,3,2,1,0:T(8,128)(2,1)S(1)}, bf16[4,4,8,2,8,512]{5,4,3,2,1,0:T(8,128)(2,1)S(1)}, u32[]{:S(2)}, u32[]{:S(2)}) collective-permute-start(bf16[4,4,8,2,8,512]{5,4,3,2,1,0:T(8,128)(2,1)S(1)} %get-tuple-element.17), channel_id=1, source_target_pairs={{0,1},{1,0},{2,3},{3,2},{4,5},{5,4},{6,7},{7,6},{8,9},{9,8},{10,11... | collective-permute-start | bytes 6291464 | tf_op jit(solution)/shard_map/ppermute | solution.py:204
  16.7 10.1 %collective-permute-start.3 = (bf16[256,512]{1,0:T(8,128)(2,1)S(1)}, bf16[256,512]{1,0:T(8,128)(2,1)S(1)}, u32[]{:S(2)}, u32[]{:S(2)}) collective-permute-start(bf16[256,512]{1,0:T(8,128)(2,1)S(1)} %shard_map.67.refs_0_), channel_id=1, source_target_pairs={{0,2},{2,0},{1,3},{3,1},{4,6},{6,4},{5,7},{7,5},{8,10},{10,8},{9,1... | collective-permute-start | bytes 786440 | tf_op jit(solution)/shard_map/ppermute | solution.py:204
  26.8 4.4 %collective-permute-start.2 = (bf16[256,512]{1,0:T(8,128)(2,1)S(1)}, bf16[256,512]{1,0:T(8,128)(2,1)S(1)}, u32[]{:S(2)}, u32[]{:S(2)}) collective-permute-start(bf16[256,512]{1,0:T(8,128)(2,1)S(1)} %shard_map.67.refs_0_), channel_id=1, source_target_pairs={{0,12},{4,0},{8,4},{12,8},{1,13},{5,1},{9,5},{13,9},{2,14},{6,2},{... | collective-permute-start | bytes 786440 | tf_op jit(solution)/shard_map/ppermute | solution.py:199
  31.2 0.0 collective-permute-done.4
  31.2 2.4 %add_convert_fusion = bf16[4,4,8,2,8,512]{5,4,3,2,1,0:T(8,128)(2,1)} fusion(bf16[4,4,8,2,8,512]{5,4,3,2,1,0:T(8,128)(2,1)S(1)} %collective-permute-done.4, bf16[4,4,8,2,8,512]{5,4,3,2,1,0:T(8,128)(2,1)S(1)} %get-tuple-element.19), kind=kLoop, calls=%fused_computation | loop fusion | flops 4194304 | bytes 6291456 | tf_op jit(solution)/shard_map/convert_element_type | solution.py:218
  33.6 4.6 %all-to-all-start = ((bf16[16,16,8,512]{3,2,1,0:T(8,128)(2,1)}), bf16[16,16,8,512]{3,2,1,0:T(8,128)(2,1)}, u32[]{:S(2)}, u32[]{:S(2)}) async-start(bf16[16,16,8,512]{3,2,1,0:T(8,128)(2,1)} %bitcast.3), calls=%async_computation | async-start | bytes 4194304 | tf_op jit(solution)/shard_map/all_to_all | solution.py:220
  38.3 4.7 %collective-permute-start.1 = (bf16[256,512]{1,0:T(8,128)(2,1)S(1)}, bf16[256,512]{1,0:T(8,128)(2,1)S(1)}, u32[]{:S(2)}, u32[]{:S(2)}) collective-permute-start(bf16[256,512]{1,0:T(8,128)(2,1)S(1)} %shard_map.67.refs_0_), channel_id=1, source_target_pairs={{0,8},{4,12},{8,0},{12,4},{1,9},{5,13},{9,1},{13,5},{2,10},{6,14},... | collective-permute-start | bytes 786440 | tf_op jit(solution)/shard_map/ppermute | solution.py:199
  43.0 2.2 %collective-permute-start = (bf16[256,512]{1,0:T(8,128)(2,1)S(1)}, bf16[256,512]{1,0:T(8,128)(2,1)S(1)}, u32[]{:S(2)}, u32[]{:S(2)}) collective-permute-start(bf16[256,512]{1,0:T(8,128)(2,1)S(1)} %shard_map.67.refs_0_), channel_id=1, source_target_pairs={{0,4},{4,8},{8,12},{12,0},{1,5},{5,9},{9,13},{13,1},{2,6},{6,10},{... | collective-permute-start | bytes 786440 | tf_op jit(solution)/shard_map/ppermute | solution.py:199
  45.2 0.0 collective-permute-done.3.refs_4_
  45.2 4.3 %collective-permute-start.7 = (bf16[256,512]{1,0:T(8,128)(2,1)S(1)}, bf16[256,512]{1,0:T(8,128)(2,1)S(1)}, u32[]{:S(2)}, u32[]{:S(2)}) collective-permute-start(bf16[256,512]{1,0:T(8,128)(2,1)S(1)} %collective-permute-done.3.refs_4_), channel_id=1, source_target_pairs={{0,12},{4,0},{8,4},{12,8},{1,13},{5,1},{9,5},{13,9},{2,14},{6,2},{... | collective-permute-start | bytes 786440 | tf_op jit(solution)/shard_map/ppermute | solution.py:199
  49.5 1.9 %collective-permute-start.6 = (bf16[256,512]{1,0:T(8,128)(2,1)S(1)}, bf16[256,512]{1,0:T(8,128)(2,1)S(1)}, u32[]{:S(2)}, u32[]{:S(2)}) collective-permute-start(bf16[256,512]{1,0:T(8,128)(2,1)S(1)} %collective-permute-done.3.refs_4_), channel_id=1, source_target_pairs={{0,8},{4,12},{8,0},{12,4},{1,9},{5,13},{9,1},{13,5},{2,10},{6,14},... | collective-permute-start | bytes 786440 | tf_op jit(solution)/shard_map/ppermute | solution.py:199
  51.4 0.0 collective-permute-done.2.refs_3_
  51.5 2.5 %collective-permute-start.5 = (bf16[256,512]{1,0:T(8,128)(2,1)S(1)}, bf16[256,512]{1,0:T(8,128)(2,1)S(1)}, u32[]{:S(2)}, u32[]{:S(2)}) collective-permute-start(bf16[256,512]{1,0:T(8,128)(2,1)S(1)} %collective-permute-done.3.refs_4_), channel_id=1, source_target_pairs={{0,4},{4,8},{8,12},{12,0},{1,5},{5,9},{9,13},{13,1},{2,6},{6,10},{... | collective-permute-start | bytes 786440 | tf_op jit(solution)/shard_map/ppermute | solution.py:199
  53.9 15.9 %collective-permute-done.1.refs_2_ = bf16[256,512]{1,0:T(8,128)(2,1)S(1)} collective-permute-done((bf16[256,512]{1,0:T(8,128)(2,1)S(1)}, bf16[256,512]{1,0:T(8,128)(2,1)S(1)}, u32[]{:S(2)}, u32[]{:S(2)}) %collective-permute-start.1) | collective-permute-done | bytes 262176 | tf_op jit(solution)/shard_map/ppermute | solution.py:199
  69.9 4.9 %collective-permute-done.refs_1_ = bf16[256,512]{1,0:T(8,128)(2,1)S(1)} collective-permute-done((bf16[256,512]{1,0:T(8,128)(2,1)S(1)}, bf16[256,512]{1,0:T(8,128)(2,1)S(1)}, u32[]{:S(2)}, u32[]{:S(2)}) %collective-permute-start) | collective-permute-done | bytes 262176 | tf_op jit(solution)/shard_map/ppermute | solution.py:199
  74.8 0.0 collective-permute-done.7.refs_7_
  74.8 6.3 %collective-permute-done.6.refs_6_ = bf16[256,512]{1,0:T(8,128)(2,1)S(1)} collective-permute-done((bf16[256,512]{1,0:T(8,128)(2,1)S(1)}, bf16[256,512]{1,0:T(8,128)(2,1)S(1)}, u32[]{:S(2)}, u32[]{:S(2)}) %collective-permute-start.6) | collective-permute-done | bytes 262176 | tf_op jit(solution)/shard_map/ppermute | solution.py:199
  81.1 5.0 %collective-permute-done.5.refs_5_ = bf16[256,512]{1,0:T(8,128)(2,1)S(1)} collective-permute-done((bf16[256,512]{1,0:T(8,128)(2,1)S(1)}, bf16[256,512]{1,0:T(8,128)(2,1)S(1)}, u32[]{:S(2)}, u32[]{:S(2)}) %collective-permute-start.5) | collective-permute-done | bytes 262176 | tf_op jit(solution)/shard_map/ppermute | solution.py:199
  86.0 0.1 shard_map.69.weight_ref
  86.2 0.0 copy-start.1
  86.2 3.8 %collective-permute-start.8 = (bf16[2048,512]{1,0:T(8,128)(2,1)S(1)}, bf16[2048,512]{1,0:T(8,128)(2,1)}, u32[]{:S(2)}, u32[]{:S(2)}) collective-permute-start(bf16[2048,512]{1,0:T(8,128)(2,1)S(1)} %shard_map.69.weight_ref), channel_id=1, source_target_pairs={{0,1},{1,0},{2,3},{3,2},{4,5},{5,4},{6,7},{7,6},{8,9},{9,8},{10,11... | collective-permute-start | bytes 6291464 | tf_op jit(solution)/shard_map/ppermute | solution.py:204
  90.0 0.0 all-to-all-done
  90.0 2.6 %reduce_sum.21 = bf16[16,8,512]{2,1,0:T(8,128)(2,1)} reduce(bf16[16,16,8,512]{3,2,1,0:T(8,128)(2,1)} %all-to-all-done, bf16[]{:T(256)} %constant.53.clone.1), dimensions={0}, to_apply=%region_0.1 | reduce | flops 983040 | bytes 2228226 | tf_op jit(solution)/shard_map/reduce_sum | solution.py:229
  92.6 4.8 %all-to-all-start.1 = ((bf16[16,8,512]{2,1,0:T(8,128)(2,1)}), bf16[16,8,512]{2,1,0:T(8,128)(2,1)S(1)}, u32[]{:S(2)}, u32[]{:S(2)}) async-start(bf16[16,8,512]{2,1,0:T(8,128)(2,1)} %reduce_sum.21), calls=%async_computation.1 | async-start | bytes 262144 | tf_op jit(solution)/shard_map/all_to_all | solution.py:230
  97.4 0.1 pad_add_fusion.place_ref
  97.5 0.0 copy-done.1
  97.5 1.6 %shard_map.70 = (f32[128,512]{1,0:T(8,128)S(1)}, bf16[8,128,256]{2,1,0:T(8,128)(2,1)S(1)}) custom-call(s32[3]{0:T(128)S(1)} %pad_add_fusion.place_ref, bf16[128,4096]{1,0:T(8,128)(2,1)S(1)} %copy-done.1, bf16[128,512]{1,0:T(8,128)(2,1)S(1)} %get-tuple-element.16.pre_ref, bf16[2048,512]{1,0:T(8,128)(2,1)S(1)} %shard_map.69.weight_ref), custom_call_target="tpu_custom_call" | custom-call | flops 536870912 | bytes 4194304 | tf_op jit(solution)/shard_map/pallas_call | solution.py:166
  99.1 0.0 collective-permute-done.8.weight_ref
  99.1 3.6 %shard_map.71 = (bf16[128,512]{1,0:T(8,128)(2,1)}, bf16[128,4096]{1,0:T(8,128)(2,1)}) custom-call(s32[3]{0:T(128)S(1)} %pad_add_fusion.place_ref, bf16[128,4096]{1,0:T(8,128)(2,1)S(1)} %copy-done.1, bf16[128,512]{1,0:T(8,128)(2,1)S(1)} %get-tuple-element.16.pre_ref, f32[128,128]{1,0:T(8,128)S(1)} %get-tuple-element.30.cos_ref, ...), custom_call_target="tpu_custom_call" | custom-call | flops 536870912 | bytes 4194304 | tf_op jit(solution)/shard_map/pallas_call | solution.py:181
  102.7 8.1 %all-to-all-done.1 = bf16[16,8,512]{2,1,0:T(8,128)(2,1)S(1)} async-done(((bf16[16,8,512]{2,1,0:T(8,128)(2,1)}), bf16[16,8,512]{2,1,0:T(8,128)(2,1)S(1)}, u32[]{:S(2)}, u32[]{:S(2)}) %all-to-all-start.1) | async-done | bytes 131104 | tf_op jit(solution)/shard_map/all_to_all | solution.py:230
  110.8 0.6 broadcast_multiply_fusion
  (3 shorter events, 0.0 us)
Async XLA Ops:
  1.5 1.0 copy-start.2
  3.0 1.2 %copy-start = (bf16[128,4096]{1,0:T(8,128)(2,1)S(1)}, bf16[128,4096]{1,0:T(8,128)(2,1)}, u32[]{:S(2)}) copy-start(bf16[128,4096]{1,0:T(8,128)(2,1)} %token_ref.4) | copy-start | bytes 3145732
  4.3 0.9 copy-start.3
  7.9 23.3 %collective-permute-start.4 = (bf16[4,4,8,2,8,512]{5,4,3,2,1,0:T(8,128)(2,1)S(1)}, bf16[4,4,8,2,8,512]{5,4,3,2,1,0:T(8,128)(2,1)S(1)}, u32[]{:S(2)}, u32[]{:S(2)}) collective-permute-start(bf16[4,4,8,2,8,512]{5,4,3,2,1,0:T(8,128)(2,1)S(1)} %get-tuple-element.17), channel_id=1, source_target_pairs={{0,1},{1,0},{2,3},{3,2},{4,5},{5,4},{6,7},{7,6},{8,9},{9,8},{10,11... | collective-permute-start | bytes 6291464 | tf_op jit(solution)/shard_map/ppermute | solution.py:204
  16.7 28.5 %collective-permute-start.3 = (bf16[256,512]{1,0:T(8,128)(2,1)S(1)}, bf16[256,512]{1,0:T(8,128)(2,1)S(1)}, u32[]{:S(2)}, u32[]{:S(2)}) collective-permute-start(bf16[256,512]{1,0:T(8,128)(2,1)S(1)} %shard_map.67.refs_0_), channel_id=1, source_target_pairs={{0,2},{2,0},{1,3},{3,1},{4,6},{6,4},{5,7},{7,5},{8,10},{10,8},{9,1... | collective-permute-start | bytes 786440 | tf_op jit(solution)/shard_map/ppermute | solution.py:204
  26.8 24.6 %collective-permute-start.2 = (bf16[256,512]{1,0:T(8,128)(2,1)S(1)}, bf16[256,512]{1,0:T(8,128)(2,1)S(1)}, u32[]{:S(2)}, u32[]{:S(2)}) collective-permute-start(bf16[256,512]{1,0:T(8,128)(2,1)S(1)} %shard_map.67.refs_0_), channel_id=1, source_target_pairs={{0,12},{4,0},{8,4},{12,8},{1,13},{5,1},{9,5},{13,9},{2,14},{6,2},{... | collective-permute-start | bytes 786440 | tf_op jit(solution)/shard_map/ppermute | solution.py:199
  33.6 56.3 %all-to-all-start = ((bf16[16,16,8,512]{3,2,1,0:T(8,128)(2,1)}), bf16[16,16,8,512]{3,2,1,0:T(8,128)(2,1)}, u32[]{:S(2)}, u32[]{:S(2)}) async-start(bf16[16,16,8,512]{3,2,1,0:T(8,128)(2,1)} %bitcast.3), calls=%async_computation | async-start | bytes 4194304 | tf_op jit(solution)/shard_map/all_to_all | solution.py:220
  38.3 31.6 %collective-permute-start.1 = (bf16[256,512]{1,0:T(8,128)(2,1)S(1)}, bf16[256,512]{1,0:T(8,128)(2,1)S(1)}, u32[]{:S(2)}, u32[]{:S(2)}) collective-permute-start(bf16[256,512]{1,0:T(8,128)(2,1)S(1)} %shard_map.67.refs_0_), channel_id=1, source_target_pairs={{0,8},{4,12},{8,0},{12,4},{1,9},{5,13},{9,1},{13,5},{2,10},{6,14},... | collective-permute-start | bytes 786440 | tf_op jit(solution)/shard_map/ppermute | solution.py:199
  43.0 31.8 %collective-permute-start = (bf16[256,512]{1,0:T(8,128)(2,1)S(1)}, bf16[256,512]{1,0:T(8,128)(2,1)S(1)}, u32[]{:S(2)}, u32[]{:S(2)}) collective-permute-start(bf16[256,512]{1,0:T(8,128)(2,1)S(1)} %shard_map.67.refs_0_), channel_id=1, source_target_pairs={{0,4},{4,8},{8,12},{12,0},{1,5},{5,9},{9,13},{13,1},{2,6},{6,10},{... | collective-permute-start | bytes 786440 | tf_op jit(solution)/shard_map/ppermute | solution.py:199
  45.2 29.6 %collective-permute-start.7 = (bf16[256,512]{1,0:T(8,128)(2,1)S(1)}, bf16[256,512]{1,0:T(8,128)(2,1)S(1)}, u32[]{:S(2)}, u32[]{:S(2)}) collective-permute-start(bf16[256,512]{1,0:T(8,128)(2,1)S(1)} %collective-permute-done.3.refs_4_), channel_id=1, source_target_pairs={{0,12},{4,0},{8,4},{12,8},{1,13},{5,1},{9,5},{13,9},{2,14},{6,2},{... | collective-permute-start | bytes 786440 | tf_op jit(solution)/shard_map/ppermute | solution.py:199
  49.5 31.5 %collective-permute-start.6 = (bf16[256,512]{1,0:T(8,128)(2,1)S(1)}, bf16[256,512]{1,0:T(8,128)(2,1)S(1)}, u32[]{:S(2)}, u32[]{:S(2)}) collective-permute-start(bf16[256,512]{1,0:T(8,128)(2,1)S(1)} %collective-permute-done.3.refs_4_), channel_id=1, source_target_pairs={{0,8},{4,12},{8,0},{12,4},{1,9},{5,13},{9,1},{13,5},{2,10},{6,14},... | collective-permute-start | bytes 786440 | tf_op jit(solution)/shard_map/ppermute | solution.py:199
  51.5 34.6 %collective-permute-start.5 = (bf16[256,512]{1,0:T(8,128)(2,1)S(1)}, bf16[256,512]{1,0:T(8,128)(2,1)S(1)}, u32[]{:S(2)}, u32[]{:S(2)}) collective-permute-start(bf16[256,512]{1,0:T(8,128)(2,1)S(1)} %collective-permute-done.3.refs_4_), channel_id=1, source_target_pairs={{0,4},{4,8},{8,12},{12,0},{1,5},{5,9},{9,13},{13,1},{2,6},{6,10},{... | collective-permute-start | bytes 786440 | tf_op jit(solution)/shard_map/ppermute | solution.py:199
  86.2 11.3 %copy-start.1 = (bf16[128,4096]{1,0:T(8,128)(2,1)S(1)}, bf16[128,4096]{1,0:T(8,128)(2,1)}, u32[]{:S(2)}) copy-start(bf16[128,4096]{1,0:T(8,128)(2,1)} %token_ref.4) | copy-start | bytes 3145732
  86.2 12.9 %collective-permute-start.8 = (bf16[2048,512]{1,0:T(8,128)(2,1)S(1)}, bf16[2048,512]{1,0:T(8,128)(2,1)}, u32[]{:S(2)}, u32[]{:S(2)}) collective-permute-start(bf16[2048,512]{1,0:T(8,128)(2,1)S(1)} %shard_map.69.weight_ref), channel_id=1, source_target_pairs={{0,1},{1,0},{2,3},{3,2},{4,5},{5,4},{6,7},{7,6},{8,9},{9,8},{10,11... | collective-permute-start | bytes 6291464 | tf_op jit(solution)/shard_map/ppermute | solution.py:204
  92.6 18.2 %all-to-all-start.1 = ((bf16[16,8,512]{2,1,0:T(8,128)(2,1)}), bf16[16,8,512]{2,1,0:T(8,128)(2,1)S(1)}, u32[]{:S(2)}, u32[]{:S(2)}) async-start(bf16[16,8,512]{2,1,0:T(8,128)(2,1)} %reduce_sum.21), calls=%async_computation.1 | async-start | bytes 262144 | tf_op jit(solution)/shard_map/all_to_all | solution.py:230

commit v3 on v1

v3 whole, which is shorter than its diff:
```python
import math

import jax
import jax.numpy as jnp
from jax import lax
from jax.experimental import pallas as pl
from jax.experimental.pallas import tpu as pltpu
from jax.sharding import Mesh
from jax.sharding import PartitionSpec as P

KVH = 4
HEAD = 128
QBLOCK = 256
SEQ = 8192
THETA = 500000.0

Y, ZL, X, ZH, CORE = 4, 8, 4, 2, 2
AXES = ("y", "zl", "x", "zh", "core")
ROW = 8

F32 = jnp.float32
BF16 = jnp.bfloat16
PARAMS = pltpu.CompilerParams(vmem_limit_bytes=20 * 1024 * 1024)
SMEM = pl.BlockSpec(memory_space=pltpu.SMEM)
VMEM = pl.BlockSpec(memory_space=pltpu.VMEM)


def dequantize_kernel(code_ref, exponent_ref, weight_ref):
    scale = jnp.exp2(exponent_ref[...].astype(F32))
    for block in range(code_ref.shape[1] // QBLOCK):
        columns = slice(block * QBLOCK, (block + 1) * QBLOCK)
        value = code_ref[:, columns].astype(F32) * scale[:, block : block + 1]
        weight_ref[:, columns] = value.astype(BF16)


def dequantize(key_codes, key_exponents):
    return pl.pallas_call(
        dequantize_kernel,
        out_shape=jax.ShapeDtypeStruct(key_codes.shape, BF16),
        compiler_params=PARAMS,
    )(key_codes, key_exponents)


def tables(positions):
    inverse = THETA ** (-(jnp.arange(HEAD // 2, dtype=F32) * 2.0 / HEAD))
    angles = positions.astype(F32)[:, None] * inverse[None, :]
    cosine, sine = jnp.cos(angles), jnp.sin(angles)
    return (
        jnp.concatenate([cosine, cosine], axis=1),
        jnp.concatenate([-sine, sine], axis=1),
    )


def pack_kernel(token_ref, cot_ref, cos_ref, sin_ref, packed_ref, pre_ref):
    width = token_ref.shape[1]

    @pl.when(pl.program_id(0) == 0)
    def _():
        for head in range(KVH):
            columns = slice(head * HEAD, (head + 1) * HEAD)
            value = cot_ref[:, columns].astype(F32)
            turned = pltpu.roll(value, HEAD // 2, 1)
            pre_ref[:, columns] = (value * cos_ref[...] - turned * sin_ref[...]).astype(BF16)

    packed_ref[0, :, :width] = token_ref[...]
    packed_ref[0, :, width:] = pre_ref[...]


def packed_for_y(tokens, key_cotangent, cosine, sine):
    count, width = tokens.shape
    features = key_cotangent.shape[1]
    whole = lambda y: (0, 0)
    return pl.pallas_call(
        pack_kernel,
        grid=(Y,),
        in_specs=[
            pl.BlockSpec((count, width // Y), lambda y: (0, y)),
            pl.BlockSpec((count, features), whole),
            pl.BlockSpec((count, HEAD), whole),
            pl.BlockSpec((count, HEAD), whole),
        ],
        out_specs=pl.BlockSpec((1, count, width // Y + features), lambda y: (y, 0, 0)),
        out_shape=jax.ShapeDtypeStruct((Y, count, width // Y + features), BF16),
        scratch_shapes=[pltpu.VMEM((count, features), BF16)],
        compiler_params=PARAMS,
    )(tokens, key_cotangent, cosine, sine)


def partial_kernel(token_ref, pre_ref, part_ref):
    rows = token_ref.shape[0] * token_ref.shape[1]
    part = lax.dot_general(
        token_ref[...].reshape(rows, token_ref.shape[2]),
        pre_ref[...].reshape(rows, pre_ref.shape[2]),
        (((0,), (0,)), ((), ())),
        preferred_element_type=F32,
    )
    part = part.reshape(-1, ROW, part.shape[1])
    for zl in range(part_ref.shape[2]):
        for x in range(X):
            for zh in range(ZH):
                for core in range(CORE):
                    place = ((zl * X + x) * ZH + zh) * CORE + core
                    part_ref[x, core, zl, zh] = part[place].astype(BF16)


def partial_products(got, features):
    count = got.shape[1]
    width = got.shape[2] - features
    steps = 4
    return pl.pallas_call(
        partial_kernel,
        grid=(steps,),
        in_specs=[
            pl.BlockSpec((Y, count, width // steps), lambda i: (0, 0, i)),
            pl.BlockSpec((Y, count, features), lambda i: (0, 0, width // features)),
        ],
        out_specs=pl.BlockSpec(
            (X, CORE, ZL // steps, ZH, ROW, features), lambda i: (0, 0, i, 0, 0, 0)
        ),
        out_shape=jax.ShapeDtypeStruct((X, CORE, ZL, ZH, ROW, features), BF16),
        compiler_params=PARAMS,
    )(got, got)


def apply_kernel(place_ref, got_ref, w00_ref, w01_ref, w10_ref, w11_ref, *out_refs):
    y, zh, core = place_ref[0], place_ref[1], place_ref[2]
    rows, features = w00_ref.shape
    width = ZH * CORE * rows
    held = ((w00_ref, zh, core), (w01_ref, zh, 1 - core), (w10_ref, 1 - zh, core), (w11_ref, 1 - zh, 1 - core))
    for ahead, out_ref in enumerate(out_refs):
        target = lax.rem(y + ahead, Y)
        pre = got_ref[target, :, width:]
        total = jnp.zeros(pre.shape, F32)
        for weight_ref, near, side in held:
            start = pl.multiple_of((near * CORE + side) * rows, rows)
            weight = weight_ref[...]
            total += jnp.dot(
                got_ref[target, :, pl.ds(start, rows)], weight, preferred_element_type=F32
            )
            out_ref[:, pl.ds(start, rows)] = lax.dot_general(
                pre, weight, (((1,), (1,)), ((), ())), preferred_element_type=F32
            ).astype(BF16)
        out_ref[:, width:] = total.astype(BF16)


def apply_weights(place, got, weights):
    count = got.shape[1]
    one = jax.ShapeDtypeStruct((count, got.shape[2]), BF16)
    return pl.pallas_call(
        apply_kernel,
        in_specs=[SMEM] + [VMEM] * 5,
        out_specs=[VMEM] * Y,
        out_shape=[one] * Y,
        compiler_params=PARAMS,
        cost_estimate=pl.CostEstimate(
            flops=2 * 2 * count * Y * got.shape[2] * 512,
            bytes_accessed=6 * 1024 * 1024,
            transcendentals=0,
        ),
    )(place, got, *weights)


def finish_kernel(place_ref, cos_ref, sin_ref, *refs):
    got_refs, keys_ref, grad_ref = refs[:Y], refs[Y], refs[Y + 1]
    width = grad_ref.shape[1] // Y
    for behind, got_ref in enumerate(got_refs):
        source = lax.rem(place_ref[0] + (Y - behind), Y)
        start = pl.multiple_of(source * width, width)
        grad_ref[:, pl.ds(start, width)] = got_ref[:, :width]
    for head in range(KVH):
        columns = slice(width + head * HEAD, width + (head + 1) * HEAD)
        value = sum(got_ref[:, columns].astype(F32) for got_ref in got_refs)
        turned = pltpu.roll(value, HEAD // 2, 1)
        columns = slice(head * HEAD, (head + 1) * HEAD)
        keys_ref[:, columns] = (value * cos_ref[...] + turned * sin_ref[...]).astype(BF16)


def finished(place, cosine, sine, got):
    count, width = got[0].shape
    features = KVH * HEAD
    return pl.pallas_call(
        finish_kernel,
        in_specs=[SMEM] + [VMEM] * (2 + Y),
        out_specs=[VMEM, VMEM],
        out_shape=[
            jax.ShapeDtypeStruct((count, features), BF16),
            jax.ShapeDtypeStruct((count, (width - features) * Y), BF16),
        ],
        compiler_params=PARAMS,
    )(place, cosine, sine, *got)


def swap(value, axis):
    return lax.ppermute(value, axis, [(0, 1), (1, 0)])


def turned_round(value, flip):
    pairs = []
    for y in range(Y):
        for x in range(X):
            for zh in range(ZH):
                source = (y * X + x) * ZH + zh
                pairs.append((source, (x * X + y) * ZH + (zh ^ flip)))
    return lax.ppermute(value, ("y", "x", "zh"), pairs)


def after(value, *others):
    return lax.optimization_barrier((value, *others))[0]


def on_device(tokens, key_codes, key_exponents, key_cotangent):
    y, zl, x, zh, core = [lax.axis_index(name) for name in AXES]
    count = tokens.shape[0]
    features = key_cotangent.shape[1]
    place = jnp.stack([y, zh, core])

    shard = dequantize(key_codes, key_exponents)
    near = turned_round(shard, 0)
    far = turned_round(shard, 1)

    device_index = (((y * ZL + zl) * X + x) * ZH + zh) * CORE + core
    positions = (device_index * count + jnp.arange(count, dtype=jnp.int32)) % SEQ
    cosine, sine = tables(positions)
    packed = packed_for_y(tokens, key_cotangent, cosine, sine)
    got = lax.all_to_all(packed, "y", split_axis=0, concat_axis=0, tiled=True)
    got = after(got, near, far)

    part = partial_products(got, features).reshape(X * CORE, ZL * ZH, ROW, features)
    parts = lax.all_to_all(part, ("x", "core"), split_axis=0, concat_axis=0, tiled=True)

    weights = (near, swap(near, "core"), far, swap(far, "core"))
    applied = apply_weights(place, after(got, part), weights)
    moved = [
        lax.ppermute(applied[k], "y", [(i, (i + k) % Y) for i in range(Y)]) for k in range(1, Y)
    ]

    parts = after(parts, *applied)
    summed = jnp.sum(parts.astype(F32), axis=0).astype(BF16)
    parts = lax.all_to_all(summed, ("zl", "zh"), split_axis=0, concat_axis=0, tiled=True)

    got = [applied[0], *[after(value, summed) for value in moved]]
    keys, input_grad = finished(place, cosine, sine, got)
    parts = after(parts, keys)
    total_tokens = count * Y * ZL * X * ZH * CORE
    weight_grad = jnp.sum(parts.astype(F32), axis=0) * (1.0 / math.sqrt(total_tokens))
    return keys, input_grad, weight_grad


def solution(mesh):
    fine = Mesh(mesh.devices.reshape(Y, ZL, X, ZH, CORE), AXES)
    split = P(AXES, None)
    return jax.shard_map(
        on_device,
        mesh=fine,
        in_specs=(split, P(("x", "zh", "core"), None), P(("x", "zh", "core"), None), split),
        out_specs=(split, split, split),
        check_vma=False,
    )
```

time: 142 us -> 124 us (0.87)
  the two profiles are of different devices: /device:TPU:16 before, /device:TPU:1 now
where the time goes in v3:
time: 124 us
  starting transfers between devices  82 us (66%)
  waiting for transfers between devices  25.6 us (21%)
  Pallas kernels  8.76 us (7%)
  local copies, waits for them, and re-layouts  3.22 us (3%)
  other arithmetic  3.2 us (3%)
    all_to_all x1, starting transfers between devices, on_device(): lax.all_to_all(part, ('x', 'core'), split_axis=0, concat_axis=0, tiled=True)  28 us
    all_to_all x1, starting transfers between devices, on_device(): lax.all_to_all(summed, ('zl', 'zh'), split_axis=0, concat_axis=0, tiled=T...  18.3 us
    ppermute x2, starting transfers between devices, turned_round(): return lax.ppermute(value, ('y', 'x', 'zh'), pairs)  16.1 us
    ppermute x3, waiting for transfers between devices, on_device(): lax.ppermute(applied[k], 'y', [(i, (i + k) % Y) for i in range(Y)])  14.3 us
    ppermute x3, starting transfers between devices, on_device(): lax.ppermute(applied[k], 'y', [(i, (i + k) % Y) for i in range(Y)])  10.1 us
    all_to_all x1, waiting for transfers between devices, on_device(): lax.all_to_all(part, ('x', 'core'), split_axis=0, concat_axis=0, tiled=True)  6.27 us
    all_to_all x1, starting transfers between devices, on_device(): got = lax.all_to_all(packed, 'y', split_axis=0, concat_axis=0, tiled=True)  5.14 us
    ppermute x2, starting transfers between devices, swap(): return lax.ppermute(value, axis, [(0, 1), (1, 0)])  4.31 us
  transfers between devices with their start and end apart: 10, of which 6 were waited for; matrix products, arithmetic and copies ran while one was open for 0% of the time, Pallas kernels for 4%

profile of v3, /device:TPU:1, one launch (start us, length us, event | category | flops | bytes accessed | tf_op | source)
XLA Modules:
  0.0 123.6 jit_solution(16272598216064424100)
XLA Ops:
  0.7 0.3 fusion
  1.0 0.1 pad_maximum_fusion
  1.1 0.0 copy-start
  1.1 1.2 copy-done
  2.3 0.0 copy-start.2
  2.3 0.9 copy-done.2
  3.2 1.9 %shard_map.67 = bf16[4,128,1536]{2,1,0:T(8,128)(2,1)} custom-call(bf16[128,4096]{1,0:T(8,128)(2,1)S(1)} %copy-done, bf16[128,512]{1,0:T(8,128)(2,1)S(1)} %copy-done.2, f32[128,128]{1,0:T(8,128)S(1)} %get-tuple-element.32.cos_ref, f32[128,128]{1,0:T(8,128)S(1)} %get-tuple-element.33.sin_ref), custom_call_target="tpu_custom_call" | custom-call | tf_op jit(solution)/shard_map/pallas_call | solution.py:73
  5.1 0.0 copy-start.5
  5.1 0.0 copy-start.1
  5.1 5.1 %all-to-all-start = ((bf16[4,128,1536]{2,1,0:T(8,128)(2,1)}), bf16[4,128,1536]{2,1,0:T(8,128)(2,1)S(1)}, u32[]{:S(2)}, u32[]{:S(2)}) async-start(bf16[4,128,1536]{2,1,0:T(8,128)(2,1)} %shard_map.67), calls=%async_computation | async-start | bytes 3145728 | tf_op jit(solution)/shard_map/all_to_all | solution.py:225
  10.3 0.0 copy-done.5
  10.3 0.1 copy.8.exponent_ref
  10.4 0.0 copy-done.1
  10.4 0.1 shard_map.68
  10.6 15.4 %collective-permute-start.1 = (bf16[256,512]{1,0:T(8,128)(2,1)S(1)}, bf16[256,512]{1,0:T(8,128)(2,1)S(1)}, u32[]{:S(2)}, u32[]{:S(2)}) collective-permute-start(bf16[256,512]{1,0:T(8,128)(2,1)S(1)} %shard_map.68), channel_id=1, source_target_pairs={{0,2},{2,0},{4,130},{6,128},{8,258},{10,256},{12,386},{14,384},{12... | collective-permute-start | bytes 786440 | tf_op jit(solution)/shard_map/ppermute | solution.py:204
  26.0 0.7 collective-permute-start
  26.7 4.0 %collective-permute-done.1.w10_ref = bf16[256,512]{1,0:T(8,128)(2,1)S(1)} collective-permute-done((bf16[256,512]{1,0:T(8,128)(2,1)S(1)}, bf16[256,512]{1,0:T(8,128)(2,1)S(1)}, u32[]{:S(2)}, u32[]{:S(2)}) %collective-permute-start.1) | collective-permute-done | bytes 262176 | tf_op jit(solution)/shard_map/ppermute | solution.py:204
  30.8 0.0 collective-permute-done.w00_ref
  30.8 0.0 copy-start.3
  30.8 0.0 all-to-all-done.token_ref.pre_ref.got_ref
  30.8 2.5 %shard_map.69 = bf16[4,2,8,2,8,512]{5,4,3,2,1,0:T(8,128)(2,1)} custom-call(bf16[4,128,1536]{2,1,0:T(8,128)(2,1)S(1)} %all-to-all-done.token_ref.pre_ref.got_ref, bf16[4,128,1536]{2,1,0:T(8,128)(2,1)S(1)} %all-to-all-done.token_ref.pre_ref.got_ref), custom_call_target="tpu_custom_call" | custom-call | tf_op jit(solution)/shard_map/pallas_call | solution.py:110
  33.3 28.0 %all-to-all-start.1 = ((bf16[8,16,8,512]{3,2,1,0:T(8,128)(2,1)}), bf16[8,16,8,512]{3,2,1,0:T(8,128)(2,1)}, u32[]{:S(2)}, u32[]{:S(2)}) async-start(bf16[8,16,8,512]{3,2,1,0:T(8,128)(2,1)} %bitcast.3), calls=%async_computation.1 | async-start | bytes 2097152 | tf_op jit(solution)/shard_map/all_to_all | solution.py:229
  61.3 1.9 %collective-permute-start.3 = (bf16[256,512]{1,0:T(8,128)(2,1)S(1)}, bf16[256,512]{1,0:T(8,128)(2,1)S(1)}, u32[]{:S(2)}, u32[]{:S(2)}) collective-permute-start(bf16[256,512]{1,0:T(8,128)(2,1)S(1)} %collective-permute-done.1.w10_ref), channel_id=1, source_target_pairs={{0,1},{1,0},{2,3},{3,2},{4,5},{5,4},{6,7},{7,6},{8,9},{9,8},{10,11... | collective-permute-start | bytes 786440 | tf_op jit(solution)/shard_map/ppermute | solution.py:194
  63.2 0.0 copy-done.3
  63.3 2.4 %collective-permute-start.2 = (bf16[256,512]{1,0:T(8,128)(2,1)S(1)}, bf16[256,512]{1,0:T(8,128)(2,1)S(1)}, u32[]{:S(2)}, u32[]{:S(2)}) collective-permute-start(bf16[256,512]{1,0:T(8,128)(2,1)S(1)} %collective-permute-done.w00_ref), channel_id=1, source_target_pairs={{0,1},{1,0},{2,3},{3,2},{4,5},{5,4},{6,7},{7,6},{8,9},{9,8},{10,11... | collective-permute-start | bytes 786440 | tf_op jit(solution)/shard_map/ppermute | solution.py:194
  65.7 0.1 pad_add_fusion.place_ref
  65.7 0.0 collective-permute-done.3.w11_ref
  65.7 1.1 collective-permute-done.2.w01_ref
  66.8 0.0 copy-start.4
  66.8 0.9 copy-done.4
  67.8 2.5 %shard_map.70 = (bf16[128,1536]{1,0:T(8,128)(2,1)S(1)}, bf16[128,1536]{1,0:T(8,128)(2,1)S(1)}, bf16[128,1536]{1,0:T(8,128)(2,1)S(1)}, bf16[128,1536]{1,0:T(8,128)(2,1)S(1)}) custom-call(s32[3]{0:T(128)S(1)} %pad_add_fusion.place_ref, bf16[4,128,1536]{2,1,0:T(8,128)(2,1)S(1)} %all-to-all-done.token_ref.pre_ref.got_ref, bf16[256,512]{1,0:T(8,128)(2,1)S(1)} %copy-done.4, ...), custom_call_target="tpu_custom_call" | custom-call | flops 1610612736 | bytes 6291456 | tf_op jit(solution)/shard_map/pallas_call | solution.py:149
  70.3 6.3 %all-to-all-done.1 = bf16[8,16,8,512]{3,2,1,0:T(8,128)(2,1)} async-done(((bf16[8,16,8,512]{3,2,1,0:T(8,128)(2,1)}), bf16[8,16,8,512]{3,2,1,0:T(8,128)(2,1)}, u32[]{:S(2)}, u32[]{:S(2)}) %all-to-all-start.1) | async-done | bytes 1048608 | tf_op jit(solution)/shard_map/all_to_all | solution.py:229
  76.5 2.1 %reduce_sum.21 = bf16[16,8,512]{2,1,0:T(8,128)(2,1)} reduce(bf16[8,16,8,512]{3,2,1,0:T(8,128)(2,1)} %all-to-all-done.1, bf16[]{:T(256)} %constant.53.clone.1), dimensions={0}, to_apply=%region_0.1 | reduce | flops 458752 | bytes 1179650 | tf_op jit(solution)/shard_map/reduce_sum | solution.py:238
  78.6 18.3 %all-to-all-start.2 = ((bf16[16,8,512]{2,1,0:T(8,128)(2,1)}), bf16[16,8,512]{2,1,0:T(8,128)(2,1)S(1)}, u32[]{:S(2)}, u32[]{:S(2)}) async-start(bf16[16,8,512]{2,1,0:T(8,128)(2,1)} %reduce_sum.21), calls=%async_computation.2 | async-start | bytes 262144 | tf_op jit(solution)/shard_map/all_to_all | solution.py:239
  96.9 1.9 %collective-permute-start.4 = (bf16[128,1536]{1,0:T(8,128)(2,1)S(1)}, bf16[128,1536]{1,0:T(8,128)(2,1)S(1)}, u32[]{:S(2)}, u32[]{:S(2)}) collective-permute-start(bf16[128,1536]{1,0:T(8,128)(2,1)S(1)} %get-tuple-element.19), channel_id=1, source_target_pairs={{0,128},{128,256},{256,384},{384,0},{1,129},{129,257},{257,385},{3... | collective-permute-start | bytes 1179656 | tf_op jit(solution)/shard_map/ppermute | solution.py:234
  98.8 6.1 %collective-permute-start.5 = (bf16[128,1536]{1,0:T(8,128)(2,1)S(1)}, bf16[128,1536]{1,0:T(8,128)(2,1)S(1)}, u32[]{:S(2)}, u32[]{:S(2)}) collective-permute-start(bf16[128,1536]{1,0:T(8,128)(2,1)S(1)} %get-tuple-element.20), channel_id=1, source_target_pairs={{0,256},{128,384},{256,0},{384,128},{1,257},{129,385},{257,1},{385... | collective-permute-start | bytes 1179656 | tf_op jit(solution)/shard_map/ppermute | solution.py:234
  104.9 2.1 %collective-permute-start.6 = (bf16[128,1536]{1,0:T(8,128)(2,1)S(1)}, bf16[128,1536]{1,0:T(8,128)(2,1)S(1)}, u32[]{:S(2)}, u32[]{:S(2)}) collective-permute-start(bf16[128,1536]{1,0:T(8,128)(2,1)S(1)} %get-tuple-element.21), channel_id=1, source_target_pairs={{0,384},{128,0},{256,128},{384,256},{1,385},{129,1},{257,129},{385... | collective-permute-start | bytes 1179656 | tf_op jit(solution)/shard_map/ppermute | solution.py:234
  107.0 3.1 %collective-permute-done.4.refs_1_ = bf16[128,1536]{1,0:T(8,128)(2,1)S(1)} collective-permute-done((bf16[128,1536]{1,0:T(8,128)(2,1)S(1)}, bf16[128,1536]{1,0:T(8,128)(2,1)S(1)}, u32[]{:S(2)}, u32[]{:S(2)}) %collective-permute-start.4) | collective-permute-done | bytes 393248 | tf_op jit(solution)/shard_map/ppermute | solution.py:234
  110.1 9.3 %collective-permute-done.5.refs_2_ = bf16[128,1536]{1,0:T(8,128)(2,1)S(1)} collective-permute-done((bf16[128,1536]{1,0:T(8,128)(2,1)S(1)}, bf16[128,1536]{1,0:T(8,128)(2,1)S(1)}, u32[]{:S(2)}, u32[]{:S(2)}) %collective-permute-start.5) | collective-permute-done | bytes 393248 | tf_op jit(solution)/shard_map/ppermute | solution.py:234
  119.4 1.9 %collective-permute-done.6.refs_3_ = bf16[128,1536]{1,0:T(8,128)(2,1)S(1)} collective-permute-done((bf16[128,1536]{1,0:T(8,128)(2,1)S(1)}, bf16[128,1536]{1,0:T(8,128)(2,1)S(1)}, u32[]{:S(2)}, u32[]{:S(2)}) %collective-permute-start.6) | collective-permute-done | bytes 393248 | tf_op jit(solution)/shard_map/ppermute | solution.py:234
  121.3 1.7 %shard_map.71 = (bf16[128,512]{1,0:T(8,128)(2,1)}, bf16[128,4096]{1,0:T(8,128)(2,1)}) custom-call(s32[3]{0:T(128)S(1)} %pad_add_fusion.place_ref, f32[128,128]{1,0:T(8,128)S(1)} %get-tuple-element.32.cos_ref, f32[128,128]{1,0:T(8,128)S(1)} %get-tuple-element.33.sin_ref, bf16[128,1536]{1,0:T(8,128)(2,1)S(1)} %get-tuple-element.18.refs_0_, ...), custom_call_target="tpu_custom_call" | custom-call | tf_op jit(solution)/shard_map/pallas_call | solution.py:181
  123.0 0.0 all-to-all-done.2
  123.0 0.6 broadcast_multiply_fusion
  (3 shorter events, 0.0 us)
Async XLA Ops:
  1.1 1.2 copy-start
  2.3 0.9 copy-start.2
  5.1 5.2 %copy-start.5 = (s32[256,2]{0,1:T(2,128)S(1)}, s32[256,2]{0,1:T(2,128)}, u32[]{:S(2)}) copy-start(s32[256,2]{0,1:T(2,128)} %param.6) | copy-start | bytes 6148
  5.1 5.3 %copy-start.1 = (bf16[256,512]{1,0:T(8,128)(2,1)S(1)}, bf16[256,512]{1,0:T(8,128)(2,1)}, u32[]{:S(2)}) copy-start(bf16[256,512]{1,0:T(8,128)(2,1)} %code_ref.1) | copy-start | bytes 786436
  5.1 25.6 %all-to-all-start = ((bf16[4,128,1536]{2,1,0:T(8,128)(2,1)}), bf16[4,128,1536]{2,1,0:T(8,128)(2,1)S(1)}, u32[]{:S(2)}, u32[]{:S(2)}) async-start(bf16[4,128,1536]{2,1,0:T(8,128)(2,1)} %shard_map.67), calls=%async_computation | async-start | bytes 3145728 | tf_op jit(solution)/shard_map/all_to_all | solution.py:225
  10.6 20.2 %collective-permute-start.1 = (bf16[256,512]{1,0:T(8,128)(2,1)S(1)}, bf16[256,512]{1,0:T(8,128)(2,1)S(1)}, u32[]{:S(2)}, u32[]{:S(2)}) collective-permute-start(bf16[256,512]{1,0:T(8,128)(2,1)S(1)} %shard_map.68), channel_id=1, source_target_pairs={{0,2},{2,0},{4,130},{6,128},{8,258},{10,256},{12,386},{14,384},{12... | collective-permute-start | bytes 786440 | tf_op jit(solution)/shard_map/ppermute | solution.py:204
  26.0 4.7 %collective-permute-start = (bf16[256,512]{1,0:T(8,128)(2,1)S(1)}, bf16[256,512]{1,0:T(8,128)(2,1)S(1)}, u32[]{:S(2)}, u32[]{:S(2)}) collective-permute-start(bf16[256,512]{1,0:T(8,128)(2,1)S(1)} %shard_map.68), channel_id=1, source_target_pairs={{0,0},{2,2},{4,128},{6,130},{8,256},{10,258},{12,384},{14,386},{12... | collective-permute-start | bytes 786440 | tf_op jit(solution)/shard_map/ppermute | solution.py:204
  30.8 32.5 %copy-start.3 = (bf16[256,512]{1,0:T(8,128)(2,1)}, bf16[256,512]{1,0:T(8,128)(2,1)S(1)}, u32[]{:S(2)}) copy-start(bf16[256,512]{1,0:T(8,128)(2,1)S(1)} %collective-permute-done.w00_ref) | copy-start | bytes 786436
  33.3 43.2 %all-to-all-start.1 = ((bf16[8,16,8,512]{3,2,1,0:T(8,128)(2,1)}), bf16[8,16,8,512]{3,2,1,0:T(8,128)(2,1)}, u32[]{:S(2)}, u32[]{:S(2)}) async-start(bf16[8,16,8,512]{3,2,1,0:T(8,128)(2,1)} %bitcast.3), calls=%async_computation.1 | async-start | bytes 2097152 | tf_op jit(solution)/shard_map/all_to_all | solution.py:229
  61.3 4.4 %collective-permute-start.3 = (bf16[256,512]{1,0:T(8,128)(2,1)S(1)}, bf16[256,512]{1,0:T(8,128)(2,1)S(1)}, u32[]{:S(2)}, u32[]{:S(2)}) collective-permute-start(bf16[256,512]{1,0:T(8,128)(2,1)S(1)} %collective-permute-done.1.w10_ref), channel_id=1, source_target_pairs={{0,1},{1,0},{2,3},{3,2},{4,5},{5,4},{6,7},{7,6},{8,9},{9,8},{10,11... | collective-permute-start | bytes 786440 | tf_op jit(solution)/shard_map/ppermute | solution.py:194
  63.3 3.6 %collective-permute-start.2 = (bf16[256,512]{1,0:T(8,128)(2,1)S(1)}, bf16[256,512]{1,0:T(8,128)(2,1)S(1)}, u32[]{:S(2)}, u32[]{:S(2)}) collective-permute-start(bf16[256,512]{1,0:T(8,128)(2,1)S(1)} %collective-permute-done.w00_ref), channel_id=1, source_target_pairs={{0,1},{1,0},{2,3},{3,2},{4,5},{5,4},{6,7},{7,6},{8,9},{9,8},{10,11... | collective-permute-start | bytes 786440 | tf_op jit(solution)/shard_map/ppermute | solution.py:194
  66.8 0.9 copy-start.4
  78.6 44.4 %all-to-all-start.2 = ((bf16[16,8,512]{2,1,0:T(8,128)(2,1)}), bf16[16,8,512]{2,1,0:T(8,128)(2,1)S(1)}, u32[]{:S(2)}, u32[]{:S(2)}) async-start(bf16[16,8,512]{2,1,0:T(8,128)(2,1)} %reduce_sum.21), calls=%async_computation.2 | async-start | bytes 262144 | tf_op jit(solution)/shard_map/all_to_all | solution.py:239
  96.9 13.2 %collective-permute-start.4 = (bf16[128,1536]{1,0:T(8,128)(2,1)S(1)}, bf16[128,1536]{1,0:T(8,128)(2,1)S(1)}, u32[]{:S(2)}, u32[]{:S(2)}) collective-permute-start(bf16[128,1536]{1,0:T(8,128)(2,1)S(1)} %get-tuple-element.19), channel_id=1, source_target_pairs={{0,128},{128,256},{256,384},{384,0},{1,129},{129,257},{257,385},{3... | collective-permute-start | bytes 1179656 | tf_op jit(solution)/shard_map/ppermute | solution.py:234
  98.8 20.6 %collective-permute-start.5 = (bf16[128,1536]{1,0:T(8,128)(2,1)S(1)}, bf16[128,1536]{1,0:T(8,128)(2,1)S(1)}, u32[]{:S(2)}, u32[]{:S(2)}) collective-permute-start(bf16[128,1536]{1,0:T(8,128)(2,1)S(1)} %get-tuple-element.20), channel_id=1, source_target_pairs={{0,256},{128,384},{256,0},{384,128},{1,257},{129,385},{257,1},{385... | collective-permute-start | bytes 1179656 | tf_op jit(solution)/shard_map/ppermute | solution.py:234
  104.9 16.4 %collective-permute-start.6 = (bf16[128,1536]{1,0:T(8,128)(2,1)S(1)}, bf16[128,1536]{1,0:T(8,128)(2,1)S(1)}, u32[]{:S(2)}, u32[]{:S(2)}) collective-permute-start(bf16[128,1536]{1,0:T(8,128)(2,1)S(1)} %get-tuple-element.21), channel_id=1, source_target_pairs={{0,384},{128,0},{256,128},{384,256},{1,385},{129,1},{257,129},{385... | collective-permute-start | bytes 1179656 | tf_op jit(solution)/shard_map/ppermute | solution.py:234

commit v4 on v3

--- a/solution.py
+++ b/solution.py
@@ -86,7 +86,7 @@
     )(tokens, key_cotangent, cosine, sine)
 
 
-def partial_kernel(token_ref, pre_ref, part_ref):
+def partial_kernel(core_ref, token_ref, pre_ref, mine_ref, theirs_ref):
     rows = token_ref.shape[0] * token_ref.shape[1]
     part = lax.dot_general(
         token_ref[...].reshape(rows, token_ref.shape[2]),
@@ -94,32 +94,34 @@
         (((0,), (0,)), ((), ())),
         preferred_element_type=F32,
     )
-    part = part.reshape(-1, ROW, part.shape[1])
-    for zl in range(part_ref.shape[2]):
-        for x in range(X):
-            for zh in range(ZH):
-                for core in range(CORE):
-                    place = ((zl * X + x) * ZH + zh) * CORE + core
-                    part_ref[x, core, zl, zh] = part[place].astype(BF16)
-
-
-def partial_products(got, features):
+    part = part.reshape(-1, CORE, ROW, part.shape[1])
+    first = core_ref[0] == 0
+    for place in range(mine_ref.shape[0]):
+        mine_ref[place] = jnp.where(first, part[place, 0], part[place, 1])
+        theirs_ref[place] = jnp.where(first, part[place, 1], part[place, 0]).astype(BF16)
+
+
+def partial_products(core, got, features):
     count = got.shape[1]
     width = got.shape[2] - features
     steps = 4
+    places = ZL * X * ZH
+    spec = pl.BlockSpec((places // steps, ROW, features), lambda i: (i, 0, 0))
     return pl.pallas_call(
         partial_kernel,
         grid=(steps,),
         in_specs=[
+            SMEM,
             pl.BlockSpec((Y, count, width // steps), lambda i: (0, 0, i)),
             pl.BlockSpec((Y, count, features), lambda i: (0, 0, width // features)),
         ],
-        out_specs=pl.BlockSpec(
-            (X, CORE, ZL // steps, ZH, ROW, features), lambda i: (0, 0, i, 0, 0, 0)
-        ),
-        out_shape=jax.ShapeDtypeStruct((X, CORE, ZL, ZH, ROW, features), BF16),
-        compiler_params=PARAMS,
-    )(got, got)
+        out_specs=[spec, spec],
+        out_shape=[
+            jax.ShapeDtypeStruct((places, ROW, features), F32),
+            jax.ShapeDtypeStruct((places, ROW, features), BF16),
+        ],
+        compiler_params=PARAMS,
+    )(core, got, got)
 
 
 def apply_kernel(place_ref, got_ref, w00_ref, w01_ref, w10_ref, w11_ref, *out_refs):
@@ -194,13 +196,15 @@
     return lax.ppermute(value, axis, [(0, 1), (1, 0)])
 
 
-def turned_round(value, flip):
+def from_column(value, flip):
+    offsets = (0, 2, 1, 3)
     pairs = []
     for y in range(Y):
         for x in range(X):
             for zh in range(ZH):
-                source = (y * X + x) * ZH + zh
-                pairs.append((source, (x * X + y) * ZH + (zh ^ flip)))
+                from_y = (y + offsets[(x - y) % X]) % Y
+                source = (from_y * X + y) * ZH + (zh ^ flip)
+                pairs.append((source, (y * X + x) * ZH + zh))
     return lax.ppermute(value, ("y", "x", "zh"), pairs)
 
 
@@ -215,31 +219,27 @@
     place = jnp.stack([y, zh, core])
 
     shard = dequantize(key_codes, key_exponents)
-    near = turned_round(shard, 0)
-    far = turned_round(shard, 1)
+    near = from_column(shard, 0)
+    far = from_column(shard, 1)
+    weights = (near, swap(near, "core"), far, swap(far, "core"))
 
     device_index = (((y * ZL + zl) * X + x) * ZH + zh) * CORE + core
     positions = (device_index * count + jnp.arange(count, dtype=jnp.int32)) % SEQ
     cosine, sine = tables(positions)
     packed = packed_for_y(tokens, key_cotangent, cosine, sine)
     got = lax.all_to_all(packed, "y", split_axis=0, concat_axis=0, tiled=True)
-    got = after(got, near, far)
-
-    part = partial_products(got, features).reshape(X * CORE, ZL * ZH, ROW, features)
-    parts = lax.all_to_all(part, ("x", "core"), split_axis=0, concat_axis=0, tiled=True)
-
-    weights = (near, swap(near, "core"), far, swap(far, "core"))
-    applied = apply_weights(place, after(got, part), weights)
+    mine, theirs = partial_products(core[None], got, features)
+    other = swap(theirs, "core")
+    applied = apply_weights(place, got, weights)
+    other = after(other, *applied)
+    summed = (mine + other.astype(F32)).astype(BF16)
+    parts = lax.all_to_all(summed, ("zl", "x", "zh"), split_axis=0, concat_axis=0, tiled=True)
+
     moved = [
         lax.ppermute(applied[k], "y", [(i, (i + k) % Y) for i in range(Y)]) for k in range(1, Y)
     ]
-
-    parts = after(parts, *applied)
-    summed = jnp.sum(parts.astype(F32), axis=0).astype(BF16)
-    parts = lax.all_to_all(summed, ("zl", "zh"), split_axis=0, concat_axis=0, tiled=True)
-
-    got = [applied[0], *[after(value, summed) for value in moved]]
-    keys, input_grad = finished(place, cosine, sine, got)
+    moved = [after(value, summed) for value in moved]
+    keys, input_grad = finished(place, cosine, sine, [applied[0], *moved])
     parts = after(parts, keys)
     total_tokens = count * Y * ZL * X * ZH * CORE
     weight_grad = jnp.sum(parts.astype(F32), axis=0) * (1.0 / math.sqrt(total_tokens))

time: 124 us -> 116 us (0.935); the launches traced: 124 us -> 114 us
  starting transfers between devices: 82 us -> 74 us
    all_to_all x2 -> x1, starting transfers between devices: 46.3 us -> 28.8 us  [on_device(): lax.all_to_all(summed, ('zl', 'x', 'zh'), split_axis=0, concat_axis=0, ti...]
    ppermute x2 -> x3, starting transfers between devices: 4.31 us -> 16.8 us  [swap(): return lax.ppermute(value, axis, [(0, 1), (1, 0)])]
    ppermute x2, waiting for transfers between devices: 4.03 us -> 0.01 us  [from_column(): return lax.ppermute(value, ('y', 'x', 'zh'), pairs)]
    ppermute x3, waiting for transfers between devices: 14.3 us -> 17.7 us  [on_device(): lax.ppermute(applied[k], 'y', [(i, (i + k) % Y) for i in range(Y)])]
    ppermute x3, starting transfers between devices: 10.1 us -> 7.2 us  [on_device(): lax.ppermute(applied[k], 'y', [(i, (i + k) % Y) for i in range(Y)])]
    all_to_all x1, waiting for transfers between devices: 0.01 us -> 2.34 us  [on_device(): got = lax.all_to_all(packed, 'y', split_axis=0, concat_axis=0, tiled=True)]
    reduce_sum x1 -> x0, other arithmetic: 2.06 us -> none  [on_device(): summed = jnp.sum(parts.astype(F32), axis=0).astype(BF16)]
    all_to_all x2 -> x1, waiting for transfers between devices: 6.27 us -> 5.35 us  [on_device(): lax.all_to_all(summed, ('zl', 'x', 'zh'), split_axis=0, concat_axis=0, ti...]
  transfers between devices with their start and end apart: 10 -> 10, of which waited for: 6 -> 6; matrix products, arithmetic and copies ran while one was open for 0% -> 0% of each run, Pallas kernels for 4% -> 5%
where the time goes in v4:
time: 116 us; the launch traced here: 114 us
  starting transfers between devices  74 us (64%)
  waiting for transfers between devices  25.7 us (22%)
  Pallas kernels  7.74 us (7%)
  local copies, waits for them, and re-layouts  3.91 us (3%)
  other arithmetic  2.18 us (2%)
    all_to_all x1, starting transfers between devices, on_device(): lax.all_to_all(summed, ('zl', 'x', 'zh'), split_axis=0, concat_axis=0, ti...  28.8 us
    ppermute x3, waiting for transfers between devices, on_device(): lax.ppermute(applied[k], 'y', [(i, (i + k) % Y) for i in range(Y)])  17.7 us
    ppermute x3, starting transfers between devices, swap(): return lax.ppermute(value, axis, [(0, 1), (1, 0)])  16.8 us
    ppermute x2, starting transfers between devices, from_column(): return lax.ppermute(value, ('y', 'x', 'zh'), pairs)  16.1 us
    ppermute x3, starting transfers between devices, on_device(): lax.ppermute(applied[k], 'y', [(i, (i + k) % Y) for i in range(Y)])  7.2 us
    all_to_all x1, waiting for transfers between devices, on_device(): lax.all_to_all(summed, ('zl', 'x', 'zh'), split_axis=0, concat_axis=0, ti...  5.35 us
    all_to_all x1, starting transfers between devices, on_device(): got = lax.all_to_all(packed, 'y', split_axis=0, concat_axis=0, tiled=True)  5.14 us
    unnamed x13, local copies, waits for them, and re-layouts  3.91 us
  transfers between devices with their start and end apart: 10, of which 6 were waited for; matrix products, arithmetic and copies ran while one was open for 0% of the time, Pallas kernels for 5%

profile of v4, /device:TPU:1, one launch (start us, length us, event | category | flops | bytes accessed | tf_op | source)
XLA Modules:
  0.0 114.4 jit_solution(9818139174039853412)
XLA Ops:
  0.7 0.3 fusion
  1.0 0.1 pad_maximum_fusion
  1.1 0.0 copy-start
  1.1 1.2 %copy-done = bf16[128,4096]{1,0:T(8,128)(2,1)S(1)} copy-done((bf16[128,4096]{1,0:T(8,128)(2,1)S(1)}, bf16[128,4096]{1,0:T(8,128)(2,1)}, u32[]{:S(2)}) %copy-start) | copy-done | bytes 1048600
  2.3 0.0 copy-start.2
  2.3 0.9 copy-done.2
  3.2 1.9 %shard_map.67 = bf16[4,128,1536]{2,1,0:T(8,128)(2,1)} custom-call(bf16[128,4096]{1,0:T(8,128)(2,1)S(1)} %copy-done, bf16[128,512]{1,0:T(8,128)(2,1)S(1)} %copy-done.2, f32[128,128]{1,0:T(8,128)S(1)} %get-tuple-element.32.cos_ref, f32[128,128]{1,0:T(8,128)S(1)} %get-tuple-element.33.sin_ref), custom_call_target="tpu_custom_call" | custom-call | tf_op jit(solution)/shard_map/pallas_call | solution.py:73
  5.1 0.0 copy-start.5
  5.1 0.0 copy-start.1
  5.2 5.1 %all-to-all-start = ((bf16[4,128,1536]{2,1,0:T(8,128)(2,1)}), bf16[4,128,1536]{2,1,0:T(8,128)(2,1)S(1)}, u32[]{:S(2)}, u32[]{:S(2)}) async-start(bf16[4,128,1536]{2,1,0:T(8,128)(2,1)} %shard_map.67), calls=%async_computation | async-start | bytes 3145728 | tf_op jit(solution)/shard_map/all_to_all | solution.py:230
  10.3 0.0 copy-done.5
  10.3 0.1 copy.7.exponent_ref
  10.4 0.0 copy-done.1
  10.4 0.1 shard_map.68
  10.6 0.7 collective-permute-start
  11.3 15.4 %collective-permute-start.2 = (bf16[256,512]{1,0:T(8,128)(2,1)S(1)}, bf16[256,512]{1,0:T(8,128)(2,1)S(1)}, u32[]{:S(2)}, u32[]{:S(2)}) collective-permute-start(bf16[256,512]{1,0:T(8,128)(2,1)S(1)} %shard_map.68), channel_id=1, source_target_pairs={{2,0},{0,2},{258,4},{256,6},{130,8},{128,10},{386,12},{384,14},{6,... | collective-permute-start | bytes 786440 | tf_op jit(solution)/shard_map/ppermute | solution.py:208
  26.7 2.3 %all-to-all-done.got_ref.token_ref.pre_ref = bf16[4,128,1536]{2,1,0:T(8,128)(2,1)S(1)} async-done(((bf16[4,128,1536]{2,1,0:T(8,128)(2,1)}), bf16[4,128,1536]{2,1,0:T(8,128)(2,1)S(1)}, u32[]{:S(2)}, u32[]{:S(2)}) %all-to-all-start) | async-done | bytes 1572896 | tf_op jit(solution)/shard_map/all_to_all | solution.py:230
  29.1 1.5 %shard_map.70 = (f32[64,8,512]{2,1,0:T(8,128)S(1)}, bf16[64,8,512]{2,1,0:T(8,128)(2,1)S(1)}) custom-call(s32[1]{0:T(128)} %bitcast.2.core_ref, bf16[4,128,1536]{2,1,0:T(8,128)(2,1)S(1)} %all-to-all-done.got_ref.token_ref.pre_ref, bf16[4,128,1536]{2,1,0:T(8,128)(2,1)S(1)} %all-to-all-done.got_ref.token_ref.pre_ref), custom_call_target="tpu_custom_call" | custom-call | tf_op jit(solution)/shard_map/pallas_call | solution.py:110
  30.6 12.4 %collective-permute-start.5 = (bf16[64,8,512]{2,1,0:T(8,128)(2,1)S(1)}, bf16[64,8,512]{2,1,0:T(8,128)(2,1)S(1)}, u32[]{:S(2)}, u32[]{:S(2)}) collective-permute-start(bf16[64,8,512]{2,1,0:T(8,128)(2,1)S(1)} %get-tuple-element.19), channel_id=1, source_target_pairs={{0,1},{1,0},{2,3},{3,2},{4,5},{5,4},{6,7},{7,6},{8,9},{9,8},{10,11... | collective-permute-start | bytes 1572872 | tf_op jit(solution)/shard_map/ppermute | solution.py:196
  43.0 0.0 collective-permute-done.w00_ref
  43.0 1.9 %collective-permute-start.1 = (bf16[256,512]{1,0:T(8,128)(2,1)S(1)}, bf16[256,512]{1,0:T(8,128)(2,1)S(1)}, u32[]{:S(2)}, u32[]{:S(2)}) collective-permute-start(bf16[256,512]{1,0:T(8,128)(2,1)S(1)} %collective-permute-done.w00_ref), channel_id=1, source_target_pairs={{0,1},{1,0},{2,3},{3,2},{4,5},{5,4},{6,7},{7,6},{8,9},{9,8},{10,11... | collective-permute-start | bytes 786440 | tf_op jit(solution)/shard_map/ppermute | solution.py:196
  45.0 0.0 collective-permute-done.2.w10_ref
  45.0 2.4 %collective-permute-start.3 = (bf16[256,512]{1,0:T(8,128)(2,1)S(1)}, bf16[256,512]{1,0:T(8,128)(2,1)S(1)}, u32[]{:S(2)}, u32[]{:S(2)}) collective-permute-start(bf16[256,512]{1,0:T(8,128)(2,1)S(1)} %collective-permute-done.2.w10_ref), channel_id=1, source_target_pairs={{0,1},{1,0},{2,3},{3,2},{4,5},{5,4},{6,7},{7,6},{8,9},{9,8},{10,11... | collective-permute-start | bytes 786440 | tf_op jit(solution)/shard_map/ppermute | solution.py:196
  47.4 0.0 copy-start.3
  47.4 0.7 copy-done.3
  48.1 0.1 pad_add_fusion.place_ref
  48.2 0.0 collective-permute-done.1.w01_ref
  48.2 0.4 collective-permute-done.3.w11_ref
  48.5 0.0 copy-start.4
  48.5 0.9 copy-done.4
  49.5 2.5 %shard_map.69 = (bf16[128,1536]{1,0:T(8,128)(2,1)S(1)}, bf16[128,1536]{1,0:T(8,128)(2,1)S(1)}, bf16[128,1536]{1,0:T(8,128)(2,1)S(1)}, bf16[128,1536]{1,0:T(8,128)(2,1)S(1)}) custom-call(s32[3]{0:T(128)S(1)} %pad_add_fusion.place_ref, bf16[4,128,1536]{2,1,0:T(8,128)(2,1)S(1)} %all-to-all-done.got_ref.token_ref.pre_ref, ...), custom_call_target="tpu_custom_call" | custom-call | flops 1610612736 | bytes 6291456 | tf_op jit(solution)/shard_map/pallas_call | solution.py:151
  52.0 0.0 collective-permute-done.5
  52.0 1.0 add_convert_fusion
  53.0 28.8 %all-to-all-start.1 = ((bf16[64,8,512]{2,1,0:T(8,128)(2,1)}), bf16[64,8,512]{2,1,0:T(8,128)(2,1)S(1)}, u32[]{:S(2)}, u32[]{:S(2)}) async-start(bf16[64,8,512]{2,1,0:T(8,128)(2,1)} %add_convert_fusion), calls=%async_computation.1 | async-start | bytes 1048576 | tf_op jit(solution)/shard_map/all_to_all | solution.py:236
  81.7 2.0 %collective-permute-start.7 = (bf16[128,1536]{1,0:T(8,128)(2,1)S(1)}, bf16[128,1536]{1,0:T(8,128)(2,1)S(1)}, u32[]{:S(2)}, u32[]{:S(2)}) collective-permute-start(bf16[128,1536]{1,0:T(8,128)(2,1)S(1)} %get-tuple-element.21), channel_id=1, source_target_pairs={{0,384},{128,0},{256,128},{384,256},{1,385},{129,1},{257,129},{385... | collective-permute-start | bytes 1179656 | tf_op jit(solution)/shard_map/ppermute | solution.py:239
  83.7 2.1 %collective-permute-start.6 = (bf16[128,1536]{1,0:T(8,128)(2,1)S(1)}, bf16[128,1536]{1,0:T(8,128)(2,1)S(1)}, u32[]{:S(2)}, u32[]{:S(2)}) collective-permute-start(bf16[128,1536]{1,0:T(8,128)(2,1)S(1)} %get-tuple-element.20), channel_id=1, source_target_pairs={{0,256},{128,384},{256,0},{384,128},{1,257},{129,385},{257,1},{385... | collective-permute-start | bytes 1179656 | tf_op jit(solution)/shard_map/ppermute | solution.py:239
  85.9 3.0 %collective-permute-start.4 = (bf16[128,1536]{1,0:T(8,128)(2,1)S(1)}, bf16[128,1536]{1,0:T(8,128)(2,1)S(1)}, u32[]{:S(2)}, u32[]{:S(2)}) collective-permute-start(bf16[128,1536]{1,0:T(8,128)(2,1)S(1)} %get-tuple-element.17), channel_id=1, source_target_pairs={{0,128},{128,256},{256,384},{384,0},{1,129},{129,257},{257,385},{3... | collective-permute-start | bytes 1179656 | tf_op jit(solution)/shard_map/ppermute | solution.py:239
  88.9 4.7 %collective-permute-done.7.refs_3_ = bf16[128,1536]{1,0:T(8,128)(2,1)S(1)} collective-permute-done((bf16[128,1536]{1,0:T(8,128)(2,1)S(1)}, bf16[128,1536]{1,0:T(8,128)(2,1)S(1)}, u32[]{:S(2)}, u32[]{:S(2)}) %collective-permute-start.7) | collective-permute-done | bytes 393248 | tf_op jit(solution)/shard_map/ppermute | solution.py:239
  93.6 3.2 %collective-permute-done.6.refs_2_ = bf16[128,1536]{1,0:T(8,128)(2,1)S(1)} collective-permute-done((bf16[128,1536]{1,0:T(8,128)(2,1)S(1)}, bf16[128,1536]{1,0:T(8,128)(2,1)S(1)}, u32[]{:S(2)}, u32[]{:S(2)}) %collective-permute-start.6) | collective-permute-done | bytes 393248 | tf_op jit(solution)/shard_map/ppermute | solution.py:239
  96.9 9.7 %collective-permute-done.4.refs_1_ = bf16[128,1536]{1,0:T(8,128)(2,1)S(1)} collective-permute-done((bf16[128,1536]{1,0:T(8,128)(2,1)S(1)}, bf16[128,1536]{1,0:T(8,128)(2,1)S(1)}, u32[]{:S(2)}, u32[]{:S(2)}) %collective-permute-start.4) | collective-permute-done | bytes 393248 | tf_op jit(solution)/shard_map/ppermute | solution.py:239
  106.6 1.7 %shard_map.71 = (bf16[128,512]{1,0:T(8,128)(2,1)}, bf16[128,4096]{1,0:T(8,128)(2,1)}) custom-call(s32[3]{0:T(128)S(1)} %pad_add_fusion.place_ref, f32[128,128]{1,0:T(8,128)S(1)} %get-tuple-element.32.cos_ref, f32[128,128]{1,0:T(8,128)S(1)} %get-tuple-element.33.sin_ref, bf16[128,1536]{1,0:T(8,128)(2,1)S(1)} %get-tuple-element.16.refs_0_, ...), custom_call_target="tpu_custom_call" | custom-call | tf_op jit(solution)/shard_map/pallas_call | solution.py:183
  108.3 5.4 %all-to-all-done.1 = bf16[64,8,512]{2,1,0:T(8,128)(2,1)S(1)} async-done(((bf16[64,8,512]{2,1,0:T(8,128)(2,1)}), bf16[64,8,512]{2,1,0:T(8,128)(2,1)S(1)}, u32[]{:S(2)}, u32[]{:S(2)}) %all-to-all-start.1) | async-done | bytes 524320 | tf_op jit(solution)/shard_map/all_to_all | solution.py:236
  113.7 0.1 convert_reduce_fusion
  113.8 0.6 broadcast_multiply_fusion
  (2 shorter events, 0.0 us)
Async XLA Ops:
  1.1 1.2 %copy-start = (bf16[128,4096]{1,0:T(8,128)(2,1)S(1)}, bf16[128,4096]{1,0:T(8,128)(2,1)}, u32[]{:S(2)}) copy-start(bf16[128,4096]{1,0:T(8,128)(2,1)} %token_ref.1) | copy-start | bytes 3145732
  2.3 0.9 copy-start.2
  5.1 5.2 %copy-start.5 = (s32[256,2]{0,1:T(2,128)S(1)}, s32[256,2]{0,1:T(2,128)}, u32[]{:S(2)}) copy-start(s32[256,2]{0,1:T(2,128)} %param.6) | copy-start | bytes 6148
  5.1 5.3 %copy-start.1 = (bf16[256,512]{1,0:T(8,128)(2,1)S(1)}, bf16[256,512]{1,0:T(8,128)(2,1)}, u32[]{:S(2)}) copy-start(bf16[256,512]{1,0:T(8,128)(2,1)} %code_ref.1) | copy-start | bytes 786436
  5.2 23.9 %all-to-all-start = ((bf16[4,128,1536]{2,1,0:T(8,128)(2,1)}), bf16[4,128,1536]{2,1,0:T(8,128)(2,1)S(1)}, u32[]{:S(2)}, u32[]{:S(2)}) async-start(bf16[4,128,1536]{2,1,0:T(8,128)(2,1)} %shard_map.67), calls=%async_computation | async-start | bytes 3145728 | tf_op jit(solution)/shard_map/all_to_all | solution.py:230
  10.6 32.4 %collective-permute-start = (bf16[256,512]{1,0:T(8,128)(2,1)S(1)}, bf16[256,512]{1,0:T(8,128)(2,1)S(1)}, u32[]{:S(2)}, u32[]{:S(2)}) collective-permute-start(bf16[256,512]{1,0:T(8,128)(2,1)S(1)} %shard_map.68), channel_id=1, source_target_pairs={{0,0},{2,2},{256,4},{258,6},{128,8},{130,10},{384,12},{386,14},{4,... | collective-permute-start | bytes 786440 | tf_op jit(solution)/shard_map/ppermute | solution.py:208
  11.3 33.7 %collective-permute-start.2 = (bf16[256,512]{1,0:T(8,128)(2,1)S(1)}, bf16[256,512]{1,0:T(8,128)(2,1)S(1)}, u32[]{:S(2)}, u32[]{:S(2)}) collective-permute-start(bf16[256,512]{1,0:T(8,128)(2,1)S(1)} %shard_map.68), channel_id=1, source_target_pairs={{2,0},{0,2},{258,4},{256,6},{130,8},{128,10},{386,12},{384,14},{6,... | collective-permute-start | bytes 786440 | tf_op jit(solution)/shard_map/ppermute | solution.py:208
  30.6 21.4 %collective-permute-start.5 = (bf16[64,8,512]{2,1,0:T(8,128)(2,1)S(1)}, bf16[64,8,512]{2,1,0:T(8,128)(2,1)S(1)}, u32[]{:S(2)}, u32[]{:S(2)}) collective-permute-start(bf16[64,8,512]{2,1,0:T(8,128)(2,1)S(1)} %get-tuple-element.19), channel_id=1, source_target_pairs={{0,1},{1,0},{2,3},{3,2},{4,5},{5,4},{6,7},{7,6},{8,9},{9,8},{10,11... | collective-permute-start | bytes 1572872 | tf_op jit(solution)/shard_map/ppermute | solution.py:196
  43.0 5.1 %collective-permute-start.1 = (bf16[256,512]{1,0:T(8,128)(2,1)S(1)}, bf16[256,512]{1,0:T(8,128)(2,1)S(1)}, u32[]{:S(2)}, u32[]{:S(2)}) collective-permute-start(bf16[256,512]{1,0:T(8,128)(2,1)S(1)} %collective-permute-done.w00_ref), channel_id=1, source_target_pairs={{0,1},{1,0},{2,3},{3,2},{4,5},{5,4},{6,7},{7,6},{8,9},{9,8},{10,11... | collective-permute-start | bytes 786440 | tf_op jit(solution)/shard_map/ppermute | solution.py:196
  45.0 3.6 %collective-permute-start.3 = (bf16[256,512]{1,0:T(8,128)(2,1)S(1)}, bf16[256,512]{1,0:T(8,128)(2,1)S(1)}, u32[]{:S(2)}, u32[]{:S(2)}) collective-permute-start(bf16[256,512]{1,0:T(8,128)(2,1)S(1)} %collective-permute-done.2.w10_ref), channel_id=1, source_target_pairs={{0,1},{1,0},{2,3},{3,2},{4,5},{5,4},{6,7},{7,6},{8,9},{9,8},{10,11... | collective-permute-start | bytes 786440 | tf_op jit(solution)/shard_map/ppermute | solution.py:196
  47.4 0.7 copy-start.3
  48.5 0.9 copy-start.4
  53.0 60.7 %all-to-all-start.1 = ((bf16[64,8,512]{2,1,0:T(8,128)(2,1)}), bf16[64,8,512]{2,1,0:T(8,128)(2,1)S(1)}, u32[]{:S(2)}, u32[]{:S(2)}) async-start(bf16[64,8,512]{2,1,0:T(8,128)(2,1)} %add_convert_fusion), calls=%async_computation.1 | async-start | bytes 1048576 | tf_op jit(solution)/shard_map/all_to_all | solution.py:236
  81.7 11.9 %collective-permute-start.7 = (bf16[128,1536]{1,0:T(8,128)(2,1)S(1)}, bf16[128,1536]{1,0:T(8,128)(2,1)S(1)}, u32[]{:S(2)}, u32[]{:S(2)}) collective-permute-start(bf16[128,1536]{1,0:T(8,128)(2,1)S(1)} %get-tuple-element.21), channel_id=1, source_target_pairs={{0,384},{128,0},{256,128},{384,256},{1,385},{129,1},{257,129},{385... | collective-permute-start | bytes 1179656 | tf_op jit(solution)/shard_map/ppermute | solution.py:239
  83.7 13.1 %collective-permute-start.6 = (bf16[128,1536]{1,0:T(8,128)(2,1)S(1)}, bf16[128,1536]{1,0:T(8,128)(2,1)S(1)}, u32[]{:S(2)}, u32[]{:S(2)}) collective-permute-start(bf16[128,1536]{1,0:T(8,128)(2,1)S(1)} %get-tuple-element.20), channel_id=1, source_target_pairs={{0,256},{128,384},{256,0},{384,128},{1,257},{129,385},{257,1},{385... | collective-permute-start | bytes 1179656 | tf_op jit(solution)/shard_map/ppermute | solution.py:239
  85.9 20.7 %collective-permute-start.4 = (bf16[128,1536]{1,0:T(8,128)(2,1)S(1)}, bf16[128,1536]{1,0:T(8,128)(2,1)S(1)}, u32[]{:S(2)}, u32[]{:S(2)}) collective-permute-start(bf16[128,1536]{1,0:T(8,128)(2,1)S(1)} %get-tuple-element.17), channel_id=1, source_target_pairs={{0,128},{128,256},{256,384},{384,0},{1,129},{129,257},{257,385},{3... | collective-permute-start | bytes 1179656 | tf_op jit(solution)/shard_map/ppermute | solution.py:239

commit v5 on v4

--- a/solution.py
+++ b/solution.py
@@ -66,21 +66,21 @@
     packed_ref[0, :, width:] = pre_ref[...]
 
 
-def packed_for_y(tokens, key_cotangent, cosine, sine):
+def packed_for_x(tokens, key_cotangent, cosine, sine):
     count, width = tokens.shape
     features = key_cotangent.shape[1]
-    whole = lambda y: (0, 0)
+    whole = lambda x: (0, 0)
     return pl.pallas_call(
         pack_kernel,
-        grid=(Y,),
+        grid=(X,),
         in_specs=[
-            pl.BlockSpec((count, width // Y), lambda y: (0, y)),
+            pl.BlockSpec((count, width // X), lambda x: (0, x)),
             pl.BlockSpec((count, features), whole),
             pl.BlockSpec((count, HEAD), whole),
             pl.BlockSpec((count, HEAD), whole),
         ],
-        out_specs=pl.BlockSpec((1, count, width // Y + features), lambda y: (y, 0, 0)),
-        out_shape=jax.ShapeDtypeStruct((Y, count, width // Y + features), BF16),
+        out_specs=pl.BlockSpec((1, count, width // X + features), lambda x: (x, 0, 0)),
+        out_shape=jax.ShapeDtypeStruct((X, count, width // X + features), BF16),
         scratch_shapes=[pltpu.VMEM((count, features), BF16)],
         compiler_params=PARAMS,
     )(tokens, key_cotangent, cosine, sine)
@@ -96,41 +96,42 @@
     )
     part = part.reshape(-1, CORE, ROW, part.shape[1])
     first = core_ref[0] == 0
-    for place in range(mine_ref.shape[0]):
-        mine_ref[place] = jnp.where(first, part[place, 0], part[place, 1])
-        theirs_ref[place] = jnp.where(first, part[place, 1], part[place, 0]).astype(BF16)
+    for zl in range(mine_ref.shape[1]):
+        for owner in range(X):
+            for zh in range(ZH):
+                place = (zl * X + owner) * ZH + zh
+                one, two = part[place, 0], part[place, 1]
+                mine_ref[owner, zl, zh] = jnp.where(first, one, two)
+                theirs_ref[owner, zl, zh] = jnp.where(first, two, one).astype(BF16)
 
 
 def partial_products(core, got, features):
     count = got.shape[1]
     width = got.shape[2] - features
     steps = 4
-    places = ZL * X * ZH
-    spec = pl.BlockSpec((places // steps, ROW, features), lambda i: (i, 0, 0))
+    shape = (X, ZL, ZH, ROW, features)
+    spec = pl.BlockSpec((X, ZL // steps, ZH, ROW, features), lambda i: (0, i, 0, 0, 0))
     return pl.pallas_call(
         partial_kernel,
         grid=(steps,),
         in_specs=[
             SMEM,
-            pl.BlockSpec((Y, count, width // steps), lambda i: (0, 0, i)),
-            pl.BlockSpec((Y, count, features), lambda i: (0, 0, width // features)),
+            pl.BlockSpec((X, count, width // steps), lambda i: (0, 0, i)),
+            pl.BlockSpec((X, count, features), lambda i: (0, 0, width // features)),
         ],
         out_specs=[spec, spec],
-        out_shape=[
-            jax.ShapeDtypeStruct((places, ROW, features), F32),
-            jax.ShapeDtypeStruct((places, ROW, features), BF16),
-        ],
+        out_shape=[jax.ShapeDtypeStruct(shape, F32), jax.ShapeDtypeStruct(shape, BF16)],
         compiler_params=PARAMS,
     )(core, got, got)
 
 
 def apply_kernel(place_ref, got_ref, w00_ref, w01_ref, w10_ref, w11_ref, *out_refs):
-    y, zh, core = place_ref[0], place_ref[1], place_ref[2]
+    x, zh, core = place_ref[0], place_ref[1], place_ref[2]
     rows, features = w00_ref.shape
     width = ZH * CORE * rows
     held = ((w00_ref, zh, core), (w01_ref, zh, 1 - core), (w10_ref, 1 - zh, core), (w11_ref, 1 - zh, 1 - core))
     for ahead, out_ref in enumerate(out_refs):
-        target = lax.rem(y + ahead, Y)
+        target = lax.rem(x + ahead, X)
         pre = got_ref[target, :, width:]
         total = jnp.zeros(pre.shape, F32)
         for weight_ref, near, side in held:
@@ -151,11 +152,11 @@
     return pl.pallas_call(
         apply_kernel,
         in_specs=[SMEM] + [VMEM] * 5,
-        out_specs=[VMEM] * Y,
-        out_shape=[one] * Y,
+        out_specs=[VMEM] * X,
+        out_shape=[one] * X,
         compiler_params=PARAMS,
         cost_estimate=pl.CostEstimate(
-            flops=2 * 2 * count * Y * got.shape[2] * 512,
+            flops=2 * 2 * count * X * got.shape[2] * 512,
             bytes_accessed=6 * 1024 * 1024,
             transcendentals=0,
         ),
@@ -163,10 +164,10 @@
 
 
 def finish_kernel(place_ref, cos_ref, sin_ref, *refs):
-    got_refs, keys_ref, grad_ref = refs[:Y], refs[Y], refs[Y + 1]
-    width = grad_ref.shape[1] // Y
+    got_refs, keys_ref, grad_ref = refs[:X], refs[X], refs[X + 1]
+    width = grad_ref.shape[1] // X
     for behind, got_ref in enumerate(got_refs):
-        source = lax.rem(place_ref[0] + (Y - behind), Y)
+        source = lax.rem(place_ref[0] + (X - behind), X)
         start = pl.multiple_of(source * width, width)
         grad_ref[:, pl.ds(start, width)] = got_ref[:, :width]
     for head in range(KVH):
@@ -182,30 +183,19 @@
     features = KVH * HEAD
     return pl.pallas_call(
         finish_kernel,
-        in_specs=[SMEM] + [VMEM] * (2 + Y),
+        in_specs=[SMEM] + [VMEM] * (2 + X),
         out_specs=[VMEM, VMEM],
         out_shape=[
             jax.ShapeDtypeStruct((count, features), BF16),
-            jax.ShapeDtypeStruct((count, (width - features) * Y), BF16),
+            jax.ShapeDtypeStruct((count, (width - features) * X), BF16),
         ],
         compiler_params=PARAMS,
+        cost_estimate=pl.CostEstimate(flops=100000000000, bytes_accessed=2 * 1024 * 1024, transcendentals=0),
     )(place, cosine, sine, *got)
 
 
 def swap(value, axis):
     return lax.ppermute(value, axis, [(0, 1), (1, 0)])
-
-
-def from_column(value, flip):
-    offsets = (0, 2, 1, 3)
-    pairs = []
-    for y in range(Y):
-        for x in range(X):
-            for zh in range(ZH):
-                from_y = (y + offsets[(x - y) % X]) % Y
-                source = (from_y * X + y) * ZH + (zh ^ flip)
-                pairs.append((source, (y * X + x) * ZH + zh))
-    return lax.ppermute(value, ("y", "x", "zh"), pairs)
 
 
 def after(value, *others):
@@ -216,33 +206,36 @@
     y, zl, x, zh, core = [lax.axis_index(name) for name in AXES]
     count = tokens.shape[0]
     features = key_cotangent.shape[1]
-    place = jnp.stack([y, zh, core])
+    place = jnp.stack([x, zh, core])
 
     shard = dequantize(key_codes, key_exponents)
-    near = from_column(shard, 0)
-    far = from_column(shard, 1)
-    weights = (near, swap(near, "core"), far, swap(far, "core"))
+    far = swap(shard, "zh")
+    weights = (shard, swap(shard, "core"), far, swap(far, "core"))
 
     device_index = (((y * ZL + zl) * X + x) * ZH + zh) * CORE + core
     positions = (device_index * count + jnp.arange(count, dtype=jnp.int32)) % SEQ
     cosine, sine = tables(positions)
-    packed = packed_for_y(tokens, key_cotangent, cosine, sine)
-    got = lax.all_to_all(packed, "y", split_axis=0, concat_axis=0, tiled=True)
+    packed = packed_for_x(after(tokens, shard), key_cotangent, cosine, sine)
+    got = lax.all_to_all(packed, "x", split_axis=0, concat_axis=0, tiled=True)
+    got = after(got, far, weights[1])
     mine, theirs = partial_products(core[None], got, features)
     other = swap(theirs, "core")
+    summed = (mine + other.astype(F32)).astype(BF16).reshape(X, ZL * ZH, ROW, features)
+    parts = lax.all_to_all(summed, "y", split_axis=0, concat_axis=0, tiled=True)
+    got = after(got, summed)
     applied = apply_weights(place, got, weights)
-    other = after(other, *applied)
-    summed = (mine + other.astype(F32)).astype(BF16)
-    parts = lax.all_to_all(summed, ("zl", "x", "zh"), split_axis=0, concat_axis=0, tiled=True)
-
     moved = [
-        lax.ppermute(applied[k], "y", [(i, (i + k) % Y) for i in range(Y)]) for k in range(1, Y)
+        lax.ppermute(applied[k], "x", [(i, (i + k) % X) for i in range(X)]) for k in range(1, X)
     ]
-    moved = [after(value, summed) for value in moved]
+    parts = after(parts, *applied)
+    summed = jnp.sum(parts.astype(F32), axis=0).astype(BF16)
+    parts = lax.all_to_all(summed, ("zl", "zh"), split_axis=0, concat_axis=0, tiled=True)
     keys, input_grad = finished(place, cosine, sine, [applied[0], *moved])
     parts = after(parts, keys)
     total_tokens = count * Y * ZL * X * ZH * CORE
     weight_grad = jnp.sum(parts.astype(F32), axis=0) * (1.0 / math.sqrt(total_tokens))
+    pairs = [(i * X + j, j * X + i) for i in range(Y) for j in range(X)]
+    weight_grad = lax.ppermute(weight_grad, ("y", "x"), pairs)
     return keys, input_grad, weight_grad
 
 

time: 116 us -> 117 us (level)
  the two profiles are of different devices: /device:TPU:1 before, /device:TPU:16 now
where the time goes in v5:
time: 117 us; the launch traced here: 116 us
  starting transfers between devices  72.5 us (62%)
  waiting for transfers between devices  23.9 us (20%)
  Pallas kernels  7.82 us (7%)
  local copies, waits for them, and re-layouts  7.69 us (7%)
  other arithmetic  3.32 us (3%)
    all_to_all x1, starting transfers between devices, on_device(): lax.all_to_all(summed, ('zl', 'zh'), split_axis=0, concat_axis=0, tiled=T...  27.9 us
    ppermute x4, starting transfers between devices, swap(): return lax.ppermute(value, axis, [(0, 1), (1, 0)])  21.9 us
    all_to_all x1, waiting for transfers between devices, on_device(): lax.all_to_all(summed, ('zl', 'zh'), split_axis=0, concat_axis=0, tiled=T...  11.9 us
    ppermute x3, starting transfers between devices, on_device(): lax.ppermute(applied[k], 'x', [(i, (i + k) % X) for i in range(X)])  11.6 us
    unnamed x20, local copies, waits for them, and re-layouts  7.69 us
    ppermute x1, waiting for transfers between devices, on_device(): weight_grad = lax.ppermute(weight_grad, ('y', 'x'), pairs)  7.61 us
    all_to_all x1, starting transfers between devices, on_device(): parts = lax.all_to_all(summed, 'y', split_axis=0, concat_axis=0, tiled=True)  4.8 us
    ppermute x4, waiting for transfers between devices, swap(): return lax.ppermute(value, axis, [(0, 1), (1, 0)])  4.39 us
  transfers between devices with their start and end apart: 11, of which 3 were waited for; matrix products, arithmetic and copies ran while one was open for 2% of the time, Pallas kernels for 4%

profile of v5, /device:TPU:16, one launch (start us, length us, event | category | flops | bytes accessed | tf_op | source)
XLA Modules:
  0.0 116.2 jit_solution(8644328100325576972)
XLA Ops:
  0.6 0.0 copy-start
  0.7 0.9 copy.8.exponent_ref
  1.6 0.0 copy-start.1
  1.6 0.9 copy-done.1
  2.5 0.1 shard_map.67.w00_ref
  2.7 0.3 fusion
  3.0 0.1 pad_maximum_fusion
  3.1 0.0 copy-done
  3.1 0.0 copy-start.2
  3.1 0.9 copy-done.2
  4.0 1.9 %shard_map.68 = bf16[4,128,1536]{2,1,0:T(8,128)(2,1)} custom-call(bf16[128,4096]{1,0:T(8,128)(2,1)S(1)} %copy-done, bf16[128,512]{1,0:T(8,128)(2,1)S(1)} %copy-done.2, f32[128,128]{1,0:T(8,128)S(1)} %get-tuple-element.32.cos_ref, f32[128,128]{1,0:T(8,128)S(1)} %get-tuple-element.33.sin_ref), custom_call_target="tpu_custom_call" | custom-call | tf_op jit(solution)/shard_map/pallas_call | solution.py:73
  5.9 4.3 %all-to-all-start = ((bf16[4,128,1536]{2,1,0:T(8,128)(2,1)}), bf16[4,128,1536]{2,1,0:T(8,128)(2,1)S(1)}, u32[]{:S(2)}, u32[]{:S(2)}) async-start(bf16[4,128,1536]{2,1,0:T(8,128)(2,1)} %shard_map.68), calls=%async_computation | async-start | bytes 3145728 | tf_op jit(solution)/shard_map/all_to_all | solution.py:219
  10.2 15.7 %collective-permute-start = (bf16[256,512]{1,0:T(8,128)(2,1)S(1)}, bf16[256,512]{1,0:T(8,128)(2,1)S(1)}, u32[]{:S(2)}, u32[]{:S(2)}) collective-permute-start(bf16[256,512]{1,0:T(8,128)(2,1)S(1)} %shard_map.67.w00_ref), channel_id=1, source_target_pairs={{0,2},{2,0},{1,3},{3,1},{4,6},{6,4},{5,7},{7,5},{8,10},{10,8},{9,1... | collective-permute-start | bytes 786440 | tf_op jit(solution)/shard_map/ppermute | solution.py:198
  25.9 1.9 %collective-permute-start.1 = (bf16[256,512]{1,0:T(8,128)(2,1)S(1)}, bf16[256,512]{1,0:T(8,128)(2,1)S(1)}, u32[]{:S(2)}, u32[]{:S(2)}) collective-permute-start(bf16[256,512]{1,0:T(8,128)(2,1)S(1)} %shard_map.67.w00_ref), channel_id=1, source_target_pairs={{0,1},{1,0},{2,3},{3,2},{4,5},{5,4},{6,7},{7,6},{8,9},{9,8},{10,11... | collective-permute-start | bytes 786440 | tf_op jit(solution)/shard_map/ppermute | solution.py:198
  27.9 4.4 %collective-permute-done.w10_ref = bf16[256,512]{1,0:T(8,128)(2,1)S(1)} collective-permute-done((bf16[256,512]{1,0:T(8,128)(2,1)S(1)}, bf16[256,512]{1,0:T(8,128)(2,1)S(1)}, u32[]{:S(2)}, u32[]{:S(2)}) %collective-permute-start) | collective-permute-done | bytes 262176 | tf_op jit(solution)/shard_map/ppermute | solution.py:198
  32.3 0.0 collective-permute-done.1.w01_ref
  32.3 0.0 all-to-all-done.token_ref.pre_ref.got_ref
  32.3 1.6 %shard_map.69 = (f32[4,8,2,8,512]{4,3,2,1,0:T(8,128)S(1)}, bf16[4,8,2,8,512]{4,3,2,1,0:T(8,128)(2,1)S(1)}) custom-call(s32[1]{0:T(128)} %bitcast.2.core_ref, bf16[4,128,1536]{2,1,0:T(8,128)(2,1)S(1)} %all-to-all-done.token_ref.pre_ref.got_ref, bf16[4,128,1536]{2,1,0:T(8,128)(2,1)S(1)} %all-to-all-done.token_ref.pre_ref.got_ref), custom_call_target="tpu_custom_call" | custom-call | tf_op jit(solution)/shard_map/pallas_call | solution.py:114
  33.9 0.0 copy-done.3
  33.9 1.9 %collective-permute-start.2 = (bf16[4,8,2,8,512]{4,3,2,1,0:T(8,128)(2,1)S(1)}, bf16[4,8,2,8,512]{4,3,2,1,0:T(8,128)(2,1)S(1)}, u32[]{:S(2)}, u32[]{:S(2)}) collective-permute-start(bf16[4,8,2,8,512]{4,3,2,1,0:T(8,128)(2,1)S(1)} %get-tuple-element.19), channel_id=1, source_target_pairs={{0,1},{1,0},{2,3},{3,2},{4,5},{5,4},{6,7},{7,6},{8,9},{9,8},{10,11... | collective-permute-start | bytes 1572872 | tf_op jit(solution)/shard_map/ppermute | solution.py:198
  35.8 0.1 pad_add_fusion.place_ref
  35.9 2.4 %collective-permute-start.3 = (bf16[256,512]{1,0:T(8,128)(2,1)S(1)}, bf16[256,512]{1,0:T(8,128)(2,1)S(1)}, u32[]{:S(2)}, u32[]{:S(2)}) collective-permute-start(bf16[256,512]{1,0:T(8,128)(2,1)S(1)} %collective-permute-done.w10_ref), channel_id=1, source_target_pairs={{0,1},{1,0},{2,3},{3,2},{4,5},{5,4},{6,7},{7,6},{8,9},{9,8},{10,11... | collective-permute-start | bytes 786440 | tf_op jit(solution)/shard_map/ppermute | solution.py:198
  38.3 0.0 collective-permute-done.2
  38.3 1.0 add_convert_fusion
  39.3 4.8 %all-to-all-start.1 = ((bf16[4,16,8,512]{3,2,1,0:T(8,128)(2,1)}), bf16[4,16,8,512]{3,2,1,0:T(8,128)(2,1)}, u32[]{:S(2)}, u32[]{:S(2)}) async-start(bf16[4,16,8,512]{3,2,1,0:T(8,128)(2,1)} %bitcast.3), calls=%async_computation.1 | async-start | bytes 1048576 | tf_op jit(solution)/shard_map/all_to_all | solution.py:224
  44.1 0.0 collective-permute-done.3.w11_ref
  44.1 0.7 copy-done.5
  44.8 0.9 copy-done.4
  45.7 0.9 copy-done.6
  46.7 2.5 %shard_map.70 = (bf16[128,1536]{1,0:T(8,128)(2,1)S(1)}, bf16[128,1536]{1,0:T(8,128)(2,1)S(1)}, bf16[128,1536]{1,0:T(8,128)(2,1)S(1)}, bf16[128,1536]{1,0:T(8,128)(2,1)S(1)}) custom-call(s32[3]{0:T(128)S(1)} %pad_add_fusion.place_ref, bf16[4,128,1536]{2,1,0:T(8,128)(2,1)S(1)} %all-to-all-done.token_ref.pre_ref.got_ref, ...), custom_call_target="tpu_custom_call" | custom-call | flops 1610612736 | bytes 6291456 | tf_op jit(solution)/shard_map/pallas_call | solution.py:152
  49.2 0.0 copy-start.7
  49.2 0.8 copy-done.7
  50.0 3.6 %collective-permute-start.4 = (bf16[128,1536]{1,0:T(8,128)(2,1)S(1)}, bf16[128,1536]{1,0:T(8,128)(2,1)S(1)}, u32[]{:S(2)}, u32[]{:S(2)}) collective-permute-start(bf16[128,1536]{1,0:T(8,128)(2,1)S(1)} %get-tuple-element.22), channel_id=1, source_target_pairs={{0,4},{4,8},{8,12},{12,0},{1,5},{5,9},{9,13},{13,1},{2,6},{6,10},{... | collective-permute-start | bytes 1179656 | tf_op jit(solution)/shard_map/ppermute | solution.py:228
  53.6 4.6 %collective-permute-start.5 = (bf16[128,1536]{1,0:T(8,128)(2,1)S(1)}, bf16[128,1536]{1,0:T(8,128)(2,1)S(1)}, u32[]{:S(2)}, u32[]{:S(2)}) collective-permute-start(bf16[128,1536]{1,0:T(8,128)(2,1)S(1)} %get-tuple-element.23), channel_id=1, source_target_pairs={{0,8},{4,12},{8,0},{12,4},{1,9},{5,13},{9,1},{13,5},{2,10},{6,14},... | collective-permute-start | bytes 1179656 | tf_op jit(solution)/shard_map/ppermute | solution.py:228
  58.2 3.4 %collective-permute-start.6 = (bf16[128,1536]{1,0:T(8,128)(2,1)S(1)}, bf16[128,1536]{1,0:T(8,128)(2,1)S(1)}, u32[]{:S(2)}, u32[]{:S(2)}) collective-permute-start(bf16[128,1536]{1,0:T(8,128)(2,1)S(1)} %get-tuple-element.24), channel_id=1, source_target_pairs={{0,12},{4,0},{8,4},{12,8},{1,13},{5,1},{9,5},{13,9},{2,14},{6,2},{... | collective-permute-start | bytes 1179656 | tf_op jit(solution)/shard_map/ppermute | solution.py:228
  61.6 0.0 all-to-all-done.1
  61.6 1.8 %reduce_sum.21 = bf16[16,8,512]{2,1,0:T(8,128)(2,1)} reduce(bf16[4,16,8,512]{3,2,1,0:T(8,128)(2,1)} %all-to-all-done.1, bf16[]{:T(256)} %constant.53.clone.1), dimensions={0}, to_apply=%region_0.1 | reduce | flops 196608 | bytes 655362 | tf_op jit(solution)/shard_map/reduce_sum | solution.py:231
  63.4 27.9 %all-to-all-start.2 = ((bf16[16,8,512]{2,1,0:T(8,128)(2,1)}), bf16[16,8,512]{2,1,0:T(8,128)(2,1)S(1)}, u32[]{:S(2)}, u32[]{:S(2)}) async-start(bf16[16,8,512]{2,1,0:T(8,128)(2,1)} %reduce_sum.21), calls=%async_computation.2 | async-start | bytes 262144 | tf_op jit(solution)/shard_map/all_to_all | solution.py:232
  91.3 0.0 collective-permute-done.4.refs_1_
  91.3 0.0 collective-permute-done.5.refs_2_
  91.4 0.0 collective-permute-done.6.refs_3_
  91.4 0.0 copy-start.8
  91.4 1.0 copy-done.8
  92.4 1.7 %shard_map.71 = (bf16[128,512]{1,0:T(8,128)(2,1)}, bf16[128,4096]{1,0:T(8,128)(2,1)}) custom-call(s32[3]{0:T(128)S(1)} %pad_add_fusion.place_ref, f32[128,128]{1,0:T(8,128)S(1)} %get-tuple-element.32.cos_ref, f32[128,128]{1,0:T(8,128)S(1)} %get-tuple-element.33.sin_ref, bf16[128,1536]{1,0:T(8,128)(2,1)S(1)} %copy-done.8, ...), custom_call_target="tpu_custom_call" | custom-call | flops 99999997952 | bytes 2097152 | tf_op jit(solution)/shard_map/pallas_call | solution.py:184
  94.0 11.9 %all-to-all-done.2 = bf16[16,8,512]{2,1,0:T(8,128)(2,1)S(1)} async-done(((bf16[16,8,512]{2,1,0:T(8,128)(2,1)}), bf16[16,8,512]{2,1,0:T(8,128)(2,1)S(1)}, u32[]{:S(2)}, u32[]{:S(2)}) %all-to-all-start.2) | async-done | bytes 131104 | tf_op jit(solution)/shard_map/all_to_all | solution.py:232
  106.0 1.9 %collective-permute-start.7 = (f32[8,512]{1,0:T(8,128)S(1)}, f32[8,512]{1,0:T(8,128)S(1)}, u32[]{:S(2)}, u32[]{:S(2)}) collective-permute-start(f32[8,512]{1,0:T(8,128)S(1)} %broadcast_multiply_fusion), channel_id=1, source_target_pairs={{0,0},{4,128},{8,256},{12,384},{128,4},{132,132},{136,260},{140,38... | collective-permute-start | bytes 49160 | tf_op jit(solution)/shard_map/ppermute | solution.py:238
  107.9 7.6 %collective-permute-done.7 = f32[8,512]{1,0:T(8,128)S(1)} collective-permute-done((f32[8,512]{1,0:T(8,128)S(1)}, f32[8,512]{1,0:T(8,128)S(1)}, u32[]{:S(2)}, u32[]{:S(2)}) %collective-permute-start.7) | collective-permute-done | bytes 16416 | tf_op jit(solution)/shard_map/ppermute | solution.py:238
  115.5 0.6 copy.10
  (8 shorter events, 0.1 us)
Async XLA Ops:
  0.6 2.5 %copy-start = (bf16[128,4096]{1,0:T(8,128)(2,1)S(1)}, bf16[128,4096]{1,0:T(8,128)(2,1)}, u32[]{:S(2)}) copy-start(bf16[128,4096]{1,0:T(8,128)(2,1)} %token_ref) | copy-start | bytes 3145732
  1.6 1.0 copy-start.1
  3.1 0.9 copy-start.2
  5.9 26.3 %all-to-all-start = ((bf16[4,128,1536]{2,1,0:T(8,128)(2,1)}), bf16[4,128,1536]{2,1,0:T(8,128)(2,1)S(1)}, u32[]{:S(2)}, u32[]{:S(2)}) async-start(bf16[4,128,1536]{2,1,0:T(8,128)(2,1)} %shard_map.68), calls=%async_computation | async-start | bytes 3145728 | tf_op jit(solution)/shard_map/all_to_all | solution.py:219
  10.2 22.0 %collective-permute-start = (bf16[256,512]{1,0:T(8,128)(2,1)S(1)}, bf16[256,512]{1,0:T(8,128)(2,1)S(1)}, u32[]{:S(2)}, u32[]{:S(2)}) collective-permute-start(bf16[256,512]{1,0:T(8,128)(2,1)S(1)} %shard_map.67.w00_ref), channel_id=1, source_target_pairs={{0,2},{2,0},{1,3},{3,1},{4,6},{6,4},{5,7},{7,5},{8,10},{10,8},{9,1... | collective-permute-start | bytes 786440 | tf_op jit(solution)/shard_map/ppermute | solution.py:198
  25.9 6.3 %collective-permute-start.1 = (bf16[256,512]{1,0:T(8,128)(2,1)S(1)}, bf16[256,512]{1,0:T(8,128)(2,1)S(1)}, u32[]{:S(2)}, u32[]{:S(2)}) collective-permute-start(bf16[256,512]{1,0:T(8,128)(2,1)S(1)} %shard_map.67.w00_ref), channel_id=1, source_target_pairs={{0,1},{1,0},{2,3},{3,2},{4,5},{5,4},{6,7},{7,6},{8,9},{9,8},{10,11... | collective-permute-start | bytes 786440 | tf_op jit(solution)/shard_map/ppermute | solution.py:198
  32.3 1.6 %copy-start.3 = (bf16[256,512]{1,0:T(8,128)(2,1)}, bf16[256,512]{1,0:T(8,128)(2,1)S(1)}, u32[]{:S(2)}) copy-start(bf16[256,512]{1,0:T(8,128)(2,1)S(1)} %collective-permute-done.1.w01_ref) | copy-start | bytes 786436
  33.9 4.4 %collective-permute-start.2 = (bf16[4,8,2,8,512]{4,3,2,1,0:T(8,128)(2,1)S(1)}, bf16[4,8,2,8,512]{4,3,2,1,0:T(8,128)(2,1)S(1)}, u32[]{:S(2)}, u32[]{:S(2)}) collective-permute-start(bf16[4,8,2,8,512]{4,3,2,1,0:T(8,128)(2,1)S(1)} %get-tuple-element.19), channel_id=1, source_target_pairs={{0,1},{1,0},{2,3},{3,2},{4,5},{5,4},{6,7},{7,6},{8,9},{9,8},{10,11... | collective-permute-start | bytes 1572872 | tf_op jit(solution)/shard_map/ppermute | solution.py:198
  35.9 8.2 %collective-permute-start.3 = (bf16[256,512]{1,0:T(8,128)(2,1)S(1)}, bf16[256,512]{1,0:T(8,128)(2,1)S(1)}, u32[]{:S(2)}, u32[]{:S(2)}) collective-permute-start(bf16[256,512]{1,0:T(8,128)(2,1)S(1)} %collective-permute-done.w10_ref), channel_id=1, source_target_pairs={{0,1},{1,0},{2,3},{3,2},{4,5},{5,4},{6,7},{7,6},{8,9},{9,8},{10,11... | collective-permute-start | bytes 786440 | tf_op jit(solution)/shard_map/ppermute | solution.py:198
  39.3 22.3 %all-to-all-start.1 = ((bf16[4,16,8,512]{3,2,1,0:T(8,128)(2,1)}), bf16[4,16,8,512]{3,2,1,0:T(8,128)(2,1)}, u32[]{:S(2)}, u32[]{:S(2)}) async-start(bf16[4,16,8,512]{3,2,1,0:T(8,128)(2,1)} %bitcast.3), calls=%async_computation.1 | async-start | bytes 1048576 | tf_op jit(solution)/shard_map/all_to_all | solution.py:224
  44.1 0.7 copy-start.5
  44.8 0.9 copy-start.4
  45.7 0.9 copy-start.6
  49.2 0.8 copy-start.7
  50.0 41.4 %collective-permute-start.4 = (bf16[128,1536]{1,0:T(8,128)(2,1)S(1)}, bf16[128,1536]{1,0:T(8,128)(2,1)S(1)}, u32[]{:S(2)}, u32[]{:S(2)}) collective-permute-start(bf16[128,1536]{1,0:T(8,128)(2,1)S(1)} %get-tuple-element.22), channel_id=1, source_target_pairs={{0,4},{4,8},{8,12},{12,0},{1,5},{5,9},{9,13},{13,1},{2,6},{6,10},{... | collective-permute-start | bytes 1179656 | tf_op jit(solution)/shard_map/ppermute | solution.py:228
  53.6 37.7 %collective-permute-start.5 = (bf16[128,1536]{1,0:T(8,128)(2,1)S(1)}, bf16[128,1536]{1,0:T(8,128)(2,1)S(1)}, u32[]{:S(2)}, u32[]{:S(2)}) collective-permute-start(bf16[128,1536]{1,0:T(8,128)(2,1)S(1)} %get-tuple-element.23), channel_id=1, source_target_pairs={{0,8},{4,12},{8,0},{12,4},{1,9},{5,13},{9,1},{13,5},{2,10},{6,14},... | collective-permute-start | bytes 1179656 | tf_op jit(solution)/shard_map/ppermute | solution.py:228
  58.2 33.2 %collective-permute-start.6 = (bf16[128,1536]{1,0:T(8,128)(2,1)S(1)}, bf16[128,1536]{1,0:T(8,128)(2,1)S(1)}, u32[]{:S(2)}, u32[]{:S(2)}) collective-permute-start(bf16[128,1536]{1,0:T(8,128)(2,1)S(1)} %get-tuple-element.24), channel_id=1, source_target_pairs={{0,12},{4,0},{8,4},{12,8},{1,13},{5,1},{9,5},{13,9},{2,14},{6,2},{... | collective-permute-start | bytes 1179656 | tf_op jit(solution)/shard_map/ppermute | solution.py:228
  63.4 42.6 %all-to-all-start.2 = ((bf16[16,8,512]{2,1,0:T(8,128)(2,1)}), bf16[16,8,512]{2,1,0:T(8,128)(2,1)S(1)}, u32[]{:S(2)}, u32[]{:S(2)}) async-start(bf16[16,8,512]{2,1,0:T(8,128)(2,1)} %reduce_sum.21), calls=%async_computation.2 | async-start | bytes 262144 | tf_op jit(solution)/shard_map/all_to_all | solution.py:232
  91.4 1.0 copy-start.8
  106.0 9.5 %collective-permute-start.7 = (f32[8,512]{1,0:T(8,128)S(1)}, f32[8,512]{1,0:T(8,128)S(1)}, u32[]{:S(2)}, u32[]{:S(2)}) collective-permute-start(f32[8,512]{1,0:T(8,128)S(1)} %broadcast_multiply_fusion), channel_id=1, source_target_pairs={{0,0},{4,128},{8,256},{12,384},{128,4},{132,132},{136,260},{140,38... | collective-permute-start | bytes 49160 | tf_op jit(solution)/shard_map/ppermute | solution.py:238

commit v6 on v2

--- a/solution.py
+++ b/solution.py
@@ -1,3 +1,4 @@
+import functools
 import math
 
 import jax
@@ -67,16 +68,16 @@
         for zl in range(ZL):
             for zh in range(ZH):
                 place = (zl * X + x) * ZH + zh
-                mine_ref[x, 0, zl, zh] = part_ref[place, core].astype(BF16)
-                theirs_ref[x, 0, zl, zh] = part_ref[place, 1 - core].astype(BF16)
+                mine_ref[0, x, zl, zh] = part_ref[place, core].astype(BF16)
+                theirs_ref[0, x, zl, zh] = part_ref[place, 1 - core].astype(BF16)
 
 
 def partial_products(core, tokens, key_cotangent, cosine, sine):
     count, width = tokens.shape
     features = key_cotangent.shape[1]
     step = width // Y
-    half = jax.ShapeDtypeStruct((X, Y, ZL, ZH, ROW, features), BF16)
-    half_spec = pl.BlockSpec((X, 1, ZL, ZH, ROW, features), lambda y: (0, y, 0, 0, 0, 0))
+    half = jax.ShapeDtypeStruct((Y, X, ZL, ZH, ROW, features), BF16)
+    half_spec = pl.BlockSpec((1, X, ZL, ZH, ROW, features), lambda y: (y, 0, 0, 0, 0, 0))
     whole = lambda y: (0, 0)
     return pl.pallas_call(
         partial_kernel,
@@ -107,6 +108,7 @@
         join_kernel,
         out_shape=jax.ShapeDtypeStruct((len(blocks) * rows, features), BF16),
         compiler_params=PARAMS,
+        cost_estimate=pl.CostEstimate(flops=100000000000, bytes_accessed=4 * 1024 * 1024, transcendentals=0),
     )(*blocks)
 
 
@@ -172,7 +174,7 @@
             jax.ShapeDtypeStruct((blocks, count, weights.shape[0] // blocks), BF16),
         ],
         compiler_params=PARAMS,
-        cost_estimate=product_cost(tokens, features),
+        cost_estimate=pl.CostEstimate(flops=100000000000, bytes_accessed=4 * 1024 * 1024, transcendentals=0),
     )(place, tokens, pre_grad, weights)
 
 
@@ -200,6 +202,29 @@
     return [shard, *moved]
 
 
+def sum_kernel(factor, *refs):
+    total = refs[0][0].astype(F32)
+    for ref in refs[:-1]:
+        for place in range(ref.shape[0]):
+            if ref is not refs[0] or place:
+                total += ref[place].astype(F32)
+    refs[-1][...] = (total * factor).astype(refs[-1].dtype)
+
+
+def summed_first(*parts, dtype=BF16, factor=1.0, steps=1):
+    shape = parts[0].shape[1:]
+    block = (shape[0] // steps, *shape[1:])
+    rest = (0,) * (len(shape) - 1)
+    return pl.pallas_call(
+        functools.partial(sum_kernel, factor),
+        grid=(steps,),
+        in_specs=[pl.BlockSpec((part.shape[0], *block), lambda i: (0, i, *rest)) for part in parts],
+        out_specs=pl.BlockSpec(block, lambda i: (i, *rest)),
+        out_shape=jax.ShapeDtypeStruct(shape, dtype),
+        compiler_params=PARAMS,
+    )(*parts)
+
+
 def swap(value, axis):
     return lax.ppermute(value, axis, [(0, 1), (1, 0)])
 
@@ -215,28 +240,32 @@
     cosine, sine = tables(positions)
     mine, theirs, pre_grad = partial_products(core[None], after(tokens, shard), key_cotangent, cosine, sine)
 
-    summed = (mine.astype(F32) + swap(theirs, "core").astype(F32)).astype(BF16)
-    summed = summed.reshape(X * Y, ZL * ZH, ROW, features)
-    got = lax.all_to_all(summed, ("x", "y"), split_axis=0, concat_axis=0, tiled=True)
+    flat = (1, Y * X * ZL * ZH, ROW, features)
+    summed = summed_first(mine.reshape(flat), swap(theirs, "core").reshape(flat), steps=8)
+    summed = summed.reshape(Y, X * ZL * ZH, ROW, features)
+    got = lax.all_to_all(summed, "y", split_axis=0, concat_axis=0, tiled=True)
 
     shard = after(shard, theirs)
     far_shard = after(swap(shard, "zh"), summed)
     near = from_x(shard)
     far = from_x(far_shard)
 
+    summed = summed_first(got, steps=4).reshape(X, ZL * ZH, ROW, features)
+    got = lax.all_to_all(summed, "x", split_axis=0, concat_axis=0, tiled=True)
+
     held = joined(near + far)
-    got = after(got, held)
-    summed = jnp.sum(got.astype(F32), axis=0).astype(BF16)
+    swapped = swap(held, "core")
+    summed = after(summed_first(got, steps=2), held)
     got = lax.all_to_all(summed, ("zl", "zh"), split_axis=0, concat_axis=0, tiled=True)
 
     place = jnp.stack([x, zh, core])
     total, half = apply_first(place, tokens, pre_grad, held)
     keys, input_grad = apply_second(
-        place, tokens, pre_grad, cosine, sine, swap(held, "core"), total, half
+        place, tokens, pre_grad, cosine, sine, swapped, total, half
     )
     got = after(got, keys)
     total_tokens = count * Y * ZL * X * ZH * CORE
-    weight_grad = jnp.sum(got.astype(F32), axis=0) * (1.0 / math.sqrt(total_tokens))
+    weight_grad = summed_first(got, dtype=F32, factor=1.0 / math.sqrt(total_tokens))
     return keys, input_grad, weight_grad
 
 

time: 113 us -> 116 us (1.027)
  waiting for transfers between devices: 40.1 us -> 20.5 us
  starting transfers between devices: 52.1 us -> 70.3 us
  Pallas kernels: 8.28 us -> 17.7 us
  other arithmetic: 6.15 us -> 0.51 us
    ppermute x6, waiting for transfers between devices: 32.1 us -> 5.9 us  [from_x(): lax.ppermute(shard, 'x', [(i, (i + k) % X) for i in range(X)])]
    all_to_all x1, starting transfers between devices: 4.84 us -> 23.2 us  [on_device(): lax.all_to_all(summed, ('zl', 'zh'), split_axis=0, concat_axis=0, tiled=T...]
    ppermute x3, waiting for transfers between devices: 0.01 us -> 7.61 us  [swap(): return lax.ppermute(value, axis, [(0, 1), (1, 0)])]
    pallas_call x0 -> x4, Pallas kernels: none -> 6.21 us  [summed_first(): pl.pallas_call(functools.partial(sum_kernel, factor), grid=(steps,), in_s...]
    all_to_all x1 -> x2, starting transfers between devices: 4.62 us -> 8.44 us  [the longest x1 4.83 us: on_device(): got = lax.all_to_all(summed, 'x', split_axis=0, concat_axis=0, tiled=True)]
    ppermute x6, starting transfers between devices: 20 us -> 16.5 us  [from_x(): lax.ppermute(shard, 'x', [(i, (i + k) % X) for i in range(X)])]
    reduce_sum x2 -> x0, other arithmetic: 2.6 us -> none  [the longest x1 2.58 us: on_device(): summed = jnp.sum(got.astype(F32), axis=0).astype(BF16)]
    pallas_call x1, Pallas kernels: 0.14 us -> 2.57 us  [joined(): pl.pallas_call(join_kernel, out_shape=jax.ShapeDtypeStruct((len(blocks) *...]
  transfers between devices with their start and end apart: 11 -> 12, of which waited for: 5 -> 4; matrix products, arithmetic and copies ran while one was open for 5% -> 0% of each run, Pallas kernels for 5% -> 10%
where the time goes in v6:
time: 116 us; the launch traced here: 114 us
  starting transfers between devices  70.3 us (61%)
  waiting for transfers between devices  20.5 us (18%)
  Pallas kernels  17.7 us (15%)
  local copies, waits for them, and re-layouts  3.95 us (3%)
    all_to_all x1, starting transfers between devices, on_device(): lax.all_to_all(summed, ('zl', 'zh'), split_axis=0, concat_axis=0, tiled=T...  23.2 us
    ppermute x3, starting transfers between devices, swap(): return lax.ppermute(value, axis, [(0, 1), (1, 0)])  22.1 us
    ppermute x6, starting transfers between devices, from_x(): lax.ppermute(shard, 'x', [(i, (i + k) % X) for i in range(X)])  16.5 us
    ppermute x3, waiting for transfers between devices, swap(): return lax.ppermute(value, axis, [(0, 1), (1, 0)])  7.61 us
    all_to_all x1, waiting for transfers between devices, on_device(): lax.all_to_all(summed, ('zl', 'zh'), split_axis=0, concat_axis=0, tiled=T...  7.03 us
    pallas_call x4, Pallas kernels, summed_first(): pl.pallas_call(functools.partial(sum_kernel, factor), grid=(steps,), in_s...  6.21 us
    ppermute x6, waiting for transfers between devices, from_x(): lax.ppermute(shard, 'x', [(i, (i + k) % X) for i in range(X)])  5.9 us
    all_to_all x1, starting transfers between devices, on_device(): got = lax.all_to_all(summed, 'x', split_axis=0, concat_axis=0, tiled=True)  4.83 us
  transfers between devices with their start and end apart: 12, of which 4 were waited for; matrix products, arithmetic and copies ran while one was open for 0% of the time, Pallas kernels for 10%

profile of v6, /device:TPU:1, one launch (start us, length us, event | category | flops | bytes accessed | tf_op | source)
XLA Modules:
  0.0 113.9 jit_solution(18373839187806330737)
XLA Ops:
  0.7 0.8 copy.7.exponent_ref
  1.5 0.0 copy-start.6
  1.5 0.9 copy-done.6
  2.5 0.1 shard_map.67.refs_0_
  2.6 0.3 fusion
  2.9 0.1 pad_maximum_fusion
  3.0 0.0 copy-start.2
  3.0 0.0 copy-start.4
  3.1 0.0 copy-start
  3.1 1.3 %copy-done = bf16[128,4096]{1,0:T(8,128)(2,1)S(1)} copy-done((bf16[128,4096]{1,0:T(8,128)(2,1)S(1)}, bf16[128,4096]{1,0:T(8,128)(2,1)}, u32[]{:S(2)}) %copy-start) | copy-done | bytes 1048600
  4.3 0.9 copy-done.7
  5.2 2.5 %shard_map.68 = (bf16[4,4,8,2,8,512]{5,4,3,2,1,0:T(8,128)(2,1)S(1)}, bf16[4,4,8,2,8,512]{5,4,3,2,1,0:T(8,128)(2,1)S(1)}, bf16[128,512]{1,0:T(8,128)(2,1)S(1)}) custom-call(s32[1]{0:T(128)} %bitcast.2.core_ref, bf16[128,4096]{1,0:T(8,128)(2,1)S(1)} %copy-done, bf16[128,512]{1,0:T(8,128)(2,1)S(1)} %copy-done.7, f32[128,128]{1,0:T(8,128)S(1)} %get-tuple-element.30.cos_ref, ...), custom_call_target="tpu_custom_call" | custom-call | tf_op jit(solution)/shard_map/pallas_call | solution.py:82
  7.7 0.0 copy-done.2
  7.7 8.8 %collective-permute-start.4 = (bf16[4,4,8,2,8,512]{5,4,3,2,1,0:T(8,128)(2,1)S(1)}, bf16[4,4,8,2,8,512]{5,4,3,2,1,0:T(8,128)(2,1)S(1)}, u32[]{:S(2)}, u32[]{:S(2)}) collective-permute-start(bf16[4,4,8,2,8,512]{5,4,3,2,1,0:T(8,128)(2,1)S(1)} %get-tuple-element.17), channel_id=1, source_target_pairs={{0,1},{1,0},{2,3},{3,2},{4,5},{5,4},{6,7},{7,6},{8,9},{9,8},{10,11... | collective-permute-start | bytes 6291464 | tf_op jit(solution)/shard_map/ppermute | solution.py:229
  16.5 3.8 %collective-permute-done.4 = bf16[4,4,8,2,8,512]{5,4,3,2,1,0:T(8,128)(2,1)S(1)} collective-permute-done((bf16[4,4,8,2,8,512]{5,4,3,2,1,0:T(8,128)(2,1)S(1)}, bf16[4,4,8,2,8,512]{5,4,3,2,1,0:T(8,128)(2,1)S(1)}, u32[]{:S(2)}, u32[]{:S(2)}) %collective-permute-start.4) | collective-permute-done | bytes 2097184 | tf_op jit(solution)/shard_map/ppermute | solution.py:229
  20.3 0.0 copy-done.4
  20.3 3.2 %shard_map.69 = bf16[256,8,512]{2,1,0:T(8,128)(2,1)} custom-call(bf16[1,256,8,512]{3,2,1,0:T(8,128)(2,1)S(1)} %bitcast.7, bf16[1,256,8,512]{3,2,1,0:T(8,128)(2,1)S(1)} %bitcast.8), custom_call_target="tpu_custom_call" | custom-call | tf_op jit(solution)/shard_map/pallas_call | solution.py:218
  23.5 3.6 %all-to-all-start = ((bf16[4,64,8,512]{3,2,1,0:T(8,128)(2,1)}), bf16[4,64,8,512]{3,2,1,0:T(8,128)(2,1)S(1)}, u32[]{:S(2)}, u32[]{:S(2)}) async-start(bf16[4,64,8,512]{3,2,1,0:T(8,128)(2,1)} %bitcast.5), calls=%async_computation | async-start | bytes 4194304 | tf_op jit(solution)/shard_map/all_to_all | solution.py:246
  27.1 10.6 %collective-permute-start.3 = (bf16[256,512]{1,0:T(8,128)(2,1)S(1)}, bf16[256,512]{1,0:T(8,128)(2,1)S(1)}, u32[]{:S(2)}, u32[]{:S(2)}) collective-permute-start(bf16[256,512]{1,0:T(8,128)(2,1)S(1)} %shard_map.67.refs_0_), channel_id=1, source_target_pairs={{0,2},{2,0},{1,3},{3,1},{4,6},{6,4},{5,7},{7,5},{8,10},{10,8},{9,1... | collective-permute-start | bytes 786440 | tf_op jit(solution)/shard_map/ppermute | solution.py:229
  37.7 4.4 %collective-permute-start.2 = (bf16[256,512]{1,0:T(8,128)(2,1)S(1)}, bf16[256,512]{1,0:T(8,128)(2,1)S(1)}, u32[]{:S(2)}, u32[]{:S(2)}) collective-permute-start(bf16[256,512]{1,0:T(8,128)(2,1)S(1)} %shard_map.67.refs_0_), channel_id=1, source_target_pairs={{0,12},{4,0},{8,4},{12,8},{1,13},{5,1},{9,5},{13,9},{2,14},{6,2},{... | collective-permute-start | bytes 786440 | tf_op jit(solution)/shard_map/ppermute | solution.py:201
  42.1 2.4 %collective-permute-start.1 = (bf16[256,512]{1,0:T(8,128)(2,1)S(1)}, bf16[256,512]{1,0:T(8,128)(2,1)S(1)}, u32[]{:S(2)}, u32[]{:S(2)}) collective-permute-start(bf16[256,512]{1,0:T(8,128)(2,1)S(1)} %shard_map.67.refs_0_), channel_id=1, source_target_pairs={{0,8},{4,12},{8,0},{12,4},{1,9},{5,13},{9,1},{13,5},{2,10},{6,14},... | collective-permute-start | bytes 786440 | tf_op jit(solution)/shard_map/ppermute | solution.py:201
  44.5 2.5 %collective-permute-start = (bf16[256,512]{1,0:T(8,128)(2,1)S(1)}, bf16[256,512]{1,0:T(8,128)(2,1)S(1)}, u32[]{:S(2)}, u32[]{:S(2)}) collective-permute-start(bf16[256,512]{1,0:T(8,128)(2,1)S(1)} %shard_map.67.refs_0_), channel_id=1, source_target_pairs={{0,4},{4,8},{8,12},{12,0},{1,5},{5,9},{9,13},{13,1},{2,6},{6,10},{... | collective-permute-start | bytes 786440 | tf_op jit(solution)/shard_map/ppermute | solution.py:201
  47.1 3.8 %collective-permute-done.3.refs_4_ = bf16[256,512]{1,0:T(8,128)(2,1)S(1)} collective-permute-done((bf16[256,512]{1,0:T(8,128)(2,1)S(1)}, bf16[256,512]{1,0:T(8,128)(2,1)S(1)}, u32[]{:S(2)}, u32[]{:S(2)}) %collective-permute-start.3) | collective-permute-done | bytes 262176 | tf_op jit(solution)/shard_map/ppermute | solution.py:229
  50.9 1.9 %collective-permute-start.7 = (bf16[256,512]{1,0:T(8,128)(2,1)S(1)}, bf16[256,512]{1,0:T(8,128)(2,1)}, u32[]{:S(2)}, u32[]{:S(2)}) collective-permute-start(bf16[256,512]{1,0:T(8,128)(2,1)S(1)} %collective-permute-done.3.refs_4_), channel_id=1, source_target_pairs={{0,12},{4,0},{8,4},{12,8},{1,13},{5,1},{9,5},{13,9},{2,14},{6,2},{... | collective-permute-start | bytes 786440 | tf_op jit(solution)/shard_map/ppermute | solution.py:201
  52.8 1.9 %collective-permute-start.6 = (bf16[256,512]{1,0:T(8,128)(2,1)S(1)}, bf16[256,512]{1,0:T(8,128)(2,1)}, u32[]{:S(2)}, u32[]{:S(2)}) collective-permute-start(bf16[256,512]{1,0:T(8,128)(2,1)S(1)} %collective-permute-done.3.refs_4_), channel_id=1, source_target_pairs={{0,8},{4,12},{8,0},{12,4},{1,9},{5,13},{9,1},{13,5},{2,10},{6,14},... | collective-permute-start | bytes 786440 | tf_op jit(solution)/shard_map/ppermute | solution.py:201
  54.7 0.0 collective-permute-done.2.refs_3_
  54.8 3.4 %collective-permute-start.5 = (bf16[256,512]{1,0:T(8,128)(2,1)S(1)}, bf16[256,512]{1,0:T(8,128)(2,1)}, u32[]{:S(2)}, u32[]{:S(2)}) collective-permute-start(bf16[256,512]{1,0:T(8,128)(2,1)S(1)} %collective-permute-done.3.refs_4_), channel_id=1, source_target_pairs={{0,4},{4,8},{8,12},{12,0},{1,5},{5,9},{9,13},{13,1},{2,6},{6,10},{... | collective-permute-start | bytes 786440 | tf_op jit(solution)/shard_map/ppermute | solution.py:201
  58.1 0.1 pad_add_fusion.place_ref
  58.2 0.0 all-to-all-done.refs_0_
  58.2 1.7 %shard_map.73 = bf16[64,8,512]{2,1,0:T(8,128)(2,1)} custom-call(bf16[4,64,8,512]{3,2,1,0:T(8,128)(2,1)S(1)} %all-to-all-done.refs_0_), custom_call_target="tpu_custom_call" | custom-call | tf_op jit(solution)/shard_map/pallas_call | solution.py:218
  59.9 4.8 %all-to-all-start.1 = ((bf16[4,16,8,512]{3,2,1,0:T(8,128)(2,1)}), bf16[4,16,8,512]{3,2,1,0:T(8,128)(2,1)S(1)}, u32[]{:S(2)}, u32[]{:S(2)}) async-start(bf16[4,16,8,512]{3,2,1,0:T(8,128)(2,1)} %bitcast.6), calls=%async_computation.1 | async-start | bytes 1048576 | tf_op jit(solution)/shard_map/all_to_all | solution.py:254
  64.7 0.0 collective-permute-done.1.refs_2_
  64.7 0.0 collective-permute-done.refs_1_
  64.7 0.0 collective-permute-done.7.refs_7_
  64.7 0.0 collective-permute-done.6.refs_6_
  64.7 5.9 %collective-permute-done.5.refs_5_ = bf16[256,512]{1,0:T(8,128)(2,1)} collective-permute-done((bf16[256,512]{1,0:T(8,128)(2,1)S(1)}, bf16[256,512]{1,0:T(8,128)(2,1)}, u32[]{:S(2)}, u32[]{:S(2)}) %collective-permute-start.5) | collective-permute-done | bytes 262176 | tf_op jit(solution)/shard_map/ppermute | solution.py:201
  70.6 2.6 %shard_map.70.weight_ref = bf16[2048,512]{1,0:T(8,128)(2,1)} custom-call(bf16[256,512]{1,0:T(8,128)(2,1)S(1)} %shard_map.67.refs_0_, bf16[256,512]{1,0:T(8,128)(2,1)S(1)} %collective-permute-done.refs_1_, bf16[256,512]{1,0:T(8,128)(2,1)S(1)} %collective-permute-done.1.refs_2_, bf16[256,512]{1,0:T(8,128)(2,1)S(1)} %collective-permute-done.2.refs_3_, ...), custom_call_target="tpu_custom_call" | custom-call | flops 99999997952 | bytes 4194304 | tf_op jit(solution)/shard_map/pallas_call | solution.py:107
  73.2 2.7 %collective-permute-start.8 = (bf16[2048,512]{1,0:T(8,128)(2,1)}, bf16[2048,512]{1,0:T(8,128)(2,1)}, u32[]{:S(2)}, u32[]{:S(2)}) collective-permute-start(bf16[2048,512]{1,0:T(8,128)(2,1)} %shard_map.70.weight_ref), channel_id=1, source_target_pairs={{0,1},{1,0},{2,3},{3,2},{4,5},{5,4},{6,7},{7,6},{8,9},{9,8},{10,11... | collective-permute-start | bytes 6291464 | tf_op jit(solution)/shard_map/ppermute | solution.py:229
  75.9 0.0 all-to-all-done.1.refs_0_
  75.9 0.8 shard_map.74
  76.7 23.2 %all-to-all-start.2 = ((bf16[16,8,512]{2,1,0:T(8,128)(2,1)}), bf16[16,8,512]{2,1,0:T(8,128)(2,1)S(1)}, u32[]{:S(2)}, u32[]{:S(2)}) async-start(bf16[16,8,512]{2,1,0:T(8,128)(2,1)} %shard_map.74), calls=%async_computation.2 | async-start | bytes 262144 | tf_op jit(solution)/shard_map/all_to_all | solution.py:259
  99.9 0.0 copy-done.1
  99.9 0.0 copy-start.3
  99.9 2.7 %shard_map.71 = (f32[128,512]{1,0:T(8,128)S(1)}, bf16[8,128,256]{2,1,0:T(8,128)(2,1)S(1)}) custom-call(s32[3]{0:T(128)S(1)} %pad_add_fusion.place_ref, bf16[128,4096]{1,0:T(8,128)(2,1)S(1)} %copy-done.1, bf16[128,512]{1,0:T(8,128)(2,1)S(1)} %get-tuple-element.16.pre_ref, bf16[2048,512]{1,0:T(8,128)(2,1)} %shard_map.70.weight_ref), custom_call_target="tpu_custom_call" | custom-call | flops 99999997952 | bytes 4194304 | tf_op jit(solution)/shard_map/pallas_call | solution.py:168
  102.6 0.0 collective-permute-done.8.weight_ref
  102.6 3.6 %shard_map.72 = (bf16[128,512]{1,0:T(8,128)(2,1)}, bf16[128,4096]{1,0:T(8,128)(2,1)}) custom-call(s32[3]{0:T(128)S(1)} %pad_add_fusion.place_ref, bf16[128,4096]{1,0:T(8,128)(2,1)S(1)} %copy-done.1, bf16[128,512]{1,0:T(8,128)(2,1)S(1)} %get-tuple-element.16.pre_ref, f32[128,128]{1,0:T(8,128)S(1)} %copy-done.3, f32[128,128]{1,0:T(8,128)S(1)} %copy-done.5, ...), custom_call_target="tpu_custom_call" | custom-call | flops 536870912 | bytes 4194304 | tf_op jit(solution)/shard_map/pallas_call | solution.py:183
  106.2 7.0 %all-to-all-done.2.refs_0_ = bf16[16,8,512]{2,1,0:T(8,128)(2,1)S(1)} async-done(((bf16[16,8,512]{2,1,0:T(8,128)(2,1)}), bf16[16,8,512]{2,1,0:T(8,128)(2,1)S(1)}, u32[]{:S(2)}, u32[]{:S(2)}) %all-to-all-start.2) | async-done | bytes 131104 | tf_op jit(solution)/shard_map/all_to_all | solution.py:259
  113.3 0.6 shard_map.75
  (7 shorter events, 0.0 us)
Async XLA Ops:
  1.5 1.0 copy-start.6
  3.0 4.7 %copy-start.2 = (f32[128,128]{1,0:T(8,128)}, f32[128,128]{1,0:T(8,128)S(1)}, u32[]{:S(2)}) copy-start(f32[128,128]{1,0:T(8,128)S(1)} %get-tuple-element.30.cos_ref) | copy-start | bytes 196612
  3.0 17.3 %copy-start.4 = (f32[128,128]{1,0:T(8,128)}, f32[128,128]{1,0:T(8,128)S(1)}, u32[]{:S(2)}) copy-start(f32[128,128]{1,0:T(8,128)S(1)} %get-tuple-element.31.sin_ref) | copy-start | bytes 196612
  3.1 1.3 %copy-start = (bf16[128,4096]{1,0:T(8,128)(2,1)S(1)}, bf16[128,4096]{1,0:T(8,128)(2,1)}, u32[]{:S(2)}) copy-start(bf16[128,4096]{1,0:T(8,128)(2,1)} %token_ref.4) | copy-start | bytes 3145732
  4.3 0.9 copy-start.7
  7.7 12.6 %collective-permute-start.4 = (bf16[4,4,8,2,8,512]{5,4,3,2,1,0:T(8,128)(2,1)S(1)}, bf16[4,4,8,2,8,512]{5,4,3,2,1,0:T(8,128)(2,1)S(1)}, u32[]{:S(2)}, u32[]{:S(2)}) collective-permute-start(bf16[4,4,8,2,8,512]{5,4,3,2,1,0:T(8,128)(2,1)S(1)} %get-tuple-element.17), channel_id=1, source_target_pairs={{0,1},{1,0},{2,3},{3,2},{4,5},{5,4},{6,7},{7,6},{8,9},{9,8},{10,11... | collective-permute-start | bytes 6291464 | tf_op jit(solution)/shard_map/ppermute | solution.py:229
  23.5 34.7 %all-to-all-start = ((bf16[4,64,8,512]{3,2,1,0:T(8,128)(2,1)}), bf16[4,64,8,512]{3,2,1,0:T(8,128)(2,1)S(1)}, u32[]{:S(2)}, u32[]{:S(2)}) async-start(bf16[4,64,8,512]{3,2,1,0:T(8,128)(2,1)} %bitcast.5), calls=%async_computation | async-start | bytes 4194304 | tf_op jit(solution)/shard_map/all_to_all | solution.py:246
  27.1 23.8 %collective-permute-start.3 = (bf16[256,512]{1,0:T(8,128)(2,1)S(1)}, bf16[256,512]{1,0:T(8,128)(2,1)S(1)}, u32[]{:S(2)}, u32[]{:S(2)}) collective-permute-start(bf16[256,512]{1,0:T(8,128)(2,1)S(1)} %shard_map.67.refs_0_), channel_id=1, source_target_pairs={{0,2},{2,0},{1,3},{3,1},{4,6},{6,4},{5,7},{7,5},{8,10},{10,8},{9,1... | collective-permute-start | bytes 786440 | tf_op jit(solution)/shard_map/ppermute | solution.py:229
  37.7 17.0 %collective-permute-start.2 = (bf16[256,512]{1,0:T(8,128)(2,1)S(1)}, bf16[256,512]{1,0:T(8,128)(2,1)S(1)}, u32[]{:S(2)}, u32[]{:S(2)}) collective-permute-start(bf16[256,512]{1,0:T(8,128)(2,1)S(1)} %shard_map.67.refs_0_), channel_id=1, source_target_pairs={{0,12},{4,0},{8,4},{12,8},{1,13},{5,1},{9,5},{13,9},{2,14},{6,2},{... | collective-permute-start | bytes 786440 | tf_op jit(solution)/shard_map/ppermute | solution.py:201
  42.1 22.6 %collective-permute-start.1 = (bf16[256,512]{1,0:T(8,128)(2,1)S(1)}, bf16[256,512]{1,0:T(8,128)(2,1)S(1)}, u32[]{:S(2)}, u32[]{:S(2)}) collective-permute-start(bf16[256,512]{1,0:T(8,128)(2,1)S(1)} %shard_map.67.refs_0_), channel_id=1, source_target_pairs={{0,8},{4,12},{8,0},{12,4},{1,9},{5,13},{9,1},{13,5},{2,10},{6,14},... | collective-permute-start | bytes 786440 | tf_op jit(solution)/shard_map/ppermute | solution.py:201
  44.5 20.2 %collective-permute-start = (bf16[256,512]{1,0:T(8,128)(2,1)S(1)}, bf16[256,512]{1,0:T(8,128)(2,1)S(1)}, u32[]{:S(2)}, u32[]{:S(2)}) collective-permute-start(bf16[256,512]{1,0:T(8,128)(2,1)S(1)} %shard_map.67.refs_0_), channel_id=1, source_target_pairs={{0,4},{4,8},{8,12},{12,0},{1,5},{5,9},{9,13},{13,1},{2,6},{6,10},{... | collective-permute-start | bytes 786440 | tf_op jit(solution)/shard_map/ppermute | solution.py:201
  50.9 13.8 %collective-permute-start.7 = (bf16[256,512]{1,0:T(8,128)(2,1)S(1)}, bf16[256,512]{1,0:T(8,128)(2,1)}, u32[]{:S(2)}, u32[]{:S(2)}) collective-permute-start(bf16[256,512]{1,0:T(8,128)(2,1)S(1)} %collective-permute-done.3.refs_4_), channel_id=1, source_target_pairs={{0,12},{4,0},{8,4},{12,8},{1,13},{5,1},{9,5},{13,9},{2,14},{6,2},{... | collective-permute-start | bytes 786440 | tf_op jit(solution)/shard_map/ppermute | solution.py:201
  52.8 11.9 %collective-permute-start.6 = (bf16[256,512]{1,0:T(8,128)(2,1)S(1)}, bf16[256,512]{1,0:T(8,128)(2,1)}, u32[]{:S(2)}, u32[]{:S(2)}) collective-permute-start(bf16[256,512]{1,0:T(8,128)(2,1)S(1)} %collective-permute-done.3.refs_4_), channel_id=1, source_target_pairs={{0,8},{4,12},{8,0},{12,4},{1,9},{5,13},{9,1},{13,5},{2,10},{6,14},... | collective-permute-start | bytes 786440 | tf_op jit(solution)/shard_map/ppermute | solution.py:201
  54.8 15.9 %collective-permute-start.5 = (bf16[256,512]{1,0:T(8,128)(2,1)S(1)}, bf16[256,512]{1,0:T(8,128)(2,1)}, u32[]{:S(2)}, u32[]{:S(2)}) collective-permute-start(bf16[256,512]{1,0:T(8,128)(2,1)S(1)} %collective-permute-done.3.refs_4_), channel_id=1, source_target_pairs={{0,4},{4,8},{8,12},{12,0},{1,5},{5,9},{9,13},{13,1},{2,6},{6,10},{... | collective-permute-start | bytes 786440 | tf_op jit(solution)/shard_map/ppermute | solution.py:201
  59.9 16.0 %all-to-all-start.1 = ((bf16[4,16,8,512]{3,2,1,0:T(8,128)(2,1)}), bf16[4,16,8,512]{3,2,1,0:T(8,128)(2,1)S(1)}, u32[]{:S(2)}, u32[]{:S(2)}) async-start(bf16[4,16,8,512]{3,2,1,0:T(8,128)(2,1)} %bitcast.6), calls=%async_computation.1 | async-start | bytes 1048576 | tf_op jit(solution)/shard_map/all_to_all | solution.py:254
  64.7 35.2 %copy-start.1 = (bf16[128,4096]{1,0:T(8,128)(2,1)S(1)}, bf16[128,4096]{1,0:T(8,128)(2,1)}, u32[]{:S(2)}) copy-start(bf16[128,4096]{1,0:T(8,128)(2,1)} %token_ref.4) | copy-start | bytes 3145732
  73.2 29.4 %collective-permute-start.8 = (bf16[2048,512]{1,0:T(8,128)(2,1)}, bf16[2048,512]{1,0:T(8,128)(2,1)}, u32[]{:S(2)}, u32[]{:S(2)}) collective-permute-start(bf16[2048,512]{1,0:T(8,128)(2,1)} %shard_map.70.weight_ref), channel_id=1, source_target_pairs={{0,1},{1,0},{2,3},{3,2},{4,5},{5,4},{6,7},{7,6},{8,9},{9,8},{10,11... | collective-permute-start | bytes 6291464 | tf_op jit(solution)/shard_map/ppermute | solution.py:229
  76.7 36.6 %all-to-all-start.2 = ((bf16[16,8,512]{2,1,0:T(8,128)(2,1)}), bf16[16,8,512]{2,1,0:T(8,128)(2,1)S(1)}, u32[]{:S(2)}, u32[]{:S(2)}) async-start(bf16[16,8,512]{2,1,0:T(8,128)(2,1)} %shard_map.74), calls=%async_computation.2 | async-start | bytes 262144 | tf_op jit(solution)/shard_map/all_to_all | solution.py:259
  99.9 2.7 %copy-start.3 = (f32[128,128]{1,0:T(8,128)S(1)}, f32[128,128]{1,0:T(8,128)}, u32[]{:S(2)}) copy-start(f32[128,128]{1,0:T(8,128)} %copy-done.2) | copy-start | bytes 196612
  99.9 2.7 %copy-start.5 = (f32[128,128]{1,0:T(8,128)S(1)}, f32[128,128]{1,0:T(8,128)}, u32[]{:S(2)}) copy-start(f32[128,128]{1,0:T(8,128)} %copy-done.4) | copy-start | bytes 196612

commit v7 on v6

--- a/solution.py
+++ b/solution.py
@@ -110,6 +110,21 @@
         compiler_params=PARAMS,
         cost_estimate=pl.CostEstimate(flops=100000000000, bytes_accessed=4 * 1024 * 1024, transcendentals=0),
     )(*blocks)
+
+
+def relay_kernel(block_ref, out_ref):
+    out_ref[...] = block_ref[...]
+
+
+def relayed(block):
+    return pl.pallas_call(
+        relay_kernel,
+        out_shape=jax.ShapeDtypeStruct(block.shape, block.dtype),
+        compiler_params=PARAMS,
+        cost_estimate=pl.CostEstimate(
+            flops=100000000000, bytes_accessed=512 * 1024, transcendentals=0
+        ),
+    )(block)
 
 
 def first_column(place_ref, block, side, rows):
@@ -246,8 +261,8 @@
     got = lax.all_to_all(summed, "y", split_axis=0, concat_axis=0, tiled=True)
 
     shard = after(shard, theirs)
-    far_shard = after(swap(shard, "zh"), summed)
-    near = from_x(shard)
+    far_shard = relayed(after(swap(shard, "zh"), summed))
+    near = from_x(after(shard, summed))
     far = from_x(far_shard)
 
     summed = summed_first(got, steps=4).reshape(X, ZL * ZH, ROW, features)

time: 116 us -> 106 us (0.914)
  starting transfers between devices: 70.3 us -> 64.4 us
  waiting for transfers between devices: 20.5 us -> 15.2 us
  local copies, waits for them, and re-layouts: 3.95 us -> 5.6 us
    ppermute x3, waiting for transfers between devices: 7.61 us -> 0.01 us  [swap(): return lax.ppermute(value, axis, [(0, 1), (1, 0)])]
    all_to_all x1, starting transfers between devices: 23.2 us -> 16.5 us  [on_device(): lax.all_to_all(summed, ('zl', 'zh'), split_axis=0, concat_axis=0, tiled=T...]
    all_to_all x1, waiting for transfers between devices: 0.01 us -> 5.77 us  [on_device(): got = lax.all_to_all(summed, 'y', split_axis=0, concat_axis=0, tiled=True)]
    ppermute x6, waiting for transfers between devices: 5.9 us -> 1.25 us  [from_x(): lax.ppermute(shard, 'x', [(i, (i + k) % X) for i in range(X)])]
    ppermute x6, starting transfers between devices: 16.5 us -> 18.4 us  [from_x(): lax.ppermute(shard, 'x', [(i, (i + k) % X) for i in range(X)])]
    unnamed x17 -> x21, local copies, waits for them, and re-layouts: 3.95 us -> 5.6 us
  transfers between devices with their start and end apart: 12 -> 12, of which waited for: 4 -> 4; matrix products, arithmetic and copies ran while one was open for 0% -> 0% of each run, Pallas kernels for 10% -> 14%
where the time goes in v7:
time: 106 us; the launch traced here: 104 us
  starting transfers between devices  64.4 us (61%)
  Pallas kernels  17.8 us (17%)
  waiting for transfers between devices  15.2 us (14%)
  local copies, waits for them, and re-layouts  5.6 us (5%)
    ppermute x3, starting transfers between devices, swap(): return lax.ppermute(value, axis, [(0, 1), (1, 0)])  21.5 us
    ppermute x6, starting transfers between devices, from_x(): lax.ppermute(shard, 'x', [(i, (i + k) % X) for i in range(X)])  18.4 us
    all_to_all x1, starting transfers between devices, on_device(): lax.all_to_all(summed, ('zl', 'zh'), split_axis=0, concat_axis=0, tiled=T...  16.5 us
    all_to_all x1, waiting for transfers between devices, on_device(): lax.all_to_all(summed, ('zl', 'zh'), split_axis=0, concat_axis=0, tiled=T...  7.17 us
    pallas_call x4, Pallas kernels, summed_first(): pl.pallas_call(functools.partial(sum_kernel, factor), grid=(steps,), in_s...  6.24 us
    all_to_all x1, waiting for transfers between devices, on_device(): got = lax.all_to_all(summed, 'y', split_axis=0, concat_axis=0, tiled=True)  5.77 us
    unnamed x21, local copies, waits for them, and re-layouts  5.6 us
    all_to_all x1, starting transfers between devices, on_device(): got = lax.all_to_all(summed, 'y', split_axis=0, concat_axis=0, tiled=True)  4.19 us
  transfers between devices with their start and end apart: 12, of which 4 were waited for; matrix products, arithmetic and copies ran while one was open for 0% of the time, Pallas kernels for 14%

profile of v7, /device:TPU:1, one launch (start us, length us, event | category | flops | bytes accessed | tf_op | source)
XLA Modules:
  0.0 104.4 jit_solution(7389027335168798994)
XLA Ops:
  0.7 0.8 copy.7.exponent_ref
  1.5 0.0 copy-start.6
  1.5 0.9 copy-done.6
  2.5 0.1 shard_map.67.refs_0_
  2.6 0.3 fusion
  2.9 0.1 pad_maximum_fusion
  3.0 0.0 copy-start.2
  3.1 0.0 copy-start
  3.1 1.3 %copy-done = bf16[128,4096]{1,0:T(8,128)(2,1)S(1)} copy-done((bf16[128,4096]{1,0:T(8,128)(2,1)S(1)}, bf16[128,4096]{1,0:T(8,128)(2,1)}, u32[]{:S(2)}) %copy-start) | copy-done | bytes 1048600
  4.3 0.9 copy-done.7
  5.2 2.5 %shard_map.68 = (bf16[4,4,8,2,8,512]{5,4,3,2,1,0:T(8,128)(2,1)S(1)}, bf16[4,4,8,2,8,512]{5,4,3,2,1,0:T(8,128)(2,1)S(1)}, bf16[128,512]{1,0:T(8,128)(2,1)S(1)}) custom-call(s32[1]{0:T(128)} %bitcast.2.core_ref, bf16[128,4096]{1,0:T(8,128)(2,1)S(1)} %copy-done, bf16[128,512]{1,0:T(8,128)(2,1)S(1)} %copy-done.7, f32[128,128]{1,0:T(8,128)S(1)} %get-tuple-element.32.cos_ref, ...), custom_call_target="tpu_custom_call" | custom-call | tf_op jit(solution)/shard_map/pallas_call | solution.py:82
  7.7 0.0 copy-done.2
  7.7 8.8 %collective-permute-start = (bf16[4,4,8,2,8,512]{5,4,3,2,1,0:T(8,128)(2,1)S(1)}, bf16[4,4,8,2,8,512]{5,4,3,2,1,0:T(8,128)(2,1)S(1)}, u32[]{:S(2)}, u32[]{:S(2)}) collective-permute-start(bf16[4,4,8,2,8,512]{5,4,3,2,1,0:T(8,128)(2,1)S(1)} %get-tuple-element.18), channel_id=1, source_target_pairs={{0,1},{1,0},{2,3},{3,2},{4,5},{5,4},{6,7},{7,6},{8,9},{9,8},{10,11... | collective-permute-start | bytes 6291464 | tf_op jit(solution)/shard_map/ppermute | solution.py:244
  16.5 10.1 %collective-permute-start.4 = (bf16[256,512]{1,0:T(8,128)(2,1)S(1)}, bf16[256,512]{1,0:T(8,128)(2,1)S(1)}, u32[]{:S(2)}, u32[]{:S(2)}) collective-permute-start(bf16[256,512]{1,0:T(8,128)(2,1)S(1)} %shard_map.67.refs_0_), channel_id=1, source_target_pairs={{0,2},{2,0},{1,3},{3,1},{4,6},{6,4},{5,7},{7,5},{8,10},{10,8},{9,1... | collective-permute-start | bytes 786440 | tf_op jit(solution)/shard_map/ppermute | solution.py:244
  26.6 0.0 collective-permute-done
  26.6 3.2 %shard_map.69 = bf16[256,8,512]{2,1,0:T(8,128)(2,1)} custom-call(bf16[1,256,8,512]{3,2,1,0:T(8,128)(2,1)S(1)} %bitcast.7, bf16[1,256,8,512]{3,2,1,0:T(8,128)(2,1)S(1)} %bitcast.8), custom_call_target="tpu_custom_call" | custom-call | tf_op jit(solution)/shard_map/pallas_call | solution.py:233
  29.8 4.2 %all-to-all-start = ((bf16[4,64,8,512]{3,2,1,0:T(8,128)(2,1)}), bf16[4,64,8,512]{3,2,1,0:T(8,128)(2,1)S(1)}, u32[]{:S(2)}, u32[]{:S(2)}) async-start(bf16[4,64,8,512]{3,2,1,0:T(8,128)(2,1)} %bitcast.5), calls=%async_computation | async-start | bytes 4194304 | tf_op jit(solution)/shard_map/all_to_all | solution.py:261
  34.0 4.4 %collective-permute-start.3 = (bf16[256,512]{1,0:T(8,128)(2,1)S(1)}, bf16[256,512]{1,0:T(8,128)(2,1)S(1)}, u32[]{:S(2)}, u32[]{:S(2)}) collective-permute-start(bf16[256,512]{1,0:T(8,128)(2,1)S(1)} %shard_map.67.refs_0_), channel_id=1, source_target_pairs={{0,12},{4,0},{8,4},{12,8},{1,13},{5,1},{9,5},{13,9},{2,14},{6,2},{... | collective-permute-start | bytes 786440 | tf_op jit(solution)/shard_map/ppermute | solution.py:216
  38.4 2.4 %collective-permute-start.2 = (bf16[256,512]{1,0:T(8,128)(2,1)S(1)}, bf16[256,512]{1,0:T(8,128)(2,1)S(1)}, u32[]{:S(2)}, u32[]{:S(2)}) collective-permute-start(bf16[256,512]{1,0:T(8,128)(2,1)S(1)} %shard_map.67.refs_0_), channel_id=1, source_target_pairs={{0,8},{4,12},{8,0},{12,4},{1,9},{5,13},{9,1},{13,5},{2,10},{6,14},... | collective-permute-start | bytes 786440 | tf_op jit(solution)/shard_map/ppermute | solution.py:216
  40.8 2.5 %collective-permute-start.1 = (bf16[256,512]{1,0:T(8,128)(2,1)S(1)}, bf16[256,512]{1,0:T(8,128)(2,1)S(1)}, u32[]{:S(2)}, u32[]{:S(2)}) collective-permute-start(bf16[256,512]{1,0:T(8,128)(2,1)S(1)} %shard_map.67.refs_0_), channel_id=1, source_target_pairs={{0,4},{4,8},{8,12},{12,0},{1,5},{5,9},{9,13},{13,1},{2,6},{6,10},{... | collective-permute-start | bytes 786440 | tf_op jit(solution)/shard_map/ppermute | solution.py:216
  43.3 0.0 collective-permute-done.4.block_ref
  43.4 0.0 copy-start.8
  43.4 0.7 copy-done.8
  44.1 0.9 copy-done.9
  45.0 4.0 %collective-permute-start.7 = (bf16[256,512]{1,0:T(8,128)(2,1)S(1)}, bf16[256,512]{1,0:T(8,128)(2,1)}, u32[]{:S(2)}, u32[]{:S(2)}) collective-permute-start(bf16[256,512]{1,0:T(8,128)(2,1)S(1)} %shard_map.70.refs_4_), channel_id=1, source_target_pairs={{0,12},{4,0},{8,4},{12,8},{1,13},{5,1},{9,5},{13,9},{2,14},{6,2},{... | collective-permute-start | bytes 786440 | tf_op jit(solution)/shard_map/ppermute | solution.py:216
  49.0 3.2 %collective-permute-start.6 = (bf16[256,512]{1,0:T(8,128)(2,1)S(1)}, bf16[256,512]{1,0:T(8,128)(2,1)}, u32[]{:S(2)}, u32[]{:S(2)}) collective-permute-start(bf16[256,512]{1,0:T(8,128)(2,1)S(1)} %shard_map.70.refs_4_), channel_id=1, source_target_pairs={{0,8},{4,12},{8,0},{12,4},{1,9},{5,13},{9,1},{13,5},{2,10},{6,14},... | collective-permute-start | bytes 786440 | tf_op jit(solution)/shard_map/ppermute | solution.py:216
  52.2 0.0 collective-permute-done.3.refs_3_
  52.2 1.9 %collective-permute-start.5 = (bf16[256,512]{1,0:T(8,128)(2,1)S(1)}, bf16[256,512]{1,0:T(8,128)(2,1)}, u32[]{:S(2)}, u32[]{:S(2)}) collective-permute-start(bf16[256,512]{1,0:T(8,128)(2,1)S(1)} %shard_map.70.refs_4_), channel_id=1, source_target_pairs={{0,4},{4,8},{8,12},{12,0},{1,5},{5,9},{9,13},{13,1},{2,6},{6,10},{... | collective-permute-start | bytes 786440 | tf_op jit(solution)/shard_map/ppermute | solution.py:216
  54.1 0.1 pad_add_fusion.place_ref
  54.2 5.8 %all-to-all-done.refs_0_ = bf16[4,64,8,512]{3,2,1,0:T(8,128)(2,1)S(1)} async-done(((bf16[4,64,8,512]{3,2,1,0:T(8,128)(2,1)}), bf16[4,64,8,512]{3,2,1,0:T(8,128)(2,1)S(1)}, u32[]{:S(2)}, u32[]{:S(2)}) %all-to-all-start) | async-done | bytes 2097184 | tf_op jit(solution)/shard_map/all_to_all | solution.py:261
  60.0 1.6 %shard_map.74 = bf16[64,8,512]{2,1,0:T(8,128)(2,1)} custom-call(bf16[4,64,8,512]{3,2,1,0:T(8,128)(2,1)S(1)} %all-to-all-done.refs_0_), custom_call_target="tpu_custom_call" | custom-call | tf_op jit(solution)/shard_map/pallas_call | solution.py:233
  61.6 3.9 %all-to-all-start.1 = ((bf16[4,16,8,512]{3,2,1,0:T(8,128)(2,1)}), bf16[4,16,8,512]{3,2,1,0:T(8,128)(2,1)S(1)}, u32[]{:S(2)}, u32[]{:S(2)}) async-start(bf16[4,16,8,512]{3,2,1,0:T(8,128)(2,1)} %bitcast.6), calls=%async_computation.1 | async-start | bytes 1048576 | tf_op jit(solution)/shard_map/all_to_all | solution.py:269
  65.5 0.0 collective-permute-done.2.refs_2_
  65.5 0.0 collective-permute-done.1.refs_1_
  65.5 0.0 collective-permute-done.7.refs_7_
  65.5 0.0 collective-permute-done.6.refs_6_
  65.6 1.2 %collective-permute-done.5.refs_5_ = bf16[256,512]{1,0:T(8,128)(2,1)} collective-permute-done((bf16[256,512]{1,0:T(8,128)(2,1)S(1)}, bf16[256,512]{1,0:T(8,128)(2,1)}, u32[]{:S(2)}, u32[]{:S(2)}) %collective-permute-start.5) | collective-permute-done | bytes 262176 | tf_op jit(solution)/shard_map/ppermute | solution.py:216
  66.8 2.6 %shard_map.71.weight_ref = bf16[2048,512]{1,0:T(8,128)(2,1)} custom-call(bf16[256,512]{1,0:T(8,128)(2,1)S(1)} %shard_map.67.refs_0_, bf16[256,512]{1,0:T(8,128)(2,1)S(1)} %collective-permute-done.1.refs_1_, bf16[256,512]{1,0:T(8,128)(2,1)S(1)} %collective-permute-done.2.refs_2_, bf16[256,512]{1,0:T(8,128)(2,1)S(1)} %collective-permute-done.3.refs_3_, ...), custom_call_target="tpu_custom_call" | custom-call | flops 99999997952 | bytes 4194304 | tf_op jit(solution)/shard_map/pallas_call | solution.py:107
  69.4 2.7 %collective-permute-start.8 = (bf16[2048,512]{1,0:T(8,128)(2,1)}, bf16[2048,512]{1,0:T(8,128)(2,1)}, u32[]{:S(2)}, u32[]{:S(2)}) collective-permute-start(bf16[2048,512]{1,0:T(8,128)(2,1)} %shard_map.71.weight_ref), channel_id=1, source_target_pairs={{0,1},{1,0},{2,3},{3,2},{4,5},{5,4},{6,7},{7,6},{8,9},{9,8},{10,11... | collective-permute-start | bytes 6291464 | tf_op jit(solution)/shard_map/ppermute | solution.py:244
  72.0 1.0 all-to-all-done.1.refs_0_
  73.0 0.8 shard_map.75
  73.8 16.5 %all-to-all-start.2 = ((bf16[16,8,512]{2,1,0:T(8,128)(2,1)}), bf16[16,8,512]{2,1,0:T(8,128)(2,1)S(1)}, u32[]{:S(2)}, u32[]{:S(2)}) async-start(bf16[16,8,512]{2,1,0:T(8,128)(2,1)} %shard_map.75), calls=%async_computation.2 | async-start | bytes 262144 | tf_op jit(solution)/shard_map/all_to_all | solution.py:274
  90.3 0.0 copy-start.3
  90.3 2.7 %shard_map.72 = (f32[128,512]{1,0:T(8,128)S(1)}, bf16[8,128,256]{2,1,0:T(8,128)(2,1)S(1)}) custom-call(s32[3]{0:T(128)S(1)} %pad_add_fusion.place_ref, bf16[128,4096]{1,0:T(8,128)(2,1)S(1)} %copy-done.1, bf16[128,512]{1,0:T(8,128)(2,1)S(1)} %get-tuple-element.17.pre_ref, bf16[2048,512]{1,0:T(8,128)(2,1)} %shard_map.71.weight_ref), custom_call_target="tpu_custom_call" | custom-call | flops 99999997952 | bytes 4194304 | tf_op jit(solution)/shard_map/pallas_call | solution.py:183
  93.0 0.0 collective-permute-done.8.weight_ref
  93.0 3.6 %shard_map.73 = (bf16[128,512]{1,0:T(8,128)(2,1)}, bf16[128,4096]{1,0:T(8,128)(2,1)}) custom-call(s32[3]{0:T(128)S(1)} %pad_add_fusion.place_ref, bf16[128,4096]{1,0:T(8,128)(2,1)S(1)} %copy-done.1, bf16[128,512]{1,0:T(8,128)(2,1)S(1)} %get-tuple-element.17.pre_ref, f32[128,128]{1,0:T(8,128)S(1)} %copy-done.3, f32[128,128]{1,0:T(8,128)S(1)} %copy-done.5, ...), custom_call_target="tpu_custom_call" | custom-call | flops 536870912 | bytes 4194304 | tf_op jit(solution)/shard_map/pallas_call | solution.py:198
  96.7 7.2 %all-to-all-done.2.refs_0_ = bf16[16,8,512]{2,1,0:T(8,128)(2,1)S(1)} async-done(((bf16[16,8,512]{2,1,0:T(8,128)(2,1)}), bf16[16,8,512]{2,1,0:T(8,128)(2,1)S(1)}, u32[]{:S(2)}, u32[]{:S(2)}) %all-to-all-start.2) | async-done | bytes 131104 | tf_op jit(solution)/shard_map/all_to_all | solution.py:274
  103.8 0.6 shard_map.76
  (12 shorter events, 0.1 us)
Async XLA Ops:
  1.5 1.0 copy-start.6
  3.0 4.7 %copy-start.2 = (f32[128,128]{1,0:T(8,128)}, f32[128,128]{1,0:T(8,128)S(1)}, u32[]{:S(2)}) copy-start(f32[128,128]{1,0:T(8,128)S(1)} %get-tuple-element.32.cos_ref) | copy-start | bytes 196612
  3.0 23.6 %copy-start.4 = (f32[128,128]{1,0:T(8,128)}, f32[128,128]{1,0:T(8,128)S(1)}, u32[]{:S(2)}) copy-start(f32[128,128]{1,0:T(8,128)S(1)} %get-tuple-element.33.sin_ref) | copy-start | bytes 196612
  3.1 1.3 %copy-start = (bf16[128,4096]{1,0:T(8,128)(2,1)S(1)}, bf16[128,4096]{1,0:T(8,128)(2,1)}, u32[]{:S(2)}) copy-start(bf16[128,4096]{1,0:T(8,128)(2,1)} %token_ref.4) | copy-start | bytes 3145732
  4.3 0.9 copy-start.7
  7.7 18.9 %collective-permute-start = (bf16[4,4,8,2,8,512]{5,4,3,2,1,0:T(8,128)(2,1)S(1)}, bf16[4,4,8,2,8,512]{5,4,3,2,1,0:T(8,128)(2,1)S(1)}, u32[]{:S(2)}, u32[]{:S(2)}) collective-permute-start(bf16[4,4,8,2,8,512]{5,4,3,2,1,0:T(8,128)(2,1)S(1)} %get-tuple-element.18), channel_id=1, source_target_pairs={{0,1},{1,0},{2,3},{3,2},{4,5},{5,4},{6,7},{7,6},{8,9},{9,8},{10,11... | collective-permute-start | bytes 6291464 | tf_op jit(solution)/shard_map/ppermute | solution.py:244
  16.5 26.8 %collective-permute-start.4 = (bf16[256,512]{1,0:T(8,128)(2,1)S(1)}, bf16[256,512]{1,0:T(8,128)(2,1)S(1)}, u32[]{:S(2)}, u32[]{:S(2)}) collective-permute-start(bf16[256,512]{1,0:T(8,128)(2,1)S(1)} %shard_map.67.refs_0_), channel_id=1, source_target_pairs={{0,2},{2,0},{1,3},{3,1},{4,6},{6,4},{5,7},{7,5},{8,10},{10,8},{9,1... | collective-permute-start | bytes 786440 | tf_op jit(solution)/shard_map/ppermute | solution.py:244
  29.8 30.1 %all-to-all-start = ((bf16[4,64,8,512]{3,2,1,0:T(8,128)(2,1)}), bf16[4,64,8,512]{3,2,1,0:T(8,128)(2,1)S(1)}, u32[]{:S(2)}, u32[]{:S(2)}) async-start(bf16[4,64,8,512]{3,2,1,0:T(8,128)(2,1)} %bitcast.5), calls=%async_computation | async-start | bytes 4194304 | tf_op jit(solution)/shard_map/all_to_all | solution.py:261
  34.0 18.2 %collective-permute-start.3 = (bf16[256,512]{1,0:T(8,128)(2,1)S(1)}, bf16[256,512]{1,0:T(8,128)(2,1)S(1)}, u32[]{:S(2)}, u32[]{:S(2)}) collective-permute-start(bf16[256,512]{1,0:T(8,128)(2,1)S(1)} %shard_map.67.refs_0_), channel_id=1, source_target_pairs={{0,12},{4,0},{8,4},{12,8},{1,13},{5,1},{9,5},{13,9},{2,14},{6,2},{... | collective-permute-start | bytes 786440 | tf_op jit(solution)/shard_map/ppermute | solution.py:216
  38.4 27.1 %collective-permute-start.2 = (bf16[256,512]{1,0:T(8,128)(2,1)S(1)}, bf16[256,512]{1,0:T(8,128)(2,1)S(1)}, u32[]{:S(2)}, u32[]{:S(2)}) collective-permute-start(bf16[256,512]{1,0:T(8,128)(2,1)S(1)} %shard_map.67.refs_0_), channel_id=1, source_target_pairs={{0,8},{4,12},{8,0},{12,4},{1,9},{5,13},{9,1},{13,5},{2,10},{6,14},... | collective-permute-start | bytes 786440 | tf_op jit(solution)/shard_map/ppermute | solution.py:216
  40.8 24.7 %collective-permute-start.1 = (bf16[256,512]{1,0:T(8,128)(2,1)S(1)}, bf16[256,512]{1,0:T(8,128)(2,1)S(1)}, u32[]{:S(2)}, u32[]{:S(2)}) collective-permute-start(bf16[256,512]{1,0:T(8,128)(2,1)S(1)} %shard_map.67.refs_0_), channel_id=1, source_target_pairs={{0,4},{4,8},{8,12},{12,0},{1,5},{5,9},{9,13},{13,1},{2,6},{6,10},{... | collective-permute-start | bytes 786440 | tf_op jit(solution)/shard_map/ppermute | solution.py:216
  43.4 0.7 copy-start.8
  44.1 0.9 copy-start.9
  45.0 20.5 %collective-permute-start.7 = (bf16[256,512]{1,0:T(8,128)(2,1)S(1)}, bf16[256,512]{1,0:T(8,128)(2,1)}, u32[]{:S(2)}, u32[]{:S(2)}) collective-permute-start(bf16[256,512]{1,0:T(8,128)(2,1)S(1)} %shard_map.70.refs_4_), channel_id=1, source_target_pairs={{0,12},{4,0},{8,4},{12,8},{1,13},{5,1},{9,5},{13,9},{2,14},{6,2},{... | collective-permute-start | bytes 786440 | tf_op jit(solution)/shard_map/ppermute | solution.py:216
  49.0 16.5 %collective-permute-start.6 = (bf16[256,512]{1,0:T(8,128)(2,1)S(1)}, bf16[256,512]{1,0:T(8,128)(2,1)}, u32[]{:S(2)}, u32[]{:S(2)}) collective-permute-start(bf16[256,512]{1,0:T(8,128)(2,1)S(1)} %shard_map.70.refs_4_), channel_id=1, source_target_pairs={{0,8},{4,12},{8,0},{12,4},{1,9},{5,13},{9,1},{13,5},{2,10},{6,14},... | collective-permute-start | bytes 786440 | tf_op jit(solution)/shard_map/ppermute | solution.py:216
  52.2 14.6 %collective-permute-start.5 = (bf16[256,512]{1,0:T(8,128)(2,1)S(1)}, bf16[256,512]{1,0:T(8,128)(2,1)}, u32[]{:S(2)}, u32[]{:S(2)}) collective-permute-start(bf16[256,512]{1,0:T(8,128)(2,1)S(1)} %shard_map.70.refs_4_), channel_id=1, source_target_pairs={{0,4},{4,8},{8,12},{12,0},{1,5},{5,9},{9,13},{13,1},{2,6},{6,10},{... | collective-permute-start | bytes 786440 | tf_op jit(solution)/shard_map/ppermute | solution.py:216
  61.6 11.4 %all-to-all-start.1 = ((bf16[4,16,8,512]{3,2,1,0:T(8,128)(2,1)}), bf16[4,16,8,512]{3,2,1,0:T(8,128)(2,1)S(1)}, u32[]{:S(2)}, u32[]{:S(2)}) async-start(bf16[4,16,8,512]{3,2,1,0:T(8,128)(2,1)} %bitcast.6), calls=%async_computation.1 | async-start | bytes 1048576 | tf_op jit(solution)/shard_map/all_to_all | solution.py:269
  65.5 24.8 %copy-start.1 = (bf16[128,4096]{1,0:T(8,128)(2,1)S(1)}, bf16[128,4096]{1,0:T(8,128)(2,1)}, u32[]{:S(2)}) copy-start(bf16[128,4096]{1,0:T(8,128)(2,1)} %token_ref.4) | copy-start | bytes 3145732
  69.4 23.6 %collective-permute-start.8 = (bf16[2048,512]{1,0:T(8,128)(2,1)}, bf16[2048,512]{1,0:T(8,128)(2,1)}, u32[]{:S(2)}, u32[]{:S(2)}) collective-permute-start(bf16[2048,512]{1,0:T(8,128)(2,1)} %shard_map.71.weight_ref), channel_id=1, source_target_pairs={{0,1},{1,0},{2,3},{3,2},{4,5},{5,4},{6,7},{7,6},{8,9},{9,8},{10,11... | collective-permute-start | bytes 6291464 | tf_op jit(solution)/shard_map/ppermute | solution.py:244
  73.8 30.0 %all-to-all-start.2 = ((bf16[16,8,512]{2,1,0:T(8,128)(2,1)}), bf16[16,8,512]{2,1,0:T(8,128)(2,1)S(1)}, u32[]{:S(2)}, u32[]{:S(2)}) async-start(bf16[16,8,512]{2,1,0:T(8,128)(2,1)} %shard_map.75), calls=%async_computation.2 | async-start | bytes 262144 | tf_op jit(solution)/shard_map/all_to_all | solution.py:274
  90.3 2.7 %copy-start.3 = (f32[128,128]{1,0:T(8,128)S(1)}, f32[128,128]{1,0:T(8,128)}, u32[]{:S(2)}) copy-start(f32[128,128]{1,0:T(8,128)} %copy-done.2) | copy-start | bytes 196612
  90.3 2.7 %copy-start.5 = (f32[128,128]{1,0:T(8,128)S(1)}, f32[128,128]{1,0:T(8,128)}, u32[]{:S(2)}) copy-start(f32[128,128]{1,0:T(8,128)} %copy-done.4) | copy-start | bytes 196612

commit v8 on v7

--- a/solution.py
+++ b/solution.py
@@ -25,11 +25,15 @@
 
 
 def dequantize_kernel(code_ref, exponent_ref, weight_ref):
+    rows = code_ref.shape[0]
     scale = jnp.exp2(exponent_ref[...].astype(F32))
+    same = lax.broadcasted_iota(jnp.int32, (rows, rows), 0) == lax.broadcasted_iota(
+        jnp.int32, (rows, rows), 1
+    )
     for block in range(code_ref.shape[1] // QBLOCK):
         columns = slice(block * QBLOCK, (block + 1) * QBLOCK)
-        value = code_ref[:, columns].astype(F32) * scale[:, block : block + 1]
-        weight_ref[:, columns] = value.astype(BF16)
+        down = jnp.sum(jnp.where(same, scale[block : block + 1, :], 0.0), axis=1, keepdims=True)
+        weight_ref[:, columns] = (code_ref[:, columns].astype(F32) * down).astype(BF16)
 
 
 def dequantize(key_codes, key_exponents):
@@ -37,7 +41,7 @@
         dequantize_kernel,
         out_shape=jax.ShapeDtypeStruct(key_codes.shape, BF16),
         compiler_params=PARAMS,
-    )(key_codes, key_exponents)
+    )(key_codes, key_exponents.T)
 
 
 def tables(positions):
@@ -253,7 +257,9 @@
     device_index = (((y * ZL + zl) * X + x) * ZH + zh) * CORE + core
     positions = (device_index * count + jnp.arange(count, dtype=jnp.int32)) % SEQ
     cosine, sine = tables(positions)
-    mine, theirs, pre_grad = partial_products(core[None], after(tokens, shard), key_cotangent, cosine, sine)
+    mine, theirs, pre_grad = partial_products(
+        core[None], tokens, key_cotangent, after(cosine, shard), sine
+    )
 
     flat = (1, Y * X * ZL * ZH, ROW, features)
     summed = summed_first(mine.reshape(flat), swap(theirs, "core").reshape(flat), steps=8)

time: 106 us -> 106 us (level)
    unnamed x21 -> x22, local copies, waits for them, and re-layouts: 5.6 us -> 5.47 us
where the time goes in v8:
time: 106 us; the launch traced here: 104 us
  starting transfers between devices  64.4 us (61%)
  Pallas kernels  17.8 us (17%)
  waiting for transfers between devices  15.2 us (14%)
  local copies, waits for them, and re-layouts  5.47 us (5%)
    ppermute x3, starting transfers between devices, swap(): return lax.ppermute(value, axis, [(0, 1), (1, 0)])  21.5 us
    ppermute x6, starting transfers between devices, from_x(): lax.ppermute(shard, 'x', [(i, (i + k) % X) for i in range(X)])  18.4 us
    all_to_all x1, starting transfers between devices, on_device(): lax.all_to_all(summed, ('zl', 'zh'), split_axis=0, concat_axis=0, tiled=T...  16.4 us
    all_to_all x1, waiting for transfers between devices, on_device(): lax.all_to_all(summed, ('zl', 'zh'), split_axis=0, concat_axis=0, tiled=T...  7.16 us
    pallas_call x4, Pallas kernels, summed_first(): pl.pallas_call(functools.partial(sum_kernel, factor), grid=(steps,), in_s...  6.28 us
    all_to_all x1, waiting for transfers between devices, on_device(): got = lax.all_to_all(summed, 'y', split_axis=0, concat_axis=0, tiled=True)  5.77 us
    unnamed x22, local copies, waits for them, and re-layouts  5.47 us
    all_to_all x1, starting transfers between devices, on_device(): got = lax.all_to_all(summed, 'y', split_axis=0, concat_axis=0, tiled=True)  4.18 us
  transfers between devices with their start and end apart: 12, of which 4 were waited for; matrix products, arithmetic and copies ran while one was open for 0% of the time, Pallas kernels for 14%

profile of v8, /device:TPU:1, one launch (start us, length us, event | category | flops | bytes accessed | tf_op | source)
XLA Modules:
  0.0 104.3 jit_solution(3780650963148577456)
XLA Ops:
  0.7 0.3 fusion
  1.0 0.0 copy-start.6
  1.0 0.9 copy-done.6
  2.0 0.7 copy-done.8
  2.6 0.1 shard_map.67.refs_0_
  2.8 0.1 pad_maximum_fusion
  2.9 0.0 copy-start.2
  2.9 0.0 copy-start
  2.9 1.3 %copy-done = bf16[128,4096]{1,0:T(8,128)(2,1)S(1)} copy-done((bf16[128,4096]{1,0:T(8,128)(2,1)S(1)}, bf16[128,4096]{1,0:T(8,128)(2,1)}, u32[]{:S(2)}) %copy-start) | copy-done | bytes 1048600
  4.2 0.9 copy-done.7
  5.1 2.5 %shard_map.68 = (bf16[4,4,8,2,8,512]{5,4,3,2,1,0:T(8,128)(2,1)S(1)}, bf16[4,4,8,2,8,512]{5,4,3,2,1,0:T(8,128)(2,1)S(1)}, bf16[128,512]{1,0:T(8,128)(2,1)S(1)}) custom-call(s32[1]{0:T(128)} %bitcast.2.core_ref, bf16[128,4096]{1,0:T(8,128)(2,1)S(1)} %copy-done, bf16[128,512]{1,0:T(8,128)(2,1)S(1)} %copy-done.7, f32[128,128]{1,0:T(8,128)S(1)} %get-tuple-element.16.cos_ref, ...), custom_call_target="tpu_custom_call" | custom-call | tf_op jit(solution)/shard_map/pallas_call | solution.py:86
  7.6 8.8 %collective-permute-start = (bf16[4,4,8,2,8,512]{5,4,3,2,1,0:T(8,128)(2,1)S(1)}, bf16[4,4,8,2,8,512]{5,4,3,2,1,0:T(8,128)(2,1)S(1)}, u32[]{:S(2)}, u32[]{:S(2)}) collective-permute-start(bf16[4,4,8,2,8,512]{5,4,3,2,1,0:T(8,128)(2,1)S(1)} %get-tuple-element.18), channel_id=1, source_target_pairs={{0,1},{1,0},{2,3},{3,2},{4,5},{5,4},{6,7},{7,6},{8,9},{9,8},{10,11... | collective-permute-start | bytes 6291464 | tf_op jit(solution)/shard_map/ppermute | solution.py:248
  16.4 10.1 %collective-permute-start.4 = (bf16[256,512]{1,0:T(8,128)(2,1)S(1)}, bf16[256,512]{1,0:T(8,128)(2,1)S(1)}, u32[]{:S(2)}, u32[]{:S(2)}) collective-permute-start(bf16[256,512]{1,0:T(8,128)(2,1)S(1)} %shard_map.67.refs_0_), channel_id=1, source_target_pairs={{0,2},{2,0},{1,3},{3,1},{4,6},{6,4},{5,7},{7,5},{8,10},{10,8},{9,1... | collective-permute-start | bytes 786440 | tf_op jit(solution)/shard_map/ppermute | solution.py:248
  26.5 0.0 collective-permute-done
  26.5 3.2 %shard_map.69 = bf16[256,8,512]{2,1,0:T(8,128)(2,1)} custom-call(bf16[1,256,8,512]{3,2,1,0:T(8,128)(2,1)S(1)} %bitcast.8, bf16[1,256,8,512]{3,2,1,0:T(8,128)(2,1)S(1)} %bitcast.9), custom_call_target="tpu_custom_call" | custom-call | tf_op jit(solution)/shard_map/pallas_call | solution.py:237
  29.7 4.2 %all-to-all-start = ((bf16[4,64,8,512]{3,2,1,0:T(8,128)(2,1)}), bf16[4,64,8,512]{3,2,1,0:T(8,128)(2,1)S(1)}, u32[]{:S(2)}, u32[]{:S(2)}) async-start(bf16[4,64,8,512]{3,2,1,0:T(8,128)(2,1)} %bitcast.6), calls=%async_computation | async-start | bytes 4194304 | tf_op jit(solution)/shard_map/all_to_all | solution.py:267
  33.9 4.4 %collective-permute-start.3 = (bf16[256,512]{1,0:T(8,128)(2,1)S(1)}, bf16[256,512]{1,0:T(8,128)(2,1)S(1)}, u32[]{:S(2)}, u32[]{:S(2)}) collective-permute-start(bf16[256,512]{1,0:T(8,128)(2,1)S(1)} %shard_map.67.refs_0_), channel_id=1, source_target_pairs={{0,12},{4,0},{8,4},{12,8},{1,13},{5,1},{9,5},{13,9},{2,14},{6,2},{... | collective-permute-start | bytes 786440 | tf_op jit(solution)/shard_map/ppermute | solution.py:220
  38.3 2.4 %collective-permute-start.2 = (bf16[256,512]{1,0:T(8,128)(2,1)S(1)}, bf16[256,512]{1,0:T(8,128)(2,1)S(1)}, u32[]{:S(2)}, u32[]{:S(2)}) collective-permute-start(bf16[256,512]{1,0:T(8,128)(2,1)S(1)} %shard_map.67.refs_0_), channel_id=1, source_target_pairs={{0,8},{4,12},{8,0},{12,4},{1,9},{5,13},{9,1},{13,5},{2,10},{6,14},... | collective-permute-start | bytes 786440 | tf_op jit(solution)/shard_map/ppermute | solution.py:220
  40.7 2.5 %collective-permute-start.1 = (bf16[256,512]{1,0:T(8,128)(2,1)S(1)}, bf16[256,512]{1,0:T(8,128)(2,1)S(1)}, u32[]{:S(2)}, u32[]{:S(2)}) collective-permute-start(bf16[256,512]{1,0:T(8,128)(2,1)S(1)} %shard_map.67.refs_0_), channel_id=1, source_target_pairs={{0,4},{4,8},{8,12},{12,0},{1,5},{5,9},{9,13},{13,1},{2,6},{6,10},{... | collective-permute-start | bytes 786440 | tf_op jit(solution)/shard_map/ppermute | solution.py:220
  43.3 0.0 collective-permute-done.4.block_ref
  43.3 0.0 copy-start.9
  43.3 0.7 copy-done.9
  44.0 0.9 copy-done.10
  45.0 4.0 %collective-permute-start.7 = (bf16[256,512]{1,0:T(8,128)(2,1)S(1)}, bf16[256,512]{1,0:T(8,128)(2,1)}, u32[]{:S(2)}, u32[]{:S(2)}) collective-permute-start(bf16[256,512]{1,0:T(8,128)(2,1)S(1)} %shard_map.70.refs_4_), channel_id=1, source_target_pairs={{0,12},{4,0},{8,4},{12,8},{1,13},{5,1},{9,5},{13,9},{2,14},{6,2},{... | collective-permute-start | bytes 786440 | tf_op jit(solution)/shard_map/ppermute | solution.py:220
  48.9 3.1 %collective-permute-start.6 = (bf16[256,512]{1,0:T(8,128)(2,1)S(1)}, bf16[256,512]{1,0:T(8,128)(2,1)}, u32[]{:S(2)}, u32[]{:S(2)}) collective-permute-start(bf16[256,512]{1,0:T(8,128)(2,1)S(1)} %shard_map.70.refs_4_), channel_id=1, source_target_pairs={{0,8},{4,12},{8,0},{12,4},{1,9},{5,13},{9,1},{13,5},{2,10},{6,14},... | collective-permute-start | bytes 786440 | tf_op jit(solution)/shard_map/ppermute | solution.py:220
  52.1 0.0 collective-permute-done.3.refs_3_
  52.1 1.9 %collective-permute-start.5 = (bf16[256,512]{1,0:T(8,128)(2,1)S(1)}, bf16[256,512]{1,0:T(8,128)(2,1)}, u32[]{:S(2)}, u32[]{:S(2)}) collective-permute-start(bf16[256,512]{1,0:T(8,128)(2,1)S(1)} %shard_map.70.refs_4_), channel_id=1, source_target_pairs={{0,4},{4,8},{8,12},{12,0},{1,5},{5,9},{9,13},{13,1},{2,6},{6,10},{... | collective-permute-start | bytes 786440 | tf_op jit(solution)/shard_map/ppermute | solution.py:220
  54.0 0.1 pad_add_fusion.place_ref
  54.1 5.8 %all-to-all-done.refs_0_ = bf16[4,64,8,512]{3,2,1,0:T(8,128)(2,1)S(1)} async-done(((bf16[4,64,8,512]{3,2,1,0:T(8,128)(2,1)}), bf16[4,64,8,512]{3,2,1,0:T(8,128)(2,1)S(1)}, u32[]{:S(2)}, u32[]{:S(2)}) %all-to-all-start) | async-done | bytes 2097184 | tf_op jit(solution)/shard_map/all_to_all | solution.py:267
  59.9 1.6 %shard_map.74 = bf16[64,8,512]{2,1,0:T(8,128)(2,1)} custom-call(bf16[4,64,8,512]{3,2,1,0:T(8,128)(2,1)S(1)} %all-to-all-done.refs_0_), custom_call_target="tpu_custom_call" | custom-call | tf_op jit(solution)/shard_map/pallas_call | solution.py:237
  61.5 3.9 %all-to-all-start.1 = ((bf16[4,16,8,512]{3,2,1,0:T(8,128)(2,1)}), bf16[4,16,8,512]{3,2,1,0:T(8,128)(2,1)S(1)}, u32[]{:S(2)}, u32[]{:S(2)}) async-start(bf16[4,16,8,512]{3,2,1,0:T(8,128)(2,1)} %bitcast.7), calls=%async_computation.1 | async-start | bytes 1048576 | tf_op jit(solution)/shard_map/all_to_all | solution.py:275
  65.4 0.0 collective-permute-done.2.refs_2_
  65.5 0.0 collective-permute-done.1.refs_1_
  65.5 0.0 collective-permute-done.7.refs_7_
  65.5 0.0 collective-permute-done.6.refs_6_
  65.5 1.2 %collective-permute-done.5.refs_5_ = bf16[256,512]{1,0:T(8,128)(2,1)} collective-permute-done((bf16[256,512]{1,0:T(8,128)(2,1)S(1)}, bf16[256,512]{1,0:T(8,128)(2,1)}, u32[]{:S(2)}, u32[]{:S(2)}) %collective-permute-start.5) | collective-permute-done | bytes 262176 | tf_op jit(solution)/shard_map/ppermute | solution.py:220
  66.7 2.6 %shard_map.71.weight_ref = bf16[2048,512]{1,0:T(8,128)(2,1)} custom-call(bf16[256,512]{1,0:T(8,128)(2,1)S(1)} %shard_map.67.refs_0_, bf16[256,512]{1,0:T(8,128)(2,1)S(1)} %collective-permute-done.1.refs_1_, bf16[256,512]{1,0:T(8,128)(2,1)S(1)} %collective-permute-done.2.refs_2_, bf16[256,512]{1,0:T(8,128)(2,1)S(1)} %collective-permute-done.3.refs_3_, ...), custom_call_target="tpu_custom_call" | custom-call | flops 99999997952 | bytes 4194304 | tf_op jit(solution)/shard_map/pallas_call | solution.py:111
  69.3 2.7 %collective-permute-start.8 = (bf16[2048,512]{1,0:T(8,128)(2,1)}, bf16[2048,512]{1,0:T(8,128)(2,1)}, u32[]{:S(2)}, u32[]{:S(2)}) collective-permute-start(bf16[2048,512]{1,0:T(8,128)(2,1)} %shard_map.71.weight_ref), channel_id=1, source_target_pairs={{0,1},{1,0},{2,3},{3,2},{4,5},{5,4},{6,7},{7,6},{8,9},{9,8},{10,11... | collective-permute-start | bytes 6291464 | tf_op jit(solution)/shard_map/ppermute | solution.py:248
  72.0 1.0 all-to-all-done.1.refs_0_
  73.0 0.8 shard_map.75
  73.7 16.4 %all-to-all-start.2 = ((bf16[16,8,512]{2,1,0:T(8,128)(2,1)}), bf16[16,8,512]{2,1,0:T(8,128)(2,1)S(1)}, u32[]{:S(2)}, u32[]{:S(2)}) async-start(bf16[16,8,512]{2,1,0:T(8,128)(2,1)} %shard_map.75), calls=%async_computation.2 | async-start | bytes 262144 | tf_op jit(solution)/shard_map/all_to_all | solution.py:280
  90.1 0.0 copy-done.1
  90.2 0.0 copy-start.3
  90.2 2.7 %shard_map.72 = (f32[128,512]{1,0:T(8,128)S(1)}, bf16[8,128,256]{2,1,0:T(8,128)(2,1)S(1)}) custom-call(s32[3]{0:T(128)S(1)} %pad_add_fusion.place_ref, bf16[128,4096]{1,0:T(8,128)(2,1)S(1)} %copy-done.1, bf16[128,512]{1,0:T(8,128)(2,1)S(1)} %get-tuple-element.17.pre_ref, bf16[2048,512]{1,0:T(8,128)(2,1)} %shard_map.71.weight_ref), custom_call_target="tpu_custom_call" | custom-call | flops 99999997952 | bytes 4194304 | tf_op jit(solution)/shard_map/pallas_call | solution.py:187
  92.9 0.0 collective-permute-done.8.weight_ref
  92.9 3.6 %shard_map.73 = (bf16[128,512]{1,0:T(8,128)(2,1)}, bf16[128,4096]{1,0:T(8,128)(2,1)}) custom-call(s32[3]{0:T(128)S(1)} %pad_add_fusion.place_ref, bf16[128,4096]{1,0:T(8,128)(2,1)S(1)} %copy-done.1, bf16[128,512]{1,0:T(8,128)(2,1)S(1)} %get-tuple-element.17.pre_ref, f32[128,128]{1,0:T(8,128)S(1)} %copy-done.3, f32[128,128]{1,0:T(8,128)S(1)} %copy-done.5, ...), custom_call_target="tpu_custom_call" | custom-call | flops 536870912 | bytes 4194304 | tf_op jit(solution)/shard_map/pallas_call | solution.py:202
  96.5 7.2 %all-to-all-done.2.refs_0_ = bf16[16,8,512]{2,1,0:T(8,128)(2,1)S(1)} async-done(((bf16[16,8,512]{2,1,0:T(8,128)(2,1)}), bf16[16,8,512]{2,1,0:T(8,128)(2,1)S(1)}, u32[]{:S(2)}, u32[]{:S(2)}) %all-to-all-start.2) | async-done | bytes 131104 | tf_op jit(solution)/shard_map/all_to_all | solution.py:280
  103.7 0.6 shard_map.76
  (13 shorter events, 0.1 us)
Async XLA Ops:
  1.0 1.0 copy-start.6
  2.0 0.7 copy-start.8
  2.9 4.7 %copy-start.2 = (f32[128,128]{1,0:T(8,128)}, f32[128,128]{1,0:T(8,128)S(1)}, u32[]{:S(2)}) copy-start(f32[128,128]{1,0:T(8,128)S(1)} %get-tuple-element.16.cos_ref) | copy-start | bytes 196612
  2.9 23.6 %copy-start.4 = (f32[128,128]{1,0:T(8,128)}, f32[128,128]{1,0:T(8,128)S(1)}, u32[]{:S(2)}) copy-start(f32[128,128]{1,0:T(8,128)S(1)} %get-tuple-element.33.sin_ref) | copy-start | bytes 196612
  2.9 1.3 %copy-start = (bf16[128,4096]{1,0:T(8,128)(2,1)S(1)}, bf16[128,4096]{1,0:T(8,128)(2,1)}, u32[]{:S(2)}) copy-start(bf16[128,4096]{1,0:T(8,128)(2,1)} %token_ref.5) | copy-start | bytes 3145732
  4.2 0.9 copy-start.7
  7.6 18.9 %collective-permute-start = (bf16[4,4,8,2,8,512]{5,4,3,2,1,0:T(8,128)(2,1)S(1)}, bf16[4,4,8,2,8,512]{5,4,3,2,1,0:T(8,128)(2,1)S(1)}, u32[]{:S(2)}, u32[]{:S(2)}) collective-permute-start(bf16[4,4,8,2,8,512]{5,4,3,2,1,0:T(8,128)(2,1)S(1)} %get-tuple-element.18), channel_id=1, source_target_pairs={{0,1},{1,0},{2,3},{3,2},{4,5},{5,4},{6,7},{7,6},{8,9},{9,8},{10,11... | collective-permute-start | bytes 6291464 | tf_op jit(solution)/shard_map/ppermute | solution.py:248
  16.4 26.9 %collective-permute-start.4 = (bf16[256,512]{1,0:T(8,128)(2,1)S(1)}, bf16[256,512]{1,0:T(8,128)(2,1)S(1)}, u32[]{:S(2)}, u32[]{:S(2)}) collective-permute-start(bf16[256,512]{1,0:T(8,128)(2,1)S(1)} %shard_map.67.refs_0_), channel_id=1, source_target_pairs={{0,2},{2,0},{1,3},{3,1},{4,6},{6,4},{5,7},{7,5},{8,10},{10,8},{9,1... | collective-permute-start | bytes 786440 | tf_op jit(solution)/shard_map/ppermute | solution.py:248
  29.7 30.1 %all-to-all-start = ((bf16[4,64,8,512]{3,2,1,0:T(8,128)(2,1)}), bf16[4,64,8,512]{3,2,1,0:T(8,128)(2,1)S(1)}, u32[]{:S(2)}, u32[]{:S(2)}) async-start(bf16[4,64,8,512]{3,2,1,0:T(8,128)(2,1)} %bitcast.6), calls=%async_computation | async-start | bytes 4194304 | tf_op jit(solution)/shard_map/all_to_all | solution.py:267
  33.9 18.2 %collective-permute-start.3 = (bf16[256,512]{1,0:T(8,128)(2,1)S(1)}, bf16[256,512]{1,0:T(8,128)(2,1)S(1)}, u32[]{:S(2)}, u32[]{:S(2)}) collective-permute-start(bf16[256,512]{1,0:T(8,128)(2,1)S(1)} %shard_map.67.refs_0_), channel_id=1, source_target_pairs={{0,12},{4,0},{8,4},{12,8},{1,13},{5,1},{9,5},{13,9},{2,14},{6,2},{... | collective-permute-start | bytes 786440 | tf_op jit(solution)/shard_map/ppermute | solution.py:220
  38.3 27.1 %collective-permute-start.2 = (bf16[256,512]{1,0:T(8,128)(2,1)S(1)}, bf16[256,512]{1,0:T(8,128)(2,1)S(1)}, u32[]{:S(2)}, u32[]{:S(2)}) collective-permute-start(bf16[256,512]{1,0:T(8,128)(2,1)S(1)} %shard_map.67.refs_0_), channel_id=1, source_target_pairs={{0,8},{4,12},{8,0},{12,4},{1,9},{5,13},{9,1},{13,5},{2,10},{6,14},... | collective-permute-start | bytes 786440 | tf_op jit(solution)/shard_map/ppermute | solution.py:220
  40.7 24.7 %collective-permute-start.1 = (bf16[256,512]{1,0:T(8,128)(2,1)S(1)}, bf16[256,512]{1,0:T(8,128)(2,1)S(1)}, u32[]{:S(2)}, u32[]{:S(2)}) collective-permute-start(bf16[256,512]{1,0:T(8,128)(2,1)S(1)} %shard_map.67.refs_0_), channel_id=1, source_target_pairs={{0,4},{4,8},{8,12},{12,0},{1,5},{5,9},{9,13},{13,1},{2,6},{6,10},{... | collective-permute-start | bytes 786440 | tf_op jit(solution)/shard_map/ppermute | solution.py:220
  43.3 0.7 copy-start.9
  44.0 0.9 copy-start.10
  45.0 20.5 %collective-permute-start.7 = (bf16[256,512]{1,0:T(8,128)(2,1)S(1)}, bf16[256,512]{1,0:T(8,128)(2,1)}, u32[]{:S(2)}, u32[]{:S(2)}) collective-permute-start(bf16[256,512]{1,0:T(8,128)(2,1)S(1)} %shard_map.70.refs_4_), channel_id=1, source_target_pairs={{0,12},{4,0},{8,4},{12,8},{1,13},{5,1},{9,5},{13,9},{2,14},{6,2},{... | collective-permute-start | bytes 786440 | tf_op jit(solution)/shard_map/ppermute | solution.py:220
  48.9 16.5 %collective-permute-start.6 = (bf16[256,512]{1,0:T(8,128)(2,1)S(1)}, bf16[256,512]{1,0:T(8,128)(2,1)}, u32[]{:S(2)}, u32[]{:S(2)}) collective-permute-start(bf16[256,512]{1,0:T(8,128)(2,1)S(1)} %shard_map.70.refs_4_), channel_id=1, source_target_pairs={{0,8},{4,12},{8,0},{12,4},{1,9},{5,13},{9,1},{13,5},{2,10},{6,14},... | collective-permute-start | bytes 786440 | tf_op jit(solution)/shard_map/ppermute | solution.py:220
  52.1 14.6 %collective-permute-start.5 = (bf16[256,512]{1,0:T(8,128)(2,1)S(1)}, bf16[256,512]{1,0:T(8,128)(2,1)}, u32[]{:S(2)}, u32[]{:S(2)}) collective-permute-start(bf16[256,512]{1,0:T(8,128)(2,1)S(1)} %shard_map.70.refs_4_), channel_id=1, source_target_pairs={{0,4},{4,8},{8,12},{12,0},{1,5},{5,9},{9,13},{13,1},{2,6},{6,10},{... | collective-permute-start | bytes 786440 | tf_op jit(solution)/shard_map/ppermute | solution.py:220
  61.5 11.4 %all-to-all-start.1 = ((bf16[4,16,8,512]{3,2,1,0:T(8,128)(2,1)}), bf16[4,16,8,512]{3,2,1,0:T(8,128)(2,1)S(1)}, u32[]{:S(2)}, u32[]{:S(2)}) async-start(bf16[4,16,8,512]{3,2,1,0:T(8,128)(2,1)} %bitcast.7), calls=%async_computation.1 | async-start | bytes 1048576 | tf_op jit(solution)/shard_map/all_to_all | solution.py:275
  65.4 24.7 %copy-start.1 = (bf16[128,4096]{1,0:T(8,128)(2,1)S(1)}, bf16[128,4096]{1,0:T(8,128)(2,1)}, u32[]{:S(2)}) copy-start(bf16[128,4096]{1,0:T(8,128)(2,1)} %token_ref.5) | copy-start | bytes 3145732
  69.3 23.6 %collective-permute-start.8 = (bf16[2048,512]{1,0:T(8,128)(2,1)}, bf16[2048,512]{1,0:T(8,128)(2,1)}, u32[]{:S(2)}, u32[]{:S(2)}) collective-permute-start(bf16[2048,512]{1,0:T(8,128)(2,1)} %shard_map.71.weight_ref), channel_id=1, source_target_pairs={{0,1},{1,0},{2,3},{3,2},{4,5},{5,4},{6,7},{7,6},{8,9},{9,8},{10,11... | collective-permute-start | bytes 6291464 | tf_op jit(solution)/shard_map/ppermute | solution.py:248
  73.7 30.0 %all-to-all-start.2 = ((bf16[16,8,512]{2,1,0:T(8,128)(2,1)}), bf16[16,8,512]{2,1,0:T(8,128)(2,1)S(1)}, u32[]{:S(2)}, u32[]{:S(2)}) async-start(bf16[16,8,512]{2,1,0:T(8,128)(2,1)} %shard_map.75), calls=%async_computation.2 | async-start | bytes 262144 | tf_op jit(solution)/shard_map/all_to_all | solution.py:280
  90.2 2.7 %copy-start.3 = (f32[128,128]{1,0:T(8,128)S(1)}, f32[128,128]{1,0:T(8,128)}, u32[]{:S(2)}) copy-start(f32[128,128]{1,0:T(8,128)} %copy-done.2) | copy-start | bytes 196612
  90.2 2.7 %copy-start.5 = (f32[128,128]{1,0:T(8,128)S(1)}, f32[128,128]{1,0:T(8,128)}, u32[]{:S(2)}) copy-start(f32[128,128]{1,0:T(8,128)} %copy-done.4) | copy-start | bytes 196612
